TPU v7x, 32 devices: a whole 2x2x4 slice. The times are simulated.
32 devices in a mesh: stream: 2 (over y), img: 16 (over z, x, core).
Axes of the slice: x: 2, y: 2, z: 4, core: 2. Of those that a mesh axis runs over, the one named last changes fastest.
Arguments:
- block_in: bfloat16 [2, 25088, 2016], P('stream', 'img'), may hold values from -6 to 6
- out_cotangent: bfloat16 [2, 25088, 2016], P('stream', 'img'), may hold values from -6 to 6
- pair_target: int32 [64, 3], P('img'), may hold values from 0 to 1
- entry_weight: bfloat16 [4064256], P('img'), may hold values from -0.125 to 0.125
- entry_gain: float32 [2016], replicated, may hold values from 0.1 to 1.9
- entry_shift: float32 [2016], replicated, may hold values from -3 to 3
- group_weight: bfloat16 [1016064], P('img'), may hold values from -0.25 to 0.25
- group_gain: float32 [2016], replicated, may hold values from 0.1 to 1.9
- group_shift: float32 [2016], replicated, may hold values from -3 to 3
- squeeze_weight: bfloat16 [1016064], P('img'), may hold values from -0.25 to 0.25
- squeeze_bias: float32 [504], replicated, may hold values from -3 to 3
- excite_weight: bfloat16 [1016064], P('img'), may hold values from -0.25 to 0.25
- excite_bias: float32 [2016], replicated, may hold values from -4 to 4
- exit_weight: bfloat16 [4064256], P('img'), may hold values from -0.125 to 0.125
- exit_gain: float32 [2016], replicated, may hold values from 0.1 to 1.9
- exit_shift: float32 [2016], replicated, may hold values from -3 to 3
Outputs:
- block_out: bfloat16 [2, 25088, 2016], P('stream', 'img')
- input_grad: bfloat16 [2, 25088, 2016], P('stream', 'img')
- entry_weight_gradient: float32 [4064256], P('img')
- entry_gain_gradient: float32 [2016], replicated
- entry_shift_gradient: float32 [2016], replicated
- group_weight_gradient: float32 [1016064], P('img')
- group_gain_gradient: float32 [2016], replicated
- group_shift_gradient: float32 [2016], replicated
- squeeze_weight_gradient: float32 [1016064], P('img')
- squeeze_bias_gradient: float32 [504], replicated
- excite_weight_gradient: float32 [1016064], P('img')
- excite_bias_gradient: float32 [2016], replicated
- exit_weight_gradient: float32 [4064256], P('img')
- exit_gain_gradient: float32 [2016], replicated
- exit_shift_gradient: float32 [2016], replicated
Inputs may be any that keep to these rules, and one draw needn't show every extreme that they name: `pair_target`: each small crop is paired with one global crop of the same image.
All inputs are finite; a program needn't handle non-finite values.
Results may differ from a plain program's by a relative error of at most 0.011.
Values may be sent and summed in bfloat16 or wider, within the bound.
A program may use at most 576 MiB of HBM per device.

v0:
```python
import jax
import jax.numpy as jnp
from jax import lax
from jax.sharding import PartitionSpec as P

CHANNELS = 2016
GROUPS = 36
SQUEEZE = 504
GROUP_WIDTH = 56
GLOBAL_SIDE = 14
SMALL_SIDE = 7
GLOBAL_CROPS = 2
SMALL_CROPS = 3
IMAGE_DEV = 4
MICRO_BATCHES = 2
IMAGE_ROWS = 392
SMALL_ROWS = 147


epsilon = 1e-05
pair_scale = 4.0
highest = lax.Precision.HIGHEST


def swapped(value, axis, bit):
    mask = 2**bit
    pairs = [(source, source ^ mask) for source in range(lax.axis_size(axis))]
    return lax.ppermute(value, axis, pairs)


def silu_slope(values):
    sig_vals = jax.nn.sigmoid(values)
    return sig_vals * (1.0 + values * (1.0 - sig_vals))


def shaped(pieces):
    entry_mat, group_mat, squeeze_mat, excite_mat, exit_mat = pieces
    return (
        entry_mat.reshape(CHANNELS, CHANNELS),
        group_mat.reshape(9, GROUPS, GROUP_WIDTH, GROUP_WIDTH),
        squeeze_mat.reshape(CHANNELS, SQUEEZE).astype(jnp.float32),
        excite_mat.reshape(SQUEEZE, CHANNELS).astype(jnp.float32),
        exit_mat.reshape(CHANNELS, CHANNELS),
    )


def neighborhood(values, side, count):
    images = values.shape[0]
    rows = count * side * side
    spatial = values[:, :rows].reshape(images * count, side, side, GROUPS, GROUP_WIDTH)
    padded = jnp.pad(spatial, ((0, 0), (1, 1), (1, 1), (0, 0), (0, 0)))
    pieces = [
        padded[:, offset // 3 : offset // 3 + side, offset % 3 : offset % 3 + side].reshape(
            images, rows, GROUPS, GROUP_WIDTH
        )
        for offset in range(9)
    ]
    stacked = jnp.stack(pieces, axis=1)
    return jnp.pad(stacked, ((0, 0), (0, 0), (0, IMAGE_ROWS - rows), (0, 0), (0, 0)))


def global_windows(values):
    return neighborhood(values, GLOBAL_SIDE, GLOBAL_CROPS)


def small_windows(values):
    return neighborhood(values, SMALL_SIDE, SMALL_CROPS)


def local(
    block_in,
    out_cotangent,
    pair_target,
    entry_weight,
    entry_gain,
    entry_shift,
    group_weight,
    group_gain,
    group_shift,
    squeeze_weight,
    squeeze_bias,
    excite_weight,
    excite_bias,
    exit_weight,
    exit_gain,
    exit_shift,
):
    stream = lax.axis_index("stream")
    on_global = stream == 0
    crop_side = jnp.where(on_global, GLOBAL_SIDE, SMALL_SIDE).astype(jnp.int32)
    crop_area = crop_side * crop_side
    live_rows = jnp.where(on_global, IMAGE_ROWS, SMALL_ROWS).astype(jnp.int32)
    per_batch = IMAGE_DEV // MICRO_BATCHES
    devices = lax.axis_size("img")
    norm_count = (live_rows * (devices * per_batch)).astype(jnp.float32)
    positions = jnp.arange(IMAGE_ROWS, dtype=jnp.int32)
    live_mask = positions < live_rows
    live_float = live_mask.astype(jnp.float32)[:, None]
    crop_index = positions // crop_area
    slot_ids = jnp.arange(SMALL_CROPS, dtype=jnp.int32)
    member = (live_mask[:, None] & (crop_index[:, None] == slot_ids[None, :])).astype(jnp.float32)
    pool_rows = member / crop_area.astype(jnp.float32)
    pair_ids = jnp.arange(GLOBAL_CROPS, dtype=jnp.int32)

    def batch_norm(values, norm_gain, norm_shift):
        masked = values * live_float
        totals = lax.psum(
            (jnp.sum(masked, axis=(0, 1)), jnp.sum(masked * values, axis=(0, 1))), "img"
        )
        average = totals[0] / norm_count
        inverse = lax.rsqrt(totals[1] / norm_count - average * average + epsilon)
        normed = (values - average) * inverse
        return (normed * norm_gain + norm_shift, normed, inverse)

    def norm_back(upstream, normed, inverse, norm_gain):
        masked = upstream * live_float
        local_shift = jnp.sum(masked, axis=(0, 1))
        local_gain = jnp.sum(masked * normed, axis=(0, 1))
        totals = lax.psum((local_shift, local_gain), "img")
        delta_act = (
            norm_gain
            * inverse
            * (upstream - totals[0] / norm_count - normed * totals[1] / norm_count)
        )
        return (delta_act * live_float, local_gain, local_shift)

    inputs = block_in[0].reshape(IMAGE_DEV, IMAGE_ROWS, CHANNELS)
    cotangent = out_cotangent[0].reshape(IMAGE_DEV, IMAGE_ROWS, CHANNELS)
    flat_weights = (entry_weight, group_weight, squeeze_weight, excite_weight, exit_weight)
    big_grads = tuple((jnp.zeros(piece.shape, jnp.float32) for piece in flat_weights))
    small_grads = (
        jnp.zeros((CHANNELS,), jnp.float32),
        jnp.zeros((CHANNELS,), jnp.float32),
        jnp.zeros((CHANNELS,), jnp.float32),
        jnp.zeros((CHANNELS,), jnp.float32),
        jnp.zeros((SQUEEZE,), jnp.float32),
        jnp.zeros((CHANNELS,), jnp.float32),
        jnp.zeros((CHANNELS,), jnp.float32),
        jnp.zeros((CHANNELS,), jnp.float32),
    )
    out_blocks = []
    grad_blocks = []
    for micro_index in range(MICRO_BATCHES):
        first_image = micro_index * per_batch
        source = inputs[first_image : first_image + per_batch]
        upstream_cot = (
            cotangent[first_image : first_image + per_batch].astype(jnp.float32) * live_float
        )
        chosen = pair_target[first_image : first_image + per_batch]
        weights = shaped(
            (
                lax.all_gather(entry_weight, "img", axis=0, tiled=True),
                lax.all_gather(group_weight, "img", axis=0, tiled=True),
                lax.all_gather(squeeze_weight, "img", axis=0, tiled=True),
                lax.all_gather(excite_weight, "img", axis=0, tiled=True),
                lax.all_gather(exit_weight, "img", axis=0, tiled=True),
            )
        )
        entry_mat, group_mat, squeeze_mat, excite_mat, exit_mat = weights
        images = source.shape[0]
        entry_act = jnp.einsum("nrc,cd->nrd", source, entry_mat, preferred_element_type=jnp.float32)
        entry_bn, normed_one, inverse_one = batch_norm(entry_act, entry_gain, entry_shift)
        hidden = jax.nn.silu(entry_bn).astype(jnp.bfloat16)
        beside_all = lax.cond(on_global, global_windows, small_windows, hidden)
        group_act = jnp.einsum(
            "nkrgi,kgio->nrgo", beside_all, group_mat, preferred_element_type=jnp.float32
        ).reshape(images, IMAGE_ROWS, CHANNELS)
        group_bn, normed_two, inverse_two = batch_norm(group_act, group_gain, group_shift)
        mixed_act = jax.nn.silu(group_bn)
        pooled = jnp.einsum("rc,nrd->ncd", pool_rows, mixed_act, precision=highest)
        squeeze_in = (
            jnp.einsum("ncd,ds->ncs", pooled, squeeze_mat, precision=highest) + squeeze_bias
        )
        squeezed = jax.nn.silu(squeeze_in)
        excite_in = jnp.einsum("ncs,sd->ncd", squeezed, excite_mat, precision=highest) + excite_bias
        gate_vals = jax.nn.sigmoid(excite_in)
        gate_rows = jnp.einsum("rc,ncd->nrd", member, gate_vals, precision=highest)
        scaled = (mixed_act * gate_rows).astype(jnp.bfloat16)
        exit_act = jnp.einsum("nrc,cd->nrd", scaled, exit_mat, preferred_element_type=jnp.float32)
        exit_bn, normed_three, inverse_three = batch_norm(exit_act, exit_gain, exit_shift)
        residual = source.astype(jnp.float32) + exit_bn
        result = jax.nn.silu(residual)
        out_blocks.append((result * live_float).astype(jnp.bfloat16))
        crop_embed = jnp.einsum("rc,nrd->ncd", pool_rows, result, precision=highest)
        choose = (chosen[:, :, None] == pair_ids[None, None, :]).astype(jnp.float32)
        summed = jnp.einsum("njk,njd->nkd", choose, crop_embed, precision=highest)
        payload = jnp.where(on_global, crop_embed[:, :GLOBAL_CROPS], summed).astype(jnp.bfloat16)
        partner = swapped(payload, "stream", 0).astype(jnp.float32)
        global_side = jnp.concatenate(
            [partner, jnp.zeros((images, SMALL_CROPS - GLOBAL_CROPS, CHANNELS), jnp.float32)],
            axis=1,
        )
        small_side = jnp.einsum("njk,nkd->njd", choose, partner, precision=highest)
        embed_grad = pair_scale * jnp.where(on_global, global_side, small_side)
        result_grad = upstream_cot + jnp.einsum(
            "rc,ncd->nrd", pool_rows, embed_grad, precision=highest
        )
        residual_grad = result_grad * silu_slope(residual)
        exit_delta, gain_three, shift_three = norm_back(
            residual_grad, normed_three, inverse_three, exit_gain
        )
        exit_low = exit_delta.astype(jnp.bfloat16)
        exit_grad = jnp.einsum("nrc,nrd->cd", scaled, exit_low, preferred_element_type=jnp.float32)
        scaled_grad = jnp.einsum(
            "nrd,cd->nrc", exit_low, exit_mat, preferred_element_type=jnp.float32
        )
        gate_grad = jnp.einsum("rc,nrd->ncd", member, scaled_grad * mixed_act, precision=highest)
        excite_delta = gate_grad * gate_vals * (1.0 - gate_vals)
        excite_mat_grad = jnp.einsum("ncs,ncd->sd", squeezed, excite_delta, precision=highest)
        squeeze_delta = jnp.einsum(
            "ncd,sd->ncs", excite_delta, excite_mat, precision=highest
        ) * silu_slope(squeeze_in)
        squeeze_mat_grad = jnp.einsum("ncd,ncs->ds", pooled, squeeze_delta, precision=highest)
        pooled_grad = jnp.einsum("ncs,ds->ncd", squeeze_delta, squeeze_mat, precision=highest)
        mixed_grad = scaled_grad * gate_rows + jnp.einsum(
            "rc,ncd->nrd", pool_rows, pooled_grad, precision=highest
        )
        group_delta, gain_two, shift_two = norm_back(
            mixed_grad * silu_slope(group_bn), normed_two, inverse_two, group_gain
        )
        group_low = group_delta.astype(jnp.bfloat16)
        group_mat_grad = jnp.einsum(
            "nkrgi,nrgo->kgio",
            beside_all,
            group_low.reshape(images, IMAGE_ROWS, GROUPS, GROUP_WIDTH),
            preferred_element_type=jnp.float32,
        )
        back_around = lax.cond(on_global, global_windows, small_windows, group_low)[:, ::-1]
        hidden_grad = jnp.einsum(
            "nkrgo,kgio->nrgi", back_around, group_mat, preferred_element_type=jnp.float32
        ).reshape(images, IMAGE_ROWS, CHANNELS)
        entry_delta, gain_one, shift_one = norm_back(
            hidden_grad * silu_slope(entry_bn), normed_one, inverse_one, entry_gain
        )
        entry_low = entry_delta.astype(jnp.bfloat16)
        entry_grad = jnp.einsum(
            "nrc,nrd->cd", source, entry_low, preferred_element_type=jnp.float32
        )
        source_grad = (
            jnp.einsum("nrd,cd->nrc", entry_low, entry_mat, preferred_element_type=jnp.float32)
            + residual_grad * live_float
        )
        grad_blocks.append(source_grad.astype(jnp.bfloat16))
        micro_grads = (
            entry_grad.reshape(-1),
            group_mat_grad.reshape(-1),
            squeeze_mat_grad.reshape(-1),
            excite_mat_grad.reshape(-1),
            exit_grad.reshape(-1),
        )
        micro_grads = (
            lax.psum_scatter(micro_grads[0], "img", scatter_dimension=0, tiled=True),
            lax.psum_scatter(micro_grads[1], "img", scatter_dimension=0, tiled=True),
            lax.psum_scatter(micro_grads[2], "img", scatter_dimension=0, tiled=True),
            lax.psum_scatter(micro_grads[3], "img", scatter_dimension=0, tiled=True),
            lax.psum_scatter(micro_grads[4], "img", scatter_dimension=0, tiled=True),
        )
        big_grads = tuple((held + fresh for held, fresh in zip(big_grads, micro_grads)))
        fresh_small = (
            gain_one,
            shift_one,
            gain_two,
            shift_two,
            jnp.sum(squeeze_delta, axis=(0, 1)),
            jnp.sum(excite_delta, axis=(0, 1)),
            gain_three,
            shift_three,
        )
        small_grads = tuple((held + fresh for held, fresh in zip(small_grads, fresh_small)))
    shards = (
        lax.psum(big_grads[0].astype(jnp.bfloat16), "stream").astype(jnp.float32),
        lax.psum(big_grads[1].astype(jnp.bfloat16), "stream").astype(jnp.float32),
        lax.psum(big_grads[2].astype(jnp.bfloat16), "stream").astype(jnp.float32),
        lax.psum(big_grads[3].astype(jnp.bfloat16), "stream").astype(jnp.float32),
        lax.psum(big_grads[4].astype(jnp.bfloat16), "stream").astype(jnp.float32),
    )
    smalls = lax.psum(
        (
            small_grads[0],
            small_grads[1],
            small_grads[2],
            small_grads[3],
            small_grads[4],
            small_grads[5],
            small_grads[6],
            small_grads[7],
        ),
        ("stream", "img"),
    )
    block_out = jnp.concatenate(out_blocks, axis=0).reshape(1, IMAGE_DEV * IMAGE_ROWS, CHANNELS)
    input_grad = jnp.concatenate(grad_blocks, axis=0).reshape(1, IMAGE_DEV * IMAGE_ROWS, CHANNELS)
    return (
        block_out,
        input_grad,
        shards[0],
        smalls[0],
        smalls[1],
        shards[1],
        smalls[2],
        smalls[3],
        shards[2],
        smalls[4],
        shards[3],
        smalls[5],
        shards[4],
        smalls[6],
        smalls[7],
    )


def solution(mesh):
    return jax.shard_map(
        local,
        mesh=mesh,
        in_specs=(
            P("stream", "img", None),
            P("stream", "img", None),
            P("img", None),
            P("img"),
            P(),
            P(),
            P("img"),
            P(),
            P(),
            P("img"),
            P(),
            P("img"),
            P(),
            P("img"),
            P(),
            P(),
        ),
        out_specs=(
            P("stream", "img", None),
            P("stream", "img", None),
            P("img"),
            P(),
            P(),
            P("img"),
            P(),
            P(),
            P("img"),
            P(),
            P("img"),
            P(),
            P("img"),
            P(),
            P(),
        ),
        check_vma=False,
    )
```

profile of v0, /device:TPU:0, one launch (start us, length us, event | category | flops | bytes accessed | tf_op | source)
XLA Modules:
  0.0 3405.5 jit_solution(12786891017617797690)
XLA Ops:
  60.6 372.3 %all-reduce.41.cloned.1.call-done = (bf16[1016064]{0:T(1024)(128)(2,1)}, bf16[4064256]{0:T(1024)(128)(2,1)}, bf16[1016064]{0:T(1024)(128)(2,1)}, bf16[1016064]{0:T(1024)(128)(2,1)}, bf16[4064256]{0:T(1024)(128)(2,1)}) async-done(((bf16[1016064]{0:T(1024)(128)(2,1)}, bf16[4064256]{0:T(1024)(128)(2,1)}, bf16[1016064]{0:T(1024)(128)(2,1)}, bf16[1016064]{0:T(1024)(128)(2,1)}, bf16[4064256]{0:T(1024)(128)(2,1)}), ...) | async-done | bytes 22353424
  470.3 60.3 %all-reduce.34 = (f32[2016]{0:T(1024)S(1)}, f32[2016]{0:T(1024)S(1)}) all-reduce(f32[2016]{0:T(1024)S(1)} %get-tuple-element.54, f32[2016]{0:T(1024)S(1)} %get-tuple-element.53), channel_id=1, replica_groups=mesh['stream'=2,'img'=16] {'img'}, use_global_device_ids=true, to_apply=%region_1.2 | all-reduce | flops 4032 | bytes 32256 | tf_op jit(solution)/shard_map/psum | solution.py:107
  535.2 172.0 %conditional.4 = (bf16[2,9,392,36,56]{2,4,3,0,1:T(8,128)(2,1)}) conditional(s32[]{:T(128)} %convert_element_type.164, bf16[2,392,2016]{2,1,0:T(8,128)(2,1)S(1)} %multiply_convert_fusion.9, bf16[2,392,2016]{2,1,0:T(8,128)(2,1)S(1)} %multiply_convert_fusion.9), branch_computations={%region_4.5_spmd, %region_5.6_spmd} | conditional | bytes 258435328 | solution.py:164
  555.8 42.9 %pad_slice_fusion.8 = (bf16[4,14,14,36,56]{4,3,2,1,0:T(8,128)(2,1)}, bf16[4,14,14,36,56]{4,3,2,1,0:T(8,128)(2,1)}, bf16[4,14,14,36,56]{4,3,2,1,0:T(8,128)(2,1)},...) fusion(bf16[4,14,14,36,56]{4,3,2,1,0:T(8,128)(2,1)} %reshape.333), kind=kLoop, calls=%fused_computation.17 | loop fusion | bytes 28449792 | tf_op jit(solution)/shard_map/cond/branch_1_fun/slice | solution.py:53
  770.2 57.9 %all-reduce.33 = (f32[2016]{0:T(1024)S(1)}, f32[2016]{0:T(1024)S(1)}) all-reduce(f32[2016]{0:T(1024)S(1)} %reduce_sum.265, f32[2016]{0:T(1024)S(1)} %reduce_sum.263), channel_id=1, replica_groups=mesh['stream'=2,'img'=16] {'img'}, use_global_device_ids=true, to_apply=%region_9.10 | all-reduce | flops 4032 | bytes 32256 | tf_op jit(solution)/shard_map/psum | solution.py:107
  855.0 58.0 %all-reduce.32 = (f32[2016]{0:T(1024)S(1)}, f32[2016]{0:T(1024)S(1)}) all-reduce(f32[2016]{0:T(1024)S(1)} %get-tuple-element.52, f32[2016]{0:T(1024)S(1)} %get-tuple-element.51), channel_id=1, replica_groups=mesh['stream'=2,'img'=16] {'img'}, use_global_device_ids=true, to_apply=%region_11.12 | all-reduce | flops 4032 | bytes 32256 | tf_op jit(solution)/shard_map/psum | solution.py:107
  960.1 57.6 %all-reduce.31 = (f32[2016]{0:T(1024)S(1)}, f32[2016]{0:T(1024)S(1)}) all-reduce(f32[2016]{0:T(1024)S(1)} %get-tuple-element.63, f32[2016]{0:T(1024)S(1)} %get-tuple-element.64), channel_id=1, replica_groups=mesh['stream'=2,'img'=16] {'img'}, use_global_device_ids=true, to_apply=%region_15.16 | all-reduce | flops 4032 | bytes 32256 | tf_op jit(solution)/shard_map/psum | solution.py:107
  1022.4 163.6 %conditional.5 = (bf16[2,9,392,36,56]{2,4,3,0,1:T(8,128)(2,1)}) conditional(s32[]{:T(128)} %convert_element_type.164, bf16[2,392,2016]{2,1,0:T(8,128)(2,1)S(1)} %multiply_convert_fusion.7, bf16[2,392,2016]{2,1,0:T(8,128)(2,1)S(1)} %multiply_convert_fusion.7), branch_computations={%region_18.19_spmd, %region_19.20_spmd} | conditional | bytes 258435328 | solution.py:164
  1035.2 42.7 %pad_slice_fusion.24 = (bf16[4,14,14,36,56]{4,3,2,1,0:T(8,128)(2,1)}, bf16[4,14,14,36,56]{4,3,2,1,0:T(8,128)(2,1)}, bf16[4,14,14,36,56]{4,3,2,1,0:T(8,128)(2,1)}...) fusion(bf16[4,14,14,36,56]{4,3,2,1,0:T(8,128)(2,1)} %reshape.353), kind=kLoop, calls=%fused_computation.51 | loop fusion | bytes 28449792 | tf_op jit(solution)/shard_map/cond/branch_1_fun/slice | solution.py:53
  1213.8 57.7 %all-reduce.30 = (f32[2016]{0:T(1024)S(1)}, f32[2016]{0:T(1024)S(1)}, f32[2016]{0:T(1024)S(1)}, f32[2016]{0:T(1024)S(1)}) all-reduce(f32[2016]{0:T(1024)S(1)} %get-tuple-element.44, f32[2016]{0:T(1024)S(1)} %get-tuple-element.43, f32[2016]{0:T(1024)S(1)} %reduce_sum.273, ...), channel_id=1, replica_groups=mesh['stream'=2,'img'=16] {'img'}, use_global_device_ids=true, to_apply=%region_31.32 | all-reduce | flops 8064 | bytes 64512 | tf_op jit(solution)/shard_map/psum | solution.py:119
  1361.3 57.7 %all-reduce.29 = (f32[2016]{0:T(1024)S(1)}, f32[2016]{0:T(1024)S(1)}, f32[2016]{0:T(1024)S(1)}, f32[2016]{0:T(1024)S(1)}) all-reduce(f32[2016]{0:T(1024)S(1)} %get-tuple-element.61, f32[2016]{0:T(1024)S(1)} %get-tuple-element.62, f32[2016]{0:T(1024)S(1)} %get-tuple-element.42, ...), channel_id=1, replica_groups=mesh['stream'=2,'img'=16] {'img'}, use_global_device_ids=true, to_apply=%region_25.26 | all-reduce | flops 8064 | bytes 64512 | tf_op jit(solution)/shard_map/psum | solution.py:107
  1439.0 164.3 %conditional.6 = (bf16[2,9,392,36,56]{2,4,3,0,1:T(8,128)(2,1)}) conditional(s32[]{:T(128)} %convert_element_type.164, bf16[2,392,2016]{1,2,0:T(8,128)(2,1)} %copy.229, bf16[2,392,2016]{1,2,0:T(8,128)(2,1)} %copy.229), branch_computations={%region_36.37_spmd, %region_37.38_spmd} | conditional | bytes 258435328 | solution.py:228
  1452.5 42.5 %pad_slice_fusion.40 = (bf16[4,14,14,36,56]{4,3,2,1,0:T(8,128)(2,1)}, bf16[4,14,14,36,56]{4,3,2,1,0:T(8,128)(2,1)}, bf16[4,14,14,36,56]{4,3,2,1,0:T(8,128)(2,1)}...) fusion(bf16[4,14,14,36,56]{4,3,2,1,0:T(8,128)(2,1)} %reshape.373), kind=kLoop, calls=%fused_computation.85 | loop fusion | bytes 28449792 | tf_op jit(solution)/shard_map/cond/branch_1_fun/slice | solution.py:53
  1603.3 25.1 rev.6
  1696.8 58.0 %all-reduce.28 = (f32[2016]{0:T(1024)S(1)}, f32[2016]{0:T(1024)S(1)}) all-reduce(f32[2016]{0:T(1024)S(1)} %get-tuple-element.59, f32[2016]{0:T(1024)S(1)} %get-tuple-element.60), channel_id=1, replica_groups=mesh['stream'=2,'img'=16] {'img'}, use_global_device_ids=true, to_apply=%region_45.46 | all-reduce | flops 4032 | bytes 32256 | tf_op jit(solution)/shard_map/psum | solution.py:119
  1795.5 57.6 %all-reduce.27 = (f32[2016]{0:T(1024)S(1)}, f32[2016]{0:T(1024)S(1)}) all-reduce(f32[2016]{0:T(1024)S(1)} %get-tuple-element.48, f32[2016]{0:T(1024)S(1)} %get-tuple-element.47), channel_id=1, replica_groups=mesh['stream'=2,'img'=16] {'img'}, use_global_device_ids=true, to_apply=%region_49.50 | all-reduce | flops 4032 | bytes 32256 | tf_op jit(solution)/shard_map/psum | solution.py:119
  1862.9 164.4 %conditional.7 = (bf16[2,9,392,36,56]{2,4,3,0,1:T(8,128)(2,1)}) conditional(s32[]{:T(128)} %convert_element_type.164, bf16[2,392,2016]{1,2,0:T(8,128)(2,1)} %copy.232, bf16[2,392,2016]{1,2,0:T(8,128)(2,1)} %copy.232), branch_computations={%region_50.51_spmd, %region_51.52_spmd} | conditional | bytes 258435328 | solution.py:228
  1876.4 42.8 %pad_slice_fusion.56 = (bf16[4,14,14,36,56]{4,3,2,1,0:T(8,128)(2,1)}, bf16[4,14,14,36,56]{4,3,2,1,0:T(8,128)(2,1)}, bf16[4,14,14,36,56]{4,3,2,1,0:T(8,128)(2,1)}...) fusion(bf16[4,14,14,36,56]{4,3,2,1,0:T(8,128)(2,1)} %reshape.393), kind=kLoop, calls=%fused_computation.119 | loop fusion | bytes 28449792 | tf_op jit(solution)/shard_map/cond/branch_1_fun/slice | solution.py:53
  2027.3 25.2 rev.7
  2095.8 57.7 %all-reduce.26 = (f32[2016]{0:T(1024)S(1)}, f32[2016]{0:T(1024)S(1)}, f32[2016]{0:T(1024)S(1)}, f32[2016]{0:T(1024)S(1)}) all-reduce(f32[2016]{0:T(1024)S(1)} %get-tuple-element.46, f32[2016]{0:T(1024)S(1)} %get-tuple-element.45, f32[2016]{0:T(1024)S(1)} %copy-done.156, ...), channel_id=1, replica_groups=mesh['stream'=2,'img'=16] {'img'}, use_global_device_ids=true, to_apply=%region_55.56 | all-reduce | flops 8064 | bytes 64512 | tf_op jit(solution)/shard_map/psum | solution.py:119
  2215.3 24.6 fusion.8
  2239.9 28.3 fusion.13
  2380.4 933.9 %all-reduce.44 = (bf16[4064256]{0:T(1024)(128)(2,1)}, bf16[1016064]{0:T(1024)(128)(2,1)}, bf16[1016064]{0:T(1024)(128)(2,1)}, bf16[1016064]{0:T(1024)(128)(2,1)}, bf16[4064256]{0:T(1024)(128)(2,1)}) all-reduce(f32[4064256]{0:T(1024)} %reshape.451, f32[1016064]{0:T(1024)} %reshape.452, ...), channel_id=7, replica_groups=mesh['stream'=2,'img'=16] {'img'}, use_global_device_ids=true, to_apply=%region_56.57.clone | all-reduce | flops 11176704 | bytes 67060224
  3323.8 50.8 %all-reduce.24 = (f32[2016]{0:T(1024)}, f32[2016]{0:T(1024)}, f32[2016]{0:T(1024)}, f32[2016]{0:T(1024)}, f32[504]{0:T(512)}, /*index=5*/f32[2016]{0:T(1024)}, f32[2016]{0:T(1024)}, f32[2016]{0:T(1024)}) all-reduce(f32[2016]{0:T(1024)S(1)} %copy-done.162, ...), channel_id=1, replica_groups=mesh['stream'=2,'img'=16] {'stream','img'}, use_global_device_ids=true, to_apply=%region_59.60 | all-reduce | flops 14616 | bytes 116928 | tf_op jit(solution)/shard_map/psum | solution.py:277
  (601 shorter events, 1222.9 us)
Async XLA Ops:
  7.2 425.7 %all-reduce.41.cloned.1.call-start = ((), (), s32[]{:S(2)}) async-start(), calls=%async_computation | async-start | bytes 44716032
  43.7 3345.8 %all-reduce.43.cloned.1.call-start = ((), (), s32[]{:S(2)}) async-start(), calls=%async_computation.1 | async-start | bytes 2813952 | tf_op jit(solution)/shard_map/psum | solution.py:271
  45.7 1374.0 %copy-start.104 = (f32[392]{0:T(512)}, f32[392]{0:T(512)S(1)}, u32[]{:S(2)}) copy-start(f32[392]{0:T(512)S(1)} %fusion.156) | copy-start | bytes 4708
  52.5 406.3 %copy-start.44 = (bf16[1,784,2016]{2,1,0:T(8,128)(2,1)}, bf16[1,784,2016]{2,1,0:T(8,128)(2,1)S(1)}, u32[]{:S(2)}) copy-start(bf16[1,784,2016]{2,1,0:T(8,128)(2,1)S(1)} %get-tuple-element.193) | copy-start | bytes 9483268
  739.0 98.9 %copy-start.1 = (bf16[504,2016,1]{1,0,2:T(8,128)(2,1)}, bf16[504,2016,1]{1,0,2:T(8,128)(2,1)S(1)}, u32[]{:S(2)}) copy-start(bf16[504,2016,1]{1,0,2:T(8,128)(2,1)S(1)} %reshape.486) | copy-start | bytes 6096388
  923.1 20.8 collective-permute-start
  944.1 73.7 %copy-start.101 = (f32[2016]{0:T(1024)S(1)}, f32[2016]{0:T(1024)}, u32[]{:S(2)}) copy-start(f32[2016]{0:T(1024)} %param.28) | copy-start | bytes 24196
  944.1 74.3 %copy-start.123 = (f32[2016]{0:T(1024)S(1)}, f32[2016]{0:T(1024)}, u32[]{:S(2)}) copy-start(f32[2016]{0:T(1024)} %param.29) | copy-start | bytes 24196
  960.1 253.7 %copy-start.147 = (f32[2016]{0:T(1024)}, f32[2016]{0:T(1024)S(1)}, u32[]{:S(2)}) copy-start(f32[2016]{0:T(1024)S(1)} %get-tuple-element.43) | copy-start | bytes 24196
  960.1 253.7 %copy-start.149 = (f32[2016]{0:T(1024)}, f32[2016]{0:T(1024)S(1)}, u32[]{:S(2)}) copy-start(f32[2016]{0:T(1024)S(1)} %get-tuple-element.44) | copy-start | bytes 24196
  1346.6 73.0 %copy-start.164 = (f32[2016]{0:T(1024)S(1)}, f32[2016]{0:T(1024)}, u32[]{:S(2)}) copy-start(f32[2016]{0:T(1024)} %param.39) | copy-start | bytes 24196
  1435.0 238.5 %collective-permute-start.1 = (bf16[2,2,2016]{2,1,0:T(2,128)(2,1)}, bf16[2,2,2016]{2,1,0:T(2,128)(2,1)}, u32[]{:S(2)}, u32[]{:S(2)}) collective-permute-start(bf16[2,2,2016]{2,1,0:T(2,128)(2,1)} %fusion.75), channel_id=1, source_target_pairs={{0,16},{16,0},{1,17},{17,1},{2,18},{18,2},{3,19},{19,3},{4,20},{20... | collective-permute-start | bytes 48392 | tf_op jit(solution)/shard_map/ppermute | solution.py:28
  1674.5 80.3 %copy-start.142 = (f32[2016]{0:T(1024)S(1)}, f32[2016]{0:T(1024)}, u32[]{:S(2)}) copy-start(f32[2016]{0:T(1024)} %get-tuple-element.117) | copy-start | bytes 24196
  2380.4 943.3 %copy-start.183 = (f32[2016]{0:T(1024)S(1)}, f32[2016]{0:T(1024)}, u32[]{:S(2)}) copy-start(f32[2016]{0:T(1024)} %get-tuple-element.221) | copy-start | bytes 24196
  2380.4 943.3 %copy-start.184 = (f32[2016]{0:T(1024)S(1)}, f32[2016]{0:T(1024)}, u32[]{:S(2)}) copy-start(f32[2016]{0:T(1024)} %get-tuple-element.223) | copy-start | bytes 24196
  2380.4 943.3 %copy-start.181 = (f32[504]{0:T(512)S(1)}, f32[504]{0:T(512)}, u32[]{:S(2)}) copy-start(f32[504]{0:T(512)} %get-tuple-element.217) | copy-start | bytes 6052
  2380.4 943.3 %copy-start.182 = (f32[504]{0:T(512)S(1)}, f32[504]{0:T(512)}, u32[]{:S(2)}) copy-start(f32[504]{0:T(512)} %get-tuple-element.219) | copy-start | bytes 6052
  2380.4 943.4 %copy-start.157 = (f32[2016]{0:T(1024)S(1)}, f32[2016]{0:T(1024)}, u32[]{:S(2)}) copy-start(f32[2016]{0:T(1024)} %add.400) | copy-start | bytes 24196
  2380.4 943.4 %copy-start.158 = (f32[2016]{0:T(1024)S(1)}, f32[2016]{0:T(1024)}, u32[]{:S(2)}) copy-start(f32[2016]{0:T(1024)} %add.401) | copy-start | bytes 24196
  2380.4 943.4 %copy-start.159 = (f32[2016]{0:T(1024)S(1)}, f32[2016]{0:T(1024)}, u32[]{:S(2)}) copy-start(f32[2016]{0:T(1024)} %add.394) | copy-start | bytes 24196
  2380.4 943.4 %copy-start.160 = (f32[2016]{0:T(1024)S(1)}, f32[2016]{0:T(1024)}, u32[]{:S(2)}) copy-start(f32[2016]{0:T(1024)} %add.393) | copy-start | bytes 24196
  2380.4 943.4 %copy-start.161 = (f32[2016]{0:T(1024)S(1)}, f32[2016]{0:T(1024)}, u32[]{:S(2)}) copy-start(f32[2016]{0:T(1024)} %add.391) | copy-start | bytes 24196
  2380.4 943.4 %copy-start.162 = (f32[2016]{0:T(1024)S(1)}, f32[2016]{0:T(1024)}, u32[]{:S(2)}) copy-start(f32[2016]{0:T(1024)} %add.390) | copy-start | bytes 24196
  2380.4 994.2 %copy-start.79 = (bf16[2,392,2016]{2,1,0:T(8,128)(2,1)S(1)}, bf16[2,392,2016]{2,1,0:T(8,128)(2,1)}, u32[]{:S(2)}) copy-start(bf16[2,392,2016]{2,1,0:T(8,128)(2,1)} %get-tuple-element.200) | copy-start | bytes 9483268
  (167 other events, 2409.8 us)
Sparse Core Ops, SparseCore 0:
  43.8 388.9 all-reduce.40
  3323.8 58.8 all-reduce.42
where the time goes:
time: 3430 us; the launch traced here: 3410 us
  blocking collectives  1510 us (44%)
  local copies, waits for them, and re-layouts  984 us (29%)
  matrix products  412 us (12%)
  waiting for transfers between devices  372 us (11%)
  other arithmetic  101 us (3%)
    unnamed x1, blocking collectives  934 us
    unnamed x3, waiting for transfers between devices  372 us
    reshape x32, local copies, waits for them, and re-layouts, neighborhood(): stacked = jnp.stack(pieces, axis=1)  332 us
    psum x5, blocking collectives, batch_norm(): lax.psum((jnp.sum(masked, axis=(0, 1)), jnp.sum(masked * values, axis=(0,...  291 us
    psum x4, blocking collectives, norm_back(): totals = lax.psum((local_shift, local_gain), 'img')  231 us
    slice x4, local copies, waits for them, and re-layouts, neighborhood(): padded[:, offset // 3:offset // 3 + side, offset % 3:offset % 3 + side]  171 us
    cond x96, local copies, waits for them, and re-layouts  91.3 us
    add x7, local copies, waits for them, and re-layouts, local(): held + fresh  89 us
  transfers between devices with their start and end apart: 4, of which 1 were waited for; matrix products, arithmetic and copies ran while one was open for 8% of the time, Pallas kernels for 0%

commit v1 on v0

v1 whole, which is shorter than its diff:
```python
import functools

import jax
import jax.numpy as jnp
import numpy as np
from jax import lax
from jax.experimental import pallas as pl
from jax.experimental.pallas import tpu as pltpu
from jax.sharding import PartitionSpec as P

CHANNELS = 2016
GROUPS = 36
SQUEEZE = 504
GROUP_WIDTH = 56
GLOBAL_SIDE = 14
SMALL_SIDE = 7
GLOBAL_CROPS = 2
SMALL_CROPS = 3
IMAGE_DEV = 4
MICRO_BATCHES = 2
IMAGE_ROWS = 392
SMALL_ROWS = 147
ROWS = IMAGE_DEV * IMAGE_ROWS
HALF = ROWS // MICRO_BATCHES

BLOCK = 224
LANES = 256
BLOCKS = CHANNELS // BLOCK
WIDE = BLOCKS * LANES
PADDED = 2048
OUT_BLOCKS = PADDED // LANES

IMAGE_PAD = 424
TOP = 16
CONV_ROWS = IMAGE_DEV * IMAGE_PAD
DEEP_ROWS = 1792
PAD_ROWS = TOP + DEEP_ROWS + 16
CROPS = 16
CHUNK = 126
CHUNK_PAD = 128
SHARDS = CHANNELS // CHUNK
PAIR = 2 * CHUNK

EPSILON = 1e-05
PAIR_SCALE = 4.0
MESH = pl.DeviceIdType.MESH
HBM = pl.ANY
VMEM_LIMIT = 62 * 2**20

f32 = jnp.float32
bf16 = jnp.bfloat16


def dot(a, b, dims=((1,), (0,))):
    return lax.dot_general(a, b, (dims, ((), ())), preferred_element_type=f32)


def img_barrier(size):
    stream = lax.axis_index("stream")
    me = lax.axis_index("img")
    barrier = pltpu.get_barrier_semaphore()

    def greet(step, carry):
        pl.semaphore_signal(
            barrier, inc=1, device_id=(stream, lax.rem(me + step, size)), device_id_type=MESH
        )
        return carry

    lax.fori_loop(1, size, greet, 0)
    return barrier


def send_sums(size, slot, packed, sent, got, send_sem, recv_sem):
    stream = lax.axis_index("stream")
    me = lax.axis_index("img")
    sent[slot] = packed
    got[slot, me] = packed

    def send(step, carry):
        pltpu.make_async_remote_copy(
            src_ref=sent.at[slot],
            dst_ref=got.at[slot, me],
            send_sem=send_sem.at[slot],
            recv_sem=recv_sem.at[slot],
            device_id=(stream, lax.rem(me + step, size)),
            device_id_type=MESH,
        ).start()
        return carry

    lax.fori_loop(1, size, send, 0)


def take_sums(size, slot, got, send_sem, recv_sem):
    others = got.at[slot, pl.ds(0, size - 1)]
    pltpu.make_async_copy(others, others, recv_sem.at[slot]).wait()
    pltpu.make_async_copy(others, others, send_sem.at[slot]).wait()
    total = got[slot, 0]
    for peer in range(1, size):
        total = total + got[slot, peer]
    return total


def row_count(size):
    live = jnp.where(lax.axis_index("stream") == 0, IMAGE_ROWS, SMALL_ROWS)
    return (live * (size * (IMAGE_DEV // MICRO_BATCHES))).astype(f32)


def column_sum(values):
    return jnp.sum(values, axis=0, keepdims=True)


def moments(total, micro, tile, count):
    mean = total[4 * micro + tile : 4 * micro + tile + 1] / count
    square = total[4 * micro + 2 + tile : 4 * micro + 3 + tile] / count
    return mean, lax.rsqrt(square - mean * mean + EPSILON)


def edge_masks():
    place = np.arange(PAD_ROWS) - TOP
    column = (place % 212) % 14
    left = (column != 13).astype(np.float32)
    right = (column != 0).astype(np.float32)
    both = np.stack([left, right])
    return jnp.broadcast_to(jnp.asarray(both)[:, :, None], (2, PAD_ROWS, 128)).astype(bf16)


def scatter_rows(rows_ref, pads, edges):
    on_global = lax.axis_index("stream") == 0
    inside = lax.broadcasted_iota(jnp.int32, (200, 128), 0)

    @pl.when(on_global)
    def _():
        for image in range(IMAGE_DEV):
            for tile in range(2):
                start = IMAGE_ROWS * image
                base = TOP + IMAGE_PAD * image
                first = jnp.where(inside < 196, rows_ref[tile, start : start + 200], 0.0)
                second = jnp.where(
                    inside >= 4, rows_ref[tile, start + 192 : start + 392], 0.0
                )
                for place, piece in ((base, first), (base + 208, second)):
                    here = slice(place, place + 200)
                    pads[0, tile, here] = piece
                    pads[1, tile, here] = piece * edges[0, here].astype(f32)
                    pads[2, tile, here] = piece * edges[1, here].astype(f32)

    @pl.when(jnp.logical_not(on_global))
    def _():
        for image in range(IMAGE_DEV):
            for crop in range(SMALL_CROPS):
                for line in range(SMALL_SIDE):
                    start = IMAGE_ROWS * image + 49 * crop + 7 * line
                    base = TOP + IMAGE_PAD * image + 114 * crop + 14 * line
                    for tile in range(2):
                        piece = rows_ref[tile, start : start + 7]
                        for kind in range(3):
                            pads[kind, tile, base : base + 7] = piece


def compact_rows(wide, image, rows_ref, slot):
    start = IMAGE_ROWS * image
    inside = lax.broadcasted_iota(jnp.int32, (8, 128), 0)
    for tile in range(2):
        lanes = slice(128 * tile, 128 * tile + 128)
        rows_ref[slot, tile, start : start + 192] = wide[0:192, lanes]
        rows_ref[slot, tile, start + 192 : start + 200] = jnp.where(
            inside < 4, wide[192:200, lanes], wide[208:216, lanes]
        )
        rows_ref[slot, tile, start + 200 : start + 392] = wide[216:408, lanes]


def compact_small(wide_ref, image, rows_ref, slot):
    for crop in range(SMALL_CROPS):
        for line in range(SMALL_SIDE):
            start = IMAGE_ROWS * image + 49 * crop + 7 * line
            base = 114 * crop + 14 * line
            for tile in range(2):
                rows_ref[slot, tile, start : start + 7] = wide_ref[tile, base : base + 7]


def take_result(wide, image, rows_ref, slot, wide_ref):
    on_global = lax.axis_index("stream") == 0

    @pl.when(on_global)
    def _():
        compact_rows(wide, image, rows_ref, slot)

    @pl.when(jnp.logical_not(on_global))
    def _():
        wide_ref[0] = wide[:, 0:128]
        wide_ref[1] = wide[:, 128:256]
        compact_small(wide_ref, image, rows_ref, slot)


def stack_windows(pads, windows, image, sign):
    for offset in range(9):
        down, across = offset // 3 - 1, offset % 3 - 1
        shift = sign * (14 * down + across)
        kind = (0, 2, 1)[sign * across]
        start = TOP + IMAGE_PAD * image + shift
        for tile in range(2):
            at = LANES * offset + 128 * tile
            windows[IMAGE_PAD * image : IMAGE_PAD * (image + 1), at : at + 128] = pads[
                kind, tile, start : start + IMAGE_PAD
            ].astype(bf16)


def same_group(rows, lanes):
    row_group = lax.broadcasted_iota(jnp.int32, (rows, lanes), 0) // GROUP_WIDTH
    lane_group = lax.broadcasted_iota(jnp.int32, (rows, lanes), 1) // GROUP_WIDTH
    return row_group == lane_group


def entry_kernel(
    size,
    x_ref,
    weight_ref,
    conv_ref,
    param_ref,
    pool_ref,
    edges,
    fold_ref,
    act_out,
    turned_out,
    group_out,
    mixed_out,
    pooled_out,
    total_out,
    first_rows,
    second_rows,
    rows_ref,
    pads,
    windows,
    wide_ref,
    full_ref,
    sent,
    got,
    send_sem,
    recv_sem,
):
    step = pl.program_id(0)
    count = row_count(size)

    @pl.when(step == 0)
    def _():
        barrier = img_barrier(size)
        pads[...] = jnp.zeros_like(pads)
        full_ref[...] = jnp.zeros_like(full_ref)
        second_rows[...] = jnp.zeros_like(second_rows)
        pl.semaphore_wait(barrier, size - 1)

    @pl.when(step < BLOCKS)
    def _():
        slot = lax.rem(step, 2)
        parts = []
        for micro in range(MICRO_BATCHES):
            here = slice(HALF * micro, HALF * (micro + 1))
            act = dot(x_ref[here], weight_ref[...])
            act_out[here] = act
            for tile in range(2):
                first_rows[slot, tile, here] = act[:, 128 * tile : 128 * tile + 128]
            plain = column_sum(act)
            square = column_sum(act * act)
            parts += [plain[:, :128], plain[:, 128:], square[:, :128], square[:, 128:]]
        send_sums(size, step, jnp.concatenate(parts), sent, got, send_sem, recv_sem)

    @pl.when((step >= 1) & (step < BLOCKS + 1))
    def _():
        block = step - 1
        slot = lax.rem(block, 2)
        total = take_sums(size, block, got, send_sem, recv_sem)
        total_out[block, 0] = total
        param = param_ref[block]
        for micro in range(MICRO_BATCHES):
            here = slice(HALF * micro, HALF * (micro + 1))
            for tile in range(2):
                mean, inverse = moments(total, micro, tile, count)
                scale = 0.5 * inverse * param[tile : tile + 1]
                shift = 0.5 * param[2 + tile : 3 + tile] - mean * scale
                half = first_rows[slot, tile, here] * scale + shift
                rows_ref[tile, here] = half + half * jnp.tanh(half)
        scatter_rows(rows_ref, pads, edges)
        for tile in range(2):
            turned_out[0, 128 * tile : 128 * tile + 128] = pads[
                0, tile, TOP : TOP + DEEP_ROWS
            ].T.astype(bf16)
        same = same_group(BLOCK, LANES)
        for offset in range(9):
            full = dot(conv_ref[offset], fold_ref[...])
            full_ref[LANES * offset : LANES * offset + BLOCK] = jnp.where(
                same, full, 0.0
            ).astype(bf16)
        for image in range(IMAGE_DEV):
            stack_windows(pads, windows, image, 1)
            here = slice(IMAGE_PAD * image, IMAGE_PAD * (image + 1))
            wide = dot(windows[here], full_ref[...])
            take_result(wide, image, second_rows, slot, wide_ref)
        parts = []
        for micro in range(MICRO_BATCHES):
            here = slice(HALF * micro, HALF * (micro + 1))
            acts = [second_rows[slot, tile, here] for tile in range(2)]
            parts += [column_sum(act) for act in acts]
            parts += [column_sum(act * act) for act in acts]
        send_sums(
            size, BLOCKS + block, jnp.concatenate(parts), sent, got, send_sem, recv_sem
        )

    @pl.when(step >= 2)
    def _():
        block = step - 2
        slot = lax.rem(block, 2)
        total = take_sums(size, BLOCKS + block, got, send_sem, recv_sem)
        total_out[block, 1] = total
        param = param_ref[block]
        for micro in range(MICRO_BATCHES):
            here = slice(HALF * micro, HALF * (micro + 1))
            for tile in range(2):
                lanes = slice(128 * tile, 128 * tile + 128)
                mean, inverse = moments(total, micro, tile, count)
                scale = 0.5 * inverse * param[4 + tile : 5 + tile]
                shift = 0.5 * param[6 + tile : 7 + tile] - mean * scale
                act = second_rows[slot, tile, here]
                group_out[here, lanes] = act
                half = act * scale + shift
                mixed_out[here, lanes] = (half + half * jnp.tanh(half)).astype(bf16)
        pooled_out[...] = dot(pool_ref[...], mixed_out[...])


def run_entry(size, x, weight, conv, params, pool, edges, fold):
    def whole(shape):
        return pl.BlockSpec(shape, lambda i: (0,) * len(shape), pipeline_mode=pl.Buffered(1))

    def at(lag):
        return lambda i: jnp.clip(i - lag, 0, BLOCKS - 1)

    return pl.pallas_call(
        functools.partial(entry_kernel, size),
        grid=(BLOCKS + 2,),
        out_shape=(
            jax.ShapeDtypeStruct((ROWS, WIDE), f32),
            jax.ShapeDtypeStruct((BLOCKS, LANES, DEEP_ROWS), bf16),
            jax.ShapeDtypeStruct((ROWS, WIDE), f32),
            jax.ShapeDtypeStruct((ROWS, WIDE), bf16),
            jax.ShapeDtypeStruct((CROPS, WIDE), f32),
            jax.ShapeDtypeStruct((BLOCKS, 2, 8, 128), f32),
        ),
        in_specs=[
            whole((ROWS, PADDED)),
            pl.BlockSpec((PADDED, LANES), lambda i: (0, at(0)(i))),
            pl.BlockSpec((9, BLOCK, GROUP_WIDTH), lambda i: (0, at(1)(i), 0)),
            whole((BLOCKS, 8, 128)),
            whole((CROPS, ROWS)),
            whole((2, PAD_ROWS, 128)),
            whole((GROUP_WIDTH, LANES)),
        ],
        out_specs=(
            pl.BlockSpec((ROWS, LANES), lambda i: (0, at(0)(i))),
            pl.BlockSpec((1, LANES, DEEP_ROWS), lambda i: (at(1)(i), 0, 0)),
            pl.BlockSpec((ROWS, LANES), lambda i: (0, at(2)(i))),
            pl.BlockSpec((ROWS, LANES), lambda i: (0, at(2)(i))),
            pl.BlockSpec((CROPS, LANES), lambda i: (0, at(2)(i))),
            pl.BlockSpec((BLOCKS, 2, 8, 128), lambda i: (0, 0, 0, 0)),
        ),
        scratch_shapes=[
            pltpu.VMEM((2, 2, ROWS, 128), f32),
            pltpu.VMEM((2, 2, ROWS, 128), f32),
            pltpu.VMEM((2, ROWS, 128), f32),
            pltpu.VMEM((3, 2, PAD_ROWS, 128), f32),
            pltpu.VMEM((CONV_ROWS, 9 * LANES), bf16),
            pltpu.VMEM((2, IMAGE_PAD, 128), f32),
            pltpu.VMEM((9 * LANES, LANES), bf16),
            pltpu.VMEM((2 * BLOCKS, 8, 128), f32),
            pltpu.VMEM((2 * BLOCKS, size, 8, 128), f32),
            pltpu.SemaphoreType.DMA((2 * BLOCKS,)),
            pltpu.SemaphoreType.DMA((2 * BLOCKS,)),
        ],
        name="entry",
        compiler_params=pltpu.CompilerParams(
            collective_id=1, has_side_effects=True, vmem_limit_bytes=VMEM_LIMIT
        ),
        cost_estimate=pl.CostEstimate(
            flops=2 * ROWS * WIDE * (PADDED + 9 * LANES),
            bytes_accessed=70 * 2**20,
            transcendentals=2 * ROWS * WIDE,
        ),
    )(x, weight, conv, params, pool, edges, fold)


def whole(shape):
    return pl.BlockSpec(shape, lambda i: (0,) * len(shape), pipeline_mode=pl.Buffered(1))


def columns(rows, lag, blocks):
    return pl.BlockSpec((rows, LANES), lambda i: (0, jnp.clip(i - lag, 0, blocks - 1)))


def lane_halves(values):
    return [values[:, :128], values[:, 128:]]


def exit_kernel(
    size,
    scaled_ref,
    turned_ref,
    weight_ref,
    x_ref,
    cot_ref,
    param_ref,
    pair_ref,
    spread_ref,
    live_ref,
    out_out,
    delta_out,
    residual_out,
    weight_out,
    total_out,
    normed_ref,
    slope_ref,
    pair_sent,
    pair_got,
    sent,
    got,
    send_sem,
    recv_sem,
    pair_send,
    pair_recv,
):
    step = pl.program_id(0)
    count = row_count(size)
    stream = lax.axis_index("stream")
    me = lax.axis_index("img")
    area = jnp.where(stream == 0, GLOBAL_SIDE**2, SMALL_SIDE**2).astype(f32)
    blocks = OUT_BLOCKS

    def pair_copy(block):
        return pltpu.make_async_remote_copy(
            src_ref=pair_sent.at[block],
            dst_ref=pair_got.at[block],
            send_sem=pair_send.at[block],
            recv_sem=pair_recv.at[block],
            device_id=(1 - stream, me),
            device_id_type=MESH,
        )

    @pl.when(step == 0)
    def _():
        barrier = img_barrier(size)
        pl.semaphore_signal(
            barrier, inc=1, device_id=(1 - stream, me), device_id_type=MESH
        )
        pl.semaphore_wait(barrier, size)

    @pl.when(step < blocks)
    def _():
        slot = lax.rem(step, 4)
        parts = []
        for micro in range(MICRO_BATCHES):
            here = slice(HALF * micro, HALF * (micro + 1))
            act = dot(scaled_ref[here], weight_ref[...])
            normed_ref[slot, here] = act
            parts += lane_halves(column_sum(act)) + lane_halves(column_sum(act * act))
        send_sums(size, step, jnp.concatenate(parts), sent, got, send_sem, recv_sem)

    @pl.when((step >= 1) & (step < blocks + 1))
    def _():
        block = step - 1
        slot = lax.rem(block, 4)
        total = take_sums(size, block, got, send_sem, recv_sem)
        total_out[block, 0] = total
        param = param_ref[block]
        for micro in range(MICRO_BATCHES):
            here = slice(HALF * micro, HALF * (micro + 1))
            for tile in range(2):
                lanes = slice(128 * tile, 128 * tile + 128)
                mean, inverse = moments(total, micro, tile, count)
                normed = normed_ref[slot, here, lanes] * inverse - mean * inverse
                normed_ref[slot, here, lanes] = normed
                gain = 0.5 * param[tile : tile + 1]
                shift = 0.5 * param[2 + tile : 3 + tile]
                half = 0.5 * x_ref[here, lanes].astype(f32) + (normed * gain + shift)
                bent = jnp.tanh(half)
                out_out[here, lanes] = (
                    (half + half * bent) * live_ref[here].astype(f32)
                ).astype(bf16)
                slope_ref[lax.rem(block, 3), here, lanes] = (0.5 + 0.5 * bent) * (
                    1.0 + half * (1.0 - bent)
                )
        embed = dot(pair_ref[...], out_out[...]) / area
        pair_sent[block] = embed[:8].astype(bf16).astype(f32)
        pair_copy(block).start()

    @pl.when((step >= 2) & (step < blocks + 2))
    def _():
        block = step - 2
        slot = lax.rem(block, 4)
        pair_copy(block).wait()
        partner = pair_got[block]
        partner = jnp.concatenate([partner, jnp.zeros_like(partner)]).astype(bf16)
        parts = []
        for micro in range(MICRO_BATCHES):
            here = slice(HALF * micro, HALF * (micro + 1))
            pull = dot(spread_ref[here], partner) * (PAIR_SCALE / area)
            upstream = cot_ref[here].astype(f32) + pull
            delta = upstream * slope_ref[lax.rem(block, 3), here]
            slope_ref[lax.rem(block, 3), here] = delta
            residual_out[here] = delta.astype(bf16)
            parts += lane_halves(column_sum(delta))
            parts += lane_halves(column_sum(delta * normed_ref[slot, here]))
        send_sums(
            size, blocks + block, jnp.concatenate(parts), sent, got, send_sem, recv_sem
        )

    @pl.when(step >= 3)
    def _():
        block = step - 3
        slot = lax.rem(block, 4)
        moment = total_out[block, 0]
        total = take_sums(size, blocks + block, got, send_sem, recv_sem)
        total_out[block, 1] = total
        param = param_ref[block]
        for micro in range(MICRO_BATCHES):
            here = slice(HALF * micro, HALF * (micro + 1))
            for tile in range(2):
                lanes = slice(128 * tile, 128 * tile + 128)
                delta_out[here, lanes] = norm_back(
                    slope_ref[lax.rem(block, 3), here, lanes],
                    normed_ref[slot, here, lanes],
                    moment,
                    total,
                    micro,
                    tile,
                    param[tile : tile + 1],
                    count,
                ).astype(bf16)
        weight_out[...] = dot(turned_ref[...], delta_out[...]).astype(bf16)


def norm_back(upstream, normed, moment, total, micro, tile, gain, count):
    _, inverse = moments(moment, micro, tile, count)
    scale = gain * inverse
    plain = total[4 * micro + tile : 4 * micro + tile + 1] / count
    along = total[4 * micro + 2 + tile : 4 * micro + 3 + tile] / count
    return scale * upstream - (scale * plain + normed * (scale * along))


def run_exit(size, scaled, turned, weight, x, cot, params, pair, spread, live):
    blocks = OUT_BLOCKS
    return pl.pallas_call(
        functools.partial(exit_kernel, size),
        grid=(blocks + 3,),
        out_shape=(
            jax.ShapeDtypeStruct((ROWS, CHANNELS), bf16),
            jax.ShapeDtypeStruct((ROWS, PADDED), bf16),
            jax.ShapeDtypeStruct((ROWS, PADDED), bf16),
            jax.ShapeDtypeStruct((PADDED, PADDED), bf16),
            jax.ShapeDtypeStruct((blocks, 2, 8, 128), f32),
        ),
        in_specs=[
            whole((ROWS, PADDED)),
            whole((PADDED, ROWS)),
            columns(PADDED, 0, blocks),
            columns(ROWS, 1, blocks),
            columns(ROWS, 2, blocks),
            whole((blocks, 8, 128)),
            whole((CROPS, ROWS)),
            whole((ROWS, CROPS)),
            whole((ROWS, 128)),
        ],
        out_specs=(
            columns(ROWS, 1, blocks),
            columns(ROWS, 3, blocks),
            columns(ROWS, 2, blocks),
            columns(PADDED, 3, blocks),
            pl.BlockSpec((blocks, 2, 8, 128), lambda i: (0, 0, 0, 0)),
        ),
        scratch_shapes=[
            pltpu.VMEM((4, ROWS, LANES), f32),
            pltpu.VMEM((3, ROWS, LANES), f32),
            pltpu.VMEM((blocks, 8, LANES), f32),
            pltpu.VMEM((blocks, 8, LANES), f32),
            pltpu.VMEM((2 * blocks, 8, 128), f32),
            pltpu.VMEM((2 * blocks, size, 8, 128), f32),
            pltpu.SemaphoreType.DMA((2 * blocks,)),
            pltpu.SemaphoreType.DMA((2 * blocks,)),
            pltpu.SemaphoreType.DMA((blocks,)),
            pltpu.SemaphoreType.DMA((blocks,)),
        ],
        name="exit",
        compiler_params=pltpu.CompilerParams(
            collective_id=2, has_side_effects=True, vmem_limit_bytes=VMEM_LIMIT
        ),
        cost_estimate=pl.CostEstimate(
            flops=4 * ROWS * PADDED * PADDED,
            bytes_accessed=70 * 2**20,
            transcendentals=ROWS * PADDED,
        ),
    )(scaled, turned, weight, x, cot, params, pair, spread, live)


def gate_kernel(delta_ref, weight_ref, mixed_ref, pool_ref, scaled_out, gate_out):
    block = pl.program_id(0)
    first = jnp.minimum((BLOCK * block) // CHUNK, SHARDS - 3)
    row = lax.broadcasted_iota(jnp.int32, (LANES, 3 * CHUNK_PAD), 0)
    lane = lax.broadcasted_iota(jnp.int32, (LANES, 3 * CHUNK_PAD), 1)
    channel = CHUNK * (first + lane // CHUNK_PAD) + lane % CHUNK_PAD
    pick = (channel == BLOCK * block + row) & (row < BLOCK) & (lane % CHUNK_PAD < CHUNK)
    rows = pl.ds(pl.multiple_of(CHUNK_PAD * first, CHUNK_PAD), 3 * CHUNK_PAD)
    weight = dot(jnp.where(pick, 1.0, 0.0).astype(bf16), weight_ref[rows]).astype(bf16)
    grad = dot(delta_ref[...], weight, ((1,), (1,)))
    scaled_out[...] = grad
    gate_out[...] = dot(pool_ref[...], (grad * mixed_ref[...].astype(f32)).astype(bf16))


def run_gate(delta, weight, mixed, pool):
    return pl.pallas_call(
        gate_kernel,
        grid=(BLOCKS,),
        out_shape=(
            jax.ShapeDtypeStruct((ROWS, WIDE), f32),
            jax.ShapeDtypeStruct((CROPS, WIDE), f32),
        ),
        in_specs=[
            whole((ROWS, PADDED)),
            whole((PADDED, PADDED)),
            columns(ROWS, 0, BLOCKS),
            whole((CROPS, ROWS)),
        ],
        out_specs=(columns(ROWS, 0, BLOCKS), columns(CROPS, 0, BLOCKS)),
        name="gate",
        compiler_params=pltpu.CompilerParams(vmem_limit_bytes=VMEM_LIMIT),
        cost_estimate=pl.CostEstimate(
            flops=2 * ROWS * WIDE * PADDED, bytes_accessed=40 * 2**20, transcendentals=0
        ),
    )(delta, weight, mixed, pool)


def pair_lane(shape, dim):
    lane = lax.broadcasted_iota(jnp.int32, shape, dim)
    inside = lane % CHUNK_PAD
    return jnp.where(inside < CHUNK, CHUNK * (lane // CHUNK_PAD) + inside, -1)


def one_hot(match):
    return jnp.where(match, 1.0, 0.0).astype(bf16)


def prepare_kernel(x_ref, chunk_out, turned_out):
    pair = pl.program_id(0)
    depth = 384
    first = (PAIR * pair) // 128
    lanes = pl.ds(pl.multiple_of(128 * first, 128), depth)
    source = 128 * first - PAIR * pair
    there = lax.broadcasted_iota(jnp.int32, (depth, LANES), 0) + source
    pick = one_hot(there == pair_lane((depth, LANES), 1))
    chunk_out[...] = dot(x_ref[:, lanes], pick).astype(bf16)
    there = lax.broadcasted_iota(jnp.int32, (LANES, depth), 1) + source
    pick = one_hot(there == pair_lane((LANES, depth), 0))
    turned_out[...] = dot(pick, x_ref[:, lanes], ((1,), (1,))).astype(bf16)


def run_prepare(x):
    return pl.pallas_call(
        prepare_kernel,
        grid=(OUT_BLOCKS,),
        out_shape=(
            jax.ShapeDtypeStruct((ROWS, PADDED), bf16),
            jax.ShapeDtypeStruct((PADDED, ROWS), bf16),
        ),
        in_specs=[whole((ROWS, PADDED))],
        out_specs=(columns(ROWS, 0, OUT_BLOCKS), pl.BlockSpec((LANES, ROWS), lambda i: (i, 0))),
        name="prepare",
        compiler_params=pltpu.CompilerParams(vmem_limit_bytes=VMEM_LIMIT),
        cost_estimate=pl.CostEstimate(
            flops=4 * ROWS * 384 * PADDED, bytes_accessed=20 * 2**20, transcendentals=0
        ),
    )(x)


def scale_kernel(mixed_ref, gates_ref, spread_ref, scaled_out, turned_out, scaled):
    step = pl.program_id(0)

    @pl.when(step < BLOCKS)
    def _():
        gate = dot(spread_ref[...], gates_ref[...])
        lanes = pl.ds(pl.multiple_of(LANES * step, LANES), LANES)
        scaled[:, lanes] = (mixed_ref[...].astype(f32) * gate).astype(bf16)

    @pl.when(step >= BLOCKS)
    def _():
        pair = step - BLOCKS
        depth = 512
        start = PAIR * pair
        first = jnp.minimum((start + (LANES - BLOCK) * (start // BLOCK)) // 128, WIDE // 128 - 4)
        lanes = pl.ds(pl.multiple_of(128 * first, 128), depth)

        def pick(shape, dim):
            inside = pair_lane(shape, dim)
            channel = start + inside
            place = channel + (LANES - BLOCK) * (channel // BLOCK) - 128 * first
            there = lax.broadcasted_iota(jnp.int32, shape, 1 - dim)
            return one_hot((there == place) & (inside >= 0))

        scaled_out[...] = dot(scaled[:, lanes], pick((depth, LANES), 1)).astype(bf16)
        turned_out[...] = dot(pick((LANES, depth), 0), scaled[:, lanes], ((1,), (1,))).astype(
            bf16
        )


def run_scale(mixed, gates, spread):
    def pair(i):
        return jnp.maximum(i - BLOCKS, 0)

    return pl.pallas_call(
        scale_kernel,
        grid=(BLOCKS + OUT_BLOCKS,),
        out_shape=(
            jax.ShapeDtypeStruct((ROWS, PADDED), bf16),
            jax.ShapeDtypeStruct((PADDED, ROWS), bf16),
        ),
        in_specs=[
            columns(ROWS, 0, BLOCKS),
            columns(2 * CROPS, 0, BLOCKS),
            whole((ROWS, 2 * CROPS)),
        ],
        out_specs=(
            pl.BlockSpec((ROWS, LANES), lambda i: (0, pair(i))),
            pl.BlockSpec((LANES, ROWS), lambda i: (pair(i), 0)),
        ),
        scratch_shapes=[pltpu.VMEM((ROWS, WIDE), bf16)],
        name="scale",
        compiler_params=pltpu.CompilerParams(vmem_limit_bytes=VMEM_LIMIT),
        cost_estimate=pl.CostEstimate(
            flops=4 * ROWS * 512 * PADDED, bytes_accessed=30 * 2**20, transcendentals=0
        ),
    )(mixed, gates, spread)


def back_kernel(
    size,
    grad_ref,
    group_ref,
    gates_ref,
    spread_ref,
    act_ref,
    turned_ref,
    conv_ref,
    x_turned_ref,
    param_ref,
    moment_ref,
    edges,
    fold_ref,
    delta_out,
    weight_out,
    conv_out,
    total_out,
    normed_two,
    delta_two,
    normed_one,
    delta_one,
    rows_ref,
    pads,
    windows,
    wide_ref,
    full_ref,
    sent,
    got,
    send_sem,
    recv_sem,
):
    step = pl.program_id(0)
    count = row_count(size)

    @pl.when(step == 0)
    def _():
        barrier = img_barrier(size)
        pads[...] = jnp.zeros_like(pads)
        full_ref[...] = jnp.zeros_like(full_ref)
        delta_one[...] = jnp.zeros_like(delta_one)
        windows[CONV_ROWS:] = jnp.zeros_like(windows[CONV_ROWS:])
        pl.semaphore_wait(barrier, size - 1)

    @pl.when(step < BLOCKS)
    def _():
        slot = lax.rem(step, 2)
        moment = moment_ref[step, 1]
        param = param_ref[step]
        parts = []
        for micro in range(MICRO_BATCHES):
            here = slice(HALF * micro, HALF * (micro + 1))
            sums = []
            products = []
            for tile in range(2):
                lanes = slice(128 * tile, 128 * tile + 128)
                mean, inverse = moments(moment, micro, tile, count)
                normed = group_ref[here, lanes] * inverse - mean * inverse
                gain = 0.5 * param[4 + tile : 5 + tile]
                half = normed * gain + 0.5 * param[6 + tile : 7 + tile]
                bent = jnp.tanh(half)
                slope = (0.5 + 0.5 * bent) * (1.0 + half * (1.0 - bent))
                gate = dot(spread_ref[here], gates_ref[0, :, lanes])
                pooled = dot(spread_ref[here], gates_ref[1, :, lanes])
                delta = (grad_ref[here, lanes] * gate + pooled) * slope
                normed_two[slot, tile, here] = normed
                delta_two[slot, tile, here] = delta
                sums.append(column_sum(delta))
                products.append(column_sum(delta * normed))
            parts += sums + products
        send_sums(size, step, jnp.concatenate(parts), sent, got, send_sem, recv_sem)

    @pl.when((step >= 1) & (step < BLOCKS + 1))
    def _():
        block = step - 1
        slot = lax.rem(block, 2)
        total = take_sums(size, block, got, send_sem, recv_sem)
        total_out[block, 0] = total
        param = param_ref[block]
        moment = moment_ref[block, 1]
        for micro in range(MICRO_BATCHES):
            here = slice(HALF * micro, HALF * (micro + 1))
            for tile in range(2):
                rows_ref[tile, here] = norm_back(
                    delta_two[slot, tile, here],
                    normed_two[slot, tile, here],
                    moment,
                    total,
                    micro,
                    tile,
                    param[4 + tile : 5 + tile],
                    count,
                )
        scatter_rows(rows_ref, pads, edges)
        same = same_group(LANES, BLOCK)
        for offset in range(9):
            full = dot(fold_ref[...], conv_ref[offset], ((1,), (1,)))
            full_ref[LANES * offset : LANES * (offset + 1), :BLOCK] = jnp.where(
                same, full, 0.0
            ).astype(bf16)
        for image in range(IMAGE_DEV):
            stack_windows(pads, windows, image, -1)
            here = slice(IMAGE_PAD * image, IMAGE_PAD * (image + 1))
            wide = dot(windows[here], full_ref[...])
            take_result(wide, image, delta_one, slot, wide_ref)
        same = same_group(LANES, LANES)
        for offset in range(9):
            lanes = slice(LANES * offset, LANES * (offset + 1))
            grad = dot(turned_ref[0], windows[:, lanes])
            grad = jnp.where(same, grad, 0.0).astype(bf16)
            conv_out[offset] = dot(grad, fold_ref[...])[:BLOCK].astype(bf16)
        moment = moment_ref[block, 0]
        parts = []
        for micro in range(MICRO_BATCHES):
            here = slice(HALF * micro, HALF * (micro + 1))
            sums = []
            products = []
            for tile in range(2):
                lanes = slice(128 * tile, 128 * tile + 128)
                mean, inverse = moments(moment, micro, tile, count)
                normed = act_ref[here, lanes] * inverse - mean * inverse
                gain = 0.5 * param[tile : tile + 1]
                half = normed * gain + 0.5 * param[2 + tile : 3 + tile]
                bent = jnp.tanh(half)
                slope = (0.5 + 0.5 * bent) * (1.0 + half * (1.0 - bent))
                delta = delta_one[slot, tile, here] * slope
                normed_one[slot, tile, here] = normed
                delta_one[slot, tile, here] = delta
                sums.append(column_sum(delta))
                products.append(column_sum(delta * normed))
            parts += sums + products
        send_sums(
            size, BLOCKS + block, jnp.concatenate(parts), sent, got, send_sem, recv_sem
        )

    @pl.when(step >= 2)
    def _():
        block = step - 2
        slot = lax.rem(block, 2)
        total = take_sums(size, BLOCKS + block, got, send_sem, recv_sem)
        total_out[block, 1] = total
        param = param_ref[block]
        moment = moment_ref[block, 0]
        for micro in range(MICRO_BATCHES):
            here = slice(HALF * micro, HALF * (micro + 1))
            for tile in range(2):
                delta_out[here, 128 * tile : 128 * tile + 128] = norm_back(
                    delta_one[slot, tile, here],
                    normed_one[slot, tile, here],
                    moment,
                    total,
                    micro,
                    tile,
                    param[tile : tile + 1],
                    count,
                ).astype(bf16)
        weight_out[...] = dot(x_turned_ref[...], delta_out[...]).astype(bf16)


def run_back(
    size, grad, group, gates, spread, act, turned, conv, x_turned, params, moment, edges, fold
):
    return pl.pallas_call(
        functools.partial(back_kernel, size),
        grid=(BLOCKS + 2,),
        out_shape=(
            jax.ShapeDtypeStruct((ROWS, WIDE), bf16),
            jax.ShapeDtypeStruct((PADDED, WIDE), bf16),
            jax.ShapeDtypeStruct((9, CHANNELS, GROUP_WIDTH), bf16),
            jax.ShapeDtypeStruct((BLOCKS, 2, 8, 128), f32),
        ),
        in_specs=[
            columns(ROWS, 0, BLOCKS),
            columns(ROWS, 0, BLOCKS),
            pl.BlockSpec((2, 2 * CROPS, LANES), lambda i: (0, 0, jnp.clip(i, 0, BLOCKS - 1))),
            whole((ROWS, 2 * CROPS)),
            columns(ROWS, 1, BLOCKS),
            pl.BlockSpec((1, LANES, DEEP_ROWS), lambda i: (jnp.clip(i - 1, 0, BLOCKS - 1), 0, 0)),
            pl.BlockSpec((9, BLOCK, GROUP_WIDTH), lambda i: (0, jnp.clip(i - 1, 0, BLOCKS - 1), 0)),
            whole((PADDED, ROWS)),
            whole((BLOCKS, 8, 128)),
            whole((BLOCKS, 2, 8, 128)),
            whole((2, PAD_ROWS, 128)),
            whole((LANES, GROUP_WIDTH)),
        ],
        out_specs=(
            columns(ROWS, 2, BLOCKS),
            columns(PADDED, 2, BLOCKS),
            pl.BlockSpec((9, BLOCK, GROUP_WIDTH), lambda i: (0, jnp.clip(i - 1, 0, BLOCKS - 1), 0)),
            pl.BlockSpec((BLOCKS, 2, 8, 128), lambda i: (0, 0, 0, 0)),
        ),
        scratch_shapes=[
            pltpu.VMEM((2, 2, ROWS, 128), f32),
            pltpu.VMEM((2, 2, ROWS, 128), f32),
            pltpu.VMEM((2, 2, ROWS, 128), f32),
            pltpu.VMEM((2, 2, ROWS, 128), f32),
            pltpu.VMEM((2, ROWS, 128), f32),
            pltpu.VMEM((3, 2, PAD_ROWS, 128), f32),
            pltpu.VMEM((DEEP_ROWS, 9 * LANES), bf16),
            pltpu.VMEM((2, IMAGE_PAD, 128), f32),
            pltpu.VMEM((9 * LANES, LANES), bf16),
            pltpu.VMEM((2 * BLOCKS, 8, 128), f32),
            pltpu.VMEM((2 * BLOCKS, size, 8, 128), f32),
            pltpu.SemaphoreType.DMA((2 * BLOCKS,)),
            pltpu.SemaphoreType.DMA((2 * BLOCKS,)),
        ],
        name="back",
        compiler_params=pltpu.CompilerParams(
            collective_id=3, has_side_effects=True, vmem_limit_bytes=VMEM_LIMIT
        ),
        cost_estimate=pl.CostEstimate(
            flops=2 * ROWS * WIDE * (PADDED + 18 * LANES),
            bytes_accessed=90 * 2**20,
            transcendentals=2 * ROWS * WIDE,
        ),
    )(grad, group, gates, spread, act, turned, conv, x_turned, params, moment, edges, fold)


def split(values):
    high = values.astype(bf16)
    low = (values - high.astype(f32)).astype(bf16)
    return jnp.concatenate([high, low], axis=-2)


def silu_slope(values):
    sig_vals = jax.nn.sigmoid(values)
    return sig_vals * (1.0 + values * (1.0 - sig_vals))


def wide_lanes(values):
    lead = values.shape[:-1]
    blocks = values.reshape(lead + (BLOCKS, BLOCK))
    padded = jnp.pad(blocks, ((0, 0),) * len(lead) + ((0, 0), (0, LANES - BLOCK)))
    return padded.reshape(lead + (WIDE,))


def narrow_lanes(values):
    lead = values.shape[:-1]
    return values.reshape(lead + (BLOCKS, LANES))[..., :BLOCK].reshape(lead + (CHANNELS,))


def gather(piece, width, size):
    across = -(-width // 128) * 128
    pads = ((0, CHUNK_PAD - CHUNK), (0, across - width))
    if size == SHARDS:
        piece = jnp.pad(piece.reshape(CHUNK, width), pads)
        return lax.all_gather(piece, "img", axis=0, tiled=True)
    pieces = lax.all_gather(piece, "img", axis=0, tiled=True).reshape(SHARDS, CHUNK, width)
    return jnp.pad(pieces, ((0, 0),) + pads).reshape(PADDED, across)


def scatter(grads, width, size):
    if size == SHARDS:
        part = lax.psum_scatter(grads, "img", scatter_dimension=0, tiled=True)
        part = swap_sum(part)
        return part[:CHUNK, :width].reshape(-1)
    grads = grads.reshape(SHARDS, CHUNK_PAD, -1)[:, :CHUNK, :width].reshape(-1)
    return swap_sum(lax.psum_scatter(grads, "img", scatter_dimension=0, tiled=True))


def swap_sum(part):
    other = lax.ppermute(part, "stream", [(0, 1), (1, 0)])
    return part.astype(f32) + other.astype(f32)


def chunked(values):
    lead = values.shape[:-1]
    values = values.reshape(lead + (SHARDS, CHUNK))
    values = jnp.pad(values, ((0, 0),) * len(lead) + ((0, 0), (0, CHUNK_PAD - CHUNK)))
    return values.reshape(lead + (PADDED,))


def unchunked(values):
    lead = values.shape[:-1]
    values = values.reshape(lead + (SHARDS, CHUNK_PAD))[..., :CHUNK]
    return values.reshape(lead + (CHANNELS,))


def local(
    block_in,
    out_cotangent,
    pair_target,
    entry_weight,
    entry_gain,
    entry_shift,
    group_weight,
    group_gain,
    group_shift,
    squeeze_weight,
    squeeze_bias,
    excite_weight,
    excite_bias,
    exit_weight,
    exit_gain,
    exit_shift,
):
    size = lax.axis_size("img")
    stream = lax.axis_index("stream")
    on_global = stream == 0
    positions = jnp.arange(ROWS, dtype=jnp.int32)
    image_of = positions // IMAGE_ROWS
    within = positions % IMAGE_ROWS
    live = within < jnp.where(on_global, IMAGE_ROWS, SMALL_ROWS)
    area = jnp.where(on_global, GLOBAL_SIDE**2, SMALL_SIDE**2)
    crop_of = within // area
    crop_ids = jnp.arange(CROPS, dtype=jnp.int32)
    per_image = jnp.where(on_global, GLOBAL_CROPS, SMALL_CROPS)
    pool_full = live[None] & ((image_of * per_image + crop_of)[None] == crop_ids[:, None])
    pool = pool_full.astype(bf16)
    target_rows = jnp.zeros((ROWS,), jnp.int32)
    for slot in range(SMALL_CROPS):
        target_rows = jnp.where(
            crop_of == slot, jnp.repeat(pair_target[:, slot], IMAGE_ROWS), target_rows
        )
    pair_of = image_of * GLOBAL_CROPS + jnp.where(on_global, crop_of, target_rows)
    pair = (live[None] & (pair_of[None] == crop_ids[:, None])).astype(bf16)
    live_lanes = jnp.broadcast_to(live[:, None], (ROWS, 128)).astype(bf16)
    edges = edge_masks()

    pad_out = ((0, 0), (0, PADDED - CHANNELS))
    x = jnp.pad(jnp.where(live[:, None], block_in[0], 0), pad_out)
    cot = jnp.pad(jnp.where(live[:, None], out_cotangent[0], 0), pad_out)

    if size == SHARDS:
        entry_piece = wide_lanes(entry_weight.reshape(CHUNK, CHANNELS)).reshape(-1)
        entry_mat = gather(entry_piece, WIDE, size)
    else:
        entry_mat = wide_lanes(gather(entry_weight, CHANNELS, size)[:, :CHANNELS])
    lines = group_weight.shape[0] // GROUP_WIDTH if size == SHARDS else 0
    if lines:
        lines_pad = -(-lines // 16) * 16
        piece = group_weight.reshape(lines, GROUP_WIDTH)
        piece = jnp.pad(piece, ((0, lines_pad - lines), (0, 128 - GROUP_WIDTH)))
        conv = lax.all_gather(piece, "img", axis=0, tiled=False)[:, :lines, :GROUP_WIDTH]
    else:
        conv = lax.all_gather(group_weight, "img", axis=0, tiled=True)
    conv = conv.reshape(9, CHANNELS, GROUP_WIDTH)
    squeeze_mat = gather(squeeze_weight, SQUEEZE, size)[:, :SQUEEZE]
    excite_mat = gather(excite_weight, SQUEEZE, size)[:, :SQUEEZE]
    exit_mat = gather(exit_weight, CHANNELS, size)

    def rows_of(*vectors):
        kept = [wide_lanes(vector).reshape(BLOCKS, 2, 128) for vector in vectors]
        return jnp.concatenate(kept, axis=1)

    params = rows_of(entry_gain, entry_shift, group_gain, group_shift)
    exit_params = [
        jnp.pad(vector, (0, PADDED - CHANNELS)).reshape(OUT_BLOCKS, 2, 128)
        for vector in (exit_gain, exit_shift)
    ]
    exit_params = jnp.concatenate(exit_params * 2, axis=1)

    fold = np.zeros((LANES, GROUP_WIDTH), np.float32)
    fold[np.arange(BLOCK), np.arange(BLOCK) % GROUP_WIDTH] = 1
    fold = jnp.asarray(fold, bf16)
    x_chunked, x_turned = run_prepare(x)
    act, turned, group, mixed, pooled, moment = run_entry(
        size, x_chunked, entry_mat, conv, params, pool, edges, fold.T
    )

    def small_dot(a, b, dims=((1,), (0,))):
        return lax.dot_general(
            a, b.astype(f32), (dims, ((), ())), precision=lax.Precision.HIGHEST
        )

    quarters = CHANNELS // SQUEEZE
    quarter = jnp.eye(quarters, dtype=f32)

    def to_rows(values):
        spread_out = values[None, :, :, None] * quarter[:, None, None, :]
        return chunked(spread_out.reshape(quarters * CROPS, CHANNELS))

    def to_quarters(values):
        return values.reshape(CROPS, quarters, SQUEEZE).transpose(1, 0, 2).reshape(-1, SQUEEZE)

    pooled = chunked(narrow_lanes(pooled) / area.astype(f32))
    squeeze_in = small_dot(pooled, squeeze_mat) + squeeze_bias
    squeezed = jax.nn.silu(squeeze_in)
    squeezed_rows = to_rows(squeezed)
    excite_in = small_dot(squeezed_rows, excite_mat).reshape(quarters, CROPS, SQUEEZE)
    excite_in = excite_in.transpose(1, 0, 2).reshape(CROPS, CHANNELS)
    gate = jax.nn.sigmoid(excite_in + excite_bias)
    spread = jnp.concatenate([pool.T, pool.T], axis=1)
    gate_terms = split(wide_lanes(gate))
    scaled, scaled_turned = run_scale(mixed, gate_terms, spread)

    block_out, exit_delta, residual, exit_grad, exit_total = run_exit(
        size, scaled, scaled_turned, exit_mat, x, cot, exit_params, pair, pair.T, live_lanes
    )
    exit_shard = scatter(exit_grad, CHANNELS, size)
    scaled_grad, gate_grad = run_gate(exit_delta, exit_mat, mixed, pool)

    used = crop_ids < IMAGE_DEV * per_image
    gate_grad = jnp.where(used[:, None], narrow_lanes(gate_grad), 0.0)
    excite_delta = gate_grad * gate * (1.0 - gate)
    excite_quarters = to_quarters(excite_delta)
    back_rows = unchunked(small_dot(excite_quarters, excite_mat, ((1,), (1,))))
    back_rows = back_rows.reshape(quarters, CROPS, SQUEEZE, quarters)
    squeeze_delta = jnp.sum(back_rows * quarter[:, None, None, :], axis=(0, 3))
    squeeze_delta = squeeze_delta * silu_slope(squeeze_in)
    pooled_grad = unchunked(small_dot(squeeze_delta, squeeze_mat, ((1,), (1,))))
    pooled_grad = pooled_grad / area.astype(f32)
    beside = ((0, 0), (0, 512 - SQUEEZE))
    excite_grad = small_dot(squeezed_rows, jnp.pad(excite_quarters, beside), ((0,), (0,)))
    squeeze_grad = small_dot(pooled, jnp.pad(squeeze_delta, beside), ((0,), (0,)))
    excite_shard = scatter(excite_grad.astype(bf16), SQUEEZE, size)
    squeeze_shard = scatter(squeeze_grad.astype(bf16), SQUEEZE, size)
    gates = jnp.stack([gate_terms, split(wide_lanes(pooled_grad))])
    entry_delta, entry_grad, conv_grad, totals = run_back(
        size, scaled_grad, group, gates, spread, act, turned, conv, x_turned, params,
        moment, edges, fold,
    )
    input_grad = unchunked(dot(entry_delta, entry_mat, ((1,), (1,))))
    input_grad = input_grad + residual[:, :CHANNELS].astype(f32)
    input_grad = jnp.where(live[:, None], input_grad, 0.0).astype(bf16)

    if size == SHARDS:
        part = lax.psum_scatter(entry_grad, "img", scatter_dimension=0, tiled=True)
        part = swap_sum(part)
        entry_shard = narrow_lanes(part[:CHUNK]).reshape(-1)
    else:
        entry_shard = scatter(narrow_lanes(entry_grad), CHANNELS, size)
    if lines:
        conv_grad = conv_grad.reshape(SHARDS, lines, GROUP_WIDTH)
        conv_grad = jnp.pad(
            conv_grad, ((0, 0), (0, lines_pad - lines), (0, 128 - GROUP_WIDTH))
        ).reshape(-1, 128)
        conv_part = lax.psum_scatter(conv_grad, "img", scatter_dimension=0, tiled=True)
        conv_shard = swap_sum(conv_part)[:lines, :GROUP_WIDTH].reshape(-1)
    else:
        conv_part = lax.psum_scatter(
            conv_grad.reshape(-1), "img", scatter_dimension=0, tiled=True
        )
        conv_shard = swap_sum(conv_part)
    shards = (entry_shard, conv_shard, squeeze_shard, excite_shard, exit_shard)

    def folded(kept):
        kept = kept.reshape(-1, MICRO_BATCHES, 2, LANES).sum(axis=1)
        return kept[:, 1].reshape(-1), kept[:, 0].reshape(-1)

    group_gain_grad, group_shift_grad = [narrow_lanes(v) for v in folded(totals[:, 0])]
    entry_gain_grad, entry_shift_grad = [narrow_lanes(v) for v in folded(totals[:, 1])]
    exit_gain_grad, exit_shift_grad = [v[:CHANNELS] for v in folded(exit_total[:, 1])]
    bias_sums = lax.psum(
        (jnp.sum(squeeze_delta, axis=0), jnp.sum(excite_delta, axis=0)), ("stream", "img")
    )
    smalls = lax.psum(
        (
            entry_gain_grad,
            entry_shift_grad,
            group_gain_grad,
            group_shift_grad,
            exit_gain_grad,
            exit_shift_grad,
        ),
        "stream",
    )
    return (
        block_out[None],
        input_grad[None],
        shards[0],
        smalls[0],
        smalls[1],
        shards[1],
        smalls[2],
        smalls[3],
        shards[2],
        bias_sums[0],
        shards[3],
        bias_sums[1],
        shards[4],
        smalls[4],
        smalls[5],
    )


def solution(mesh):
    return jax.shard_map(
        local,
        mesh=mesh,
        in_specs=(
            P("stream", "img", None),
            P("stream", "img", None),
            P("img", None),
            P("img"),
            P(),
            P(),
            P("img"),
            P(),
            P(),
            P("img"),
            P(),
            P("img"),
            P(),
            P("img"),
            P(),
            P(),
        ),
        out_specs=(
            P("stream", "img", None),
            P("stream", "img", None),
            P("img"),
            P(),
            P(),
            P("img"),
            P(),
            P(),
            P("img"),
            P(),
            P("img"),
            P(),
            P("img"),
            P(),
            P(),
        ),
        check_vma=False,
    )
```

time: 3430 us -> 954 us (0.28)
  blocking collectives: 1510 us -> 46.2 us
  local copies, waits for them, and re-layouts: 984 us -> 95.6 us
  Pallas kernels: 0 us -> 381 us
  matrix products: 412 us -> 41.5 us
  other arithmetic: 101 us -> 36.5 us
  waiting for transfers between devices: 372 us -> 322 us
    unnamed x1 -> x0, blocking collectives: 934 us -> none
    psum x10 -> x2, blocking collectives: 573 us -> 46.2 us  [the longest x1 38.2 us: local(): lax.psum((jnp.sum(squeeze_delta, axis=0), jnp.sum(excite_delta, axis=0)),...]
    reshape x46 -> x27, local copies, waits for them, and re-layouts: 461 us -> 37.9 us  [the longest x1 16.2 us: unchunked(): return values.reshape(lead + (CHANNELS,))]
    pallas_call x0 -> x6, Pallas kernels: none -> 381 us  [the longest x1 160 us: run_back(): pl.pallas_call(functools.partial(back_kernel, size), grid=(BLOCKS + 2,),...]
    dot_general x46 -> x6, matrix products: 412 us -> 39.2 us  [the longest x1 21.8 us: dot(): return lax.dot_general(a, b, (dims, ((), ())), preferred_element_type=f32)]
    unnamed x3 -> x10, waiting for transfers between devices: 372 us -> 1.33 us
    slice x7 -> x9, local copies, waits for them, and re-layouts: 185 us -> 2.36 us  [the longest x2 1.74 us: narrow_lanes(): values.reshape(lead + (BLOCKS, LANES))[..., :BLOCK]]
    reduce_scatter x0 -> x5, waiting for transfers between devices: none -> 178 us  [the longest x1 111 us: local(): part = lax.psum_scatter(entry_grad, 'img', scatter_dimension=0, tiled=True)]
  transfers between devices with their start and end apart: 4 -> 15, of which waited for: 1 -> 6; matrix products, arithmetic and copies ran while one was open for 8% -> 16% of each run, Pallas kernels for 0% -> 30%
where the time goes in v1:
time: 954 us; the launch traced here: 946 us
  Pallas kernels  381 us (40%)
  waiting for transfers between devices  322 us (34%)
  local copies, waits for them, and re-layouts  95.6 us (10%)
  blocking collectives  46.2 us (5%)
  matrix products  41.5 us (4%)
  other arithmetic  36.5 us (4%)
  between operations  15.3 us (2%)
    pallas_call x1, Pallas kernels, run_back(): pl.pallas_call(functools.partial(back_kernel, size), grid=(BLOCKS + 2,),...  160 us
    all_gather x4, waiting for transfers between devices, gather(): return lax.all_gather(piece, 'img', axis=0, tiled=True)  118 us
    reduce_scatter x1, waiting for transfers between devices, local(): part = lax.psum_scatter(entry_grad, 'img', scatter_dimension=0, tiled=True)  111 us
    pallas_call x1, Pallas kernels, run_entry(): pl.pallas_call(functools.partial(entry_kernel, size), grid=(BLOCKS + 2,),...  94.3 us
    reduce_scatter x3, waiting for transfers between devices, scatter(): part = lax.psum_scatter(grads, 'img', scatter_dimension=0, tiled=True)  66.7 us
    pallas_call x1, Pallas kernels, run_exit(): pl.pallas_call(functools.partial(exit_kernel, size), grid=(blocks + 3,),...  65.3 us
    psum x1, blocking collectives, local(): lax.psum((jnp.sum(squeeze_delta, axis=0), jnp.sum(excite_delta, axis=0)),...  38.2 us
    pallas_call x1, Pallas kernels, run_gate(): pl.pallas_call(gate_kernel, grid=(BLOCKS,), out_shape=(jax.ShapeDtypeStru...  30.2 us
  transfers between devices with their start and end apart: 15, of which 6 were waited for; matrix products, arithmetic and copies ran while one was open for 16% of the time, Pallas kernels for 30%

profile of v1, /device:TPU:0, one launch (start us, length us, event | category | flops | bytes accessed | tf_op | source)
XLA Modules:
  0.0 946.1 jit_solution(5278005738991809059)
XLA Ops:
  18.9 5.9 bitcast_select_fusion
  37.3 12.7 %prepare.1 = (bf16[1568,2048]{1,0:T(8,128)(2,1)}, bf16[2048,1568]{1,0:T(8,128)(2,1)}) custom-call(bf16[1568,2048]{1,0:T(8,128)(2,1)} %pad.77.x_ref), custom_call_target="tpu_custom_call" | custom-call | flops 4932501504 | bytes 20971520 | tf_op jit(solution)/shard_map/prepare/pallas_call | solution.py:662
  50.0 16.0 %all-gather.15.cloned.1.call-done = bf16[18176,128]{1,0:T(8,128)(2,1)} async-done(((bf16[1136,128]{1,0:T(8,128)(2,1)}), bf16[18176,128]{1,0:T(8,128)(2,1)}) %all-gather.15.cloned.1.call-update) | async-done | bytes 4653072 | tf_op jit(solution)/shard_map/all_gather | solution.py:1071
  66.0 5.7 reshape.309.conv_ref
  71.6 77.2 %all-gather.7.cloned.1.call-done.weight_ref = bf16[2048,2304]{1,0:T(8,128)(2,1)} async-done(((bf16[128,2304]{1,0:T(8,128)(2,1)}), bf16[2048,2304]{1,0:T(8,128)(2,1)}) %all-gather.7.cloned.1.call-update) | async-done | bytes 9437200 | tf_op jit(solution)/shard_map/all_gather | solution.py:984
  150.3 94.3 %entry.1 = (f32[1568,2304]{1,0:T(8,128)}, bf16[9,256,1792]{2,1,0:T(8,128)(2,1)}, f32[1568,2304]{1,0:T(8,128)}, bf16[1568,2304]{1,0:T(8,128)(2,1)}, f32[16,2304]{1,0:T(8,128)}, /*index=5*/f32[9,2,8,128]{3,2,1,0:T(8,128)}) custom-call(bf16[1568,2048]{1,0:T(8,128)(2,1)} %get-tuple-element.36.x_ref, bf16[2048,2304]{1,0:T(8,128)(2,1)} %all-gather.7.cloned.1.call-done.weight_ref, ...), custom_call_target="tpu_custom_call" | custom-call | flops 31444697088 | bytes 73400320 | tf_op jit(solution)/shard_map/entry/pallas_call | solution.py:336
  260.6 18.3 %scale.1 = (bf16[1568,2048]{1,0:T(8,128)(2,1)}, bf16[2048,1568]{1,0:T(8,128)(2,1)}) custom-call(bf16[1568,2304]{1,0:T(8,128)(2,1)} %get-tuple-element.37.mixed_ref, bf16[32,2304]{1,0:T(8,128)(2,1)} %get-tuple-element.75.gates_ref, bf16[1568,32]{1,0:T(8,128)(2,1)} %add_convert_fusion.spread_ref), custom_call_target="tpu_custom_call" | custom-call | flops 6576668672 | bytes 31457280 | tf_op jit(solution)/shard_map/scale/pallas_call | solution.py:713
  278.9 40.8 %all-gather.13.cloned.1.call-done.weight_ref = bf16[2048,2048]{1,0:T(8,128)(2,1)} async-done(((bf16[128,2048]{1,0:T(8,128)(2,1)}), bf16[2048,2048]{1,0:T(8,128)(2,1)}) %all-gather.13.cloned.1.call-update) | async-done | bytes 8388624 | tf_op jit(solution)/shard_map/all_gather | solution.py:984
  320.7 65.3 %exit.1 = (bf16[1568,2016]{1,0:T(8,128)(2,1)}, bf16[1568,2048]{1,0:T(8,128)(2,1)}, bf16[1568,2048]{1,0:T(8,128)(2,1)}, bf16[2048,2048]{1,0:T(8,128)(2,1)}, f32[8,2,8,128]{3,2,1,0:T(8,128)}) custom-call(bf16[1568,2048]{1,0:T(8,128)(2,1)} %get-tuple-element.39.scaled_ref, bf16[2048,1568]{1,0:T(8,128)(2,1)} %get-tuple-element.40.turned_ref, ...), custom_call_target="tpu_custom_call" | custom-call | flops 26306674688 | bytes 73400320 | tf_op jit(solution)/shard_map/exit/pallas_call | solution.py:548
  386.0 30.2 %gate.1 = (f32[1568,2304]{1,0:T(8,128)}, f32[16,2304]{1,0:T(8,128)}) custom-call(bf16[1568,2048]{1,0:T(8,128)(2,1)} %get-tuple-element.42.delta_ref, bf16[2048,2048]{1,0:T(8,128)(2,1)} %all-gather.13.cloned.1.call-done.weight_ref, bf16[1568,2304]{1,0:T(8,128)(2,1)} %get-tuple-element.37.mixed_ref, bf16[16,1568]{1,0:T(8,128)(2,1)} %get-tuple-element.87.pool_ref), custom_call_target="tpu_custom_call" | custom-call | flops 14797504512 | bytes 41943040 | tf_op jit(solution)/shard_map/gate/pallas_call | solution.py:615
  417.7 5.0 convolution_convert_fusion
  442.4 160.4 %back.1 = (bf16[1568,2304]{1,0:T(8,128)(2,1)}, bf16[2048,2304]{1,0:T(8,128)(2,1)}, bf16[9,2016,56]{2,1,0:T(8,128)(2,1)}, f32[9,2,8,128]{3,2,1,0:T(8,128)}) custom-call(f32[1568,2304]{1,0:T(8,128)} %get-tuple-element.43.grad_ref, f32[1568,2304]{1,0:T(8,128)} %get-tuple-element.44.group_ref, bf16[2,32,2304]{2,1,0:T(8,128)(2,1)} %pad_maximum_fusion.gates_ref, ...), custom_call_target="tpu_custom_call" | custom-call | flops 48091889664 | bytes 94371840 | tf_op jit(solution)/shard_map/back/pallas_call | solution.py:900
  602.8 5.4 reshape.313
  608.2 5.4 pad.95.clone
  615.4 21.8 %convolution_bitcast_fusion = f32[196,8,16,128]{3,1,2,0:T(8,128)} fusion(bf16[1568,2304]{1,0:T(8,128)(2,1)} %get-tuple-element.50, bf16[2048,2304]{1,0:T(8,128)(2,1)} %all-gather.7.cloned.1.call-done.weight_ref), kind=kOutput, calls=%fused_computation.1 | convolution fusion | flops 14797504512 | bytes 29507584 | tf_op jit(solution)/shard_map/dot_general | solution.py:55
  637.2 13.0 %copy.119 = f32[196,8,16,128]{3,2,1,0:T(8,128)} copy(f32[196,8,16,128]{3,1,2,0:T(8,128)} %convolution_bitcast_fusion) | data formatting | bytes 25690112
  650.2 16.2 %reshape.293 = f32[1568,2016]{1,0:T(8,128)} reshape(f32[1568,16,126]{2,1,0:T(8,128)} %bitcast.94) | data formatting | bytes 25288704 | tf_op jit(solution)/shard_map/reshape | solution.py:1013
  667.0 38.2 %all-reduce.21 = (f32[504]{0:T(512)}, f32[2016]{0:T(1024)}) all-reduce(f32[504]{0:T(512)S(1)} %get-tuple-element.68, f32[2016]{0:T(1024)S(1)} %reduce_sum.61), channel_id=1, replica_groups=mesh['stream'=2,'img'=16] {'stream','img'}, use_global_device_ids=true, to_apply=%region_11.12 | all-reduce | flops 2520 | bytes 20160 | tf_op jit(solution)/shard_map/psum | solution.py:1181
  705.2 12.2 %fusion = bf16[1,1568,2016]{2,1,0:T(8,128)(2,1)} fusion(f32[1568,2016]{1,0:T(8,128)} %reshape.293, bf16[1568,2048]{1,0:T(8,128)(2,1)} %get-tuple-element.51, pred[1568]{0:T(1024)(128)(4,1)S(1)} %copy-done.7), kind=kLoop, calls=%fused_computation.2 | loop fusion | flops 12644352 | bytes 25290272 | tf_op jit(solution)/shard_map/broadcast_in_dim | solution.py:1197
  720.0 8.0 all-reduce.22
  731.0 66.7 %reduce-scatter.14.cloned.1.call-done = bf16[128,2048]{1,0:T(8,128)(2,1)} async-done(((bf16[2048,2048]{1,0:T(8,128)(2,1)}), bf16[128,2048]{1,0:T(8,128)(2,1)}) %reduce-scatter.14.cloned.1.call-update) | async-done | bytes 524304 | tf_op jit(solution)/shard_map/reduce_scatter | solution.py:991
  801.8 110.9 %reduce-scatter.6.cloned.1.call-done = bf16[128,2304]{1,0:T(8,128)(2,1)} async-done(((bf16[2048,2304]{1,0:T(8,128)(2,1)}), bf16[128,2304]{1,0:T(8,128)(2,1)}) %reduce-scatter.6.cloned.1.call-update) | async-done | bytes 589840 | tf_op jit(solution)/shard_map/reduce_scatter | solution.py:1155
  919.1 8.8 collective-permute-done
  932.1 6.7 copy.146
  (196 shorter events, 85.6 us)
Async XLA Ops:
  7.2 7.5 copy-start.4
  7.2 58.8 %all-gather.15.cloned.1.call-start = ((), (), s32[]{:S(2)}) async-start(), calls=%async_computation.14 | async-start | bytes 4943872 | tf_op jit(solution)/shard_map/all_gather | solution.py:1071
  9.5 139.4 %all-gather.7.cloned.1.call-start = ((), (), s32[]{:S(2)}) async-start(), calls=%async_computation.5 | async-start | bytes 10027008 | tf_op jit(solution)/shard_map/all_gather | solution.py:984
  11.6 7.0 copy-start.12
  13.7 232.2 %all-gather.9.cloned.1.call-start = ((), (), s32[]{:S(2)}) async-start(), calls=%async_computation.6 | async-start | bytes 2228224 | tf_op jit(solution)/shard_map/all_gather | solution.py:984
  14.7 241.2 %all-gather.11.cloned.1.call-start = ((), (), s32[]{:S(2)}) async-start(), calls=%async_computation.7 | async-start | bytes 2228224 | tf_op jit(solution)/shard_map/all_gather | solution.py:984
  15.9 303.8 %all-gather.13.cloned.1.call-start = ((), (), s32[]{:S(2)}) async-start(), calls=%async_computation.8 | async-start | bytes 8912896 | tf_op jit(solution)/shard_map/all_gather | solution.py:984
  17.5 699.9 %reduce-scatter.12.cloned.1.call-start = ((), (), s32[]{:S(2)}) async-start(), calls=%async_computation.12 | async-start | bytes 2228224 | tf_op jit(solution)/shard_map/reduce_scatter | solution.py:991
  18.9 17.7 %copy-start.6 = (pred[1568]{0:T(1024)(128)(4,1)}, pred[1568]{0:T(1024)(128)(4,1)S(1)}, u32[]{:S(2)}) copy-start(pred[1568]{0:T(1024)(128)(4,1)S(1)} %get-tuple-element.92) | copy-start | bytes 4708
  50.0 98.9 %copy-start.17 = (bf16[2,1824]{1,0:T(2,128)(2,1)S(1)}, bf16[2,1824]{1,0:T(2,128)(2,1)}, u32[]{:S(2)}) copy-start(bf16[2,1824]{1,0:T(2,128)(2,1)} %constant.108) | copy-start | bytes 21892
  150.3 95.5 %copy-start.18 = (f32[504]{0:T(512)S(1)}, f32[504]{0:T(512)}, u32[]{:S(2)}) copy-start(f32[504]{0:T(512)} %param.28) | copy-start | bytes 6052
  422.7 305.3 %reduce-scatter.10.cloned.1.call-start = ((), (), s32[]{:S(2)}) async-start(), calls=%async_computation.11 | async-start | bytes 2228224 | tf_op jit(solution)/shard_map/reduce_scatter | solution.py:991
  427.4 7.3 copy-start
  442.4 287.6 %reduce-scatter.8.cloned.1.call-start = ((), (), s32[]{:S(2)}) async-start(), calls=%async_computation.10 | async-start | bytes 4943872 | tf_op jit(solution)/shard_map/reduce_scatter | solution.py:1165
  613.6 184.0 %reduce-scatter.14.cloned.1.call-start = ((), (), s32[]{:S(2)}) async-start(), calls=%async_computation.13 | async-start | bytes 8912896 | tf_op jit(solution)/shard_map/reduce_scatter | solution.py:991
  614.4 298.3 %reduce-scatter.6.cloned.1.call-start = ((), (), s32[]{:S(2)}) async-start(), calls=%async_computation.9 | async-start | bytes 10027008 | tf_op jit(solution)/shard_map/reduce_scatter | solution.py:1155
  650.2 16.2 %copy-start.5 = (f32[9,2,8,128]{3,2,1,0:T(8,128)S(1)}, f32[9,2,8,128]{3,2,1,0:T(8,128)}, u32[]{:S(2)}) copy-start(f32[9,2,8,128]{3,2,1,0:T(8,128)} %get-tuple-element.53) | copy-start | bytes 221188
  650.2 55.0 %copy-start.7 = (pred[1568]{0:T(1024)(128)(4,1)S(1)}, pred[1568]{0:T(1024)(128)(4,1)}, u32[]{:S(2)}) copy-start(pred[1568]{0:T(1024)(128)(4,1)} %copy-done.6) | copy-start | bytes 4708
  717.4 12.6 %collective-permute-start.3 = (bf16[128,512]{1,0:T(8,128)(2,1)}, bf16[128,512]{1,0:T(8,128)(2,1)S(1)}, u32[]{:S(2)}, u32[]{:S(2)}) collective-permute-start(bf16[128,512]{1,0:T(8,128)(2,1)} %reduce-scatter.12.cloned.1.call-done), channel_id=1, source_target_pairs={{0,16},{16,0},{1,17},{17,1},{2,18},{18,2},{3,19},{19,3},{4,20},{20... | collective-permute-start | bytes 393224 | tf_op jit(solution)/shard_map/ppermute | solution.py:999
  728.0 71.1 %collective-permute-start.2 = (bf16[128,512]{1,0:T(8,128)(2,1)}, bf16[128,512]{1,0:T(8,128)(2,1)S(1)}, u32[]{:S(2)}, u32[]{:S(2)}) collective-permute-start(bf16[128,512]{1,0:T(8,128)(2,1)} %reduce-scatter.10.cloned.1.call-done), channel_id=1, source_target_pairs={{0,16},{16,0},{1,17},{17,1},{2,18},{18,2},{3,19},{19,3},{4,20},{20... | collective-permute-start | bytes 393224 | tf_op jit(solution)/shard_map/ppermute | solution.py:999
  730.0 184.2 %collective-permute-start.1 = (bf16[1136,128]{1,0:T(8,128)(2,1)}, bf16[1136,128]{1,0:T(8,128)(2,1)S(1)}, u32[]{:S(2)}, u32[]{:S(2)}) collective-permute-start(bf16[1136,128]{1,0:T(8,128)(2,1)} %reduce-scatter.8.cloned.1.call-done), channel_id=1, source_target_pairs={{0,16},{16,0},{1,17},{17,1},{2,18},{18,2},{3,19},{19,3},{4,20},{20... | collective-permute-start | bytes 872456 | tf_op jit(solution)/shard_map/ppermute | solution.py:999
  797.6 118.7 %collective-permute-start.4 = (bf16[128,2048]{1,0:T(8,128)(2,1)}, bf16[128,2048]{1,0:T(8,128)(2,1)S(1)}, u32[]{:S(2)}, u32[]{:S(2)}) collective-permute-start(bf16[128,2048]{1,0:T(8,128)(2,1)} %reduce-scatter.14.cloned.1.call-done), channel_id=1, source_target_pairs={{0,16},{16,0},{1,17},{17,1},{2,18},{18,2},{3,19},{19,3},{4,20},{20... | collective-permute-start | bytes 1572872 | tf_op jit(solution)/shard_map/ppermute | solution.py:999
  912.7 15.2 %copy-start.1 = (bf16[128,2304]{1,0:T(8,128)(2,1)S(1)}, bf16[128,2304]{1,0:T(8,128)(2,1)}, u32[]{:S(2)}) copy-start(bf16[128,2304]{1,0:T(8,128)(2,1)} %reduce-scatter.6.cloned.1.call-done) | copy-start | bytes 1769476
  912.7 15.2 %collective-permute-start = (bf16[128,2304]{1,0:T(8,128)(2,1)}, bf16[128,2304]{1,0:T(8,128)(2,1)S(1)}, u32[]{:S(2)}, u32[]{:S(2)}) collective-permute-start(bf16[128,2304]{1,0:T(8,128)(2,1)} %reduce-scatter.6.cloned.1.call-done), channel_id=1, source_target_pairs={{0,16},{16,0},{1,17},{17,1},{2,18},{18,2},{3,19},{19,3},{4,20},{20... | collective-permute-start | bytes 1769480 | tf_op jit(solution)/shard_map/ppermute | solution.py:999
  (10 other events, 59.5 us)
Sparse Core Ops, SparseCore 0:
  10.2 55.7 all-gather.14
  68.8 79.9 all-gather.6
  151.6 43.9 all-gather.8
  198.1 43.6 all-gather.10
  244.4 75.2 all-gather.12
  422.8 62.4 reduce-scatter.11
  489.5 63.0 reduce-scatter.9
  613.8 76.2 reduce-scatter.7
  694.1 103.4 reduce-scatter.13
  801.6 111.0 reduce-scatter.5

commit v2 on v1

--- a/solution.py
+++ b/solution.py
@@ -36,6 +36,9 @@
 DEEP_ROWS = 1792
 PAD_ROWS = TOP + DEEP_ROWS + 16
 CROPS = 16
+STEP = 112
+STEPS = ROWS // STEP
+HALF_STEPS = HALF // STEP
 CHUNK = 126
 CHUNK_PAD = 128
 SHARDS = CHANNELS // CHUNK
@@ -116,80 +119,109 @@
 
 
 def edge_masks():
-    place = np.arange(PAD_ROWS) - TOP
-    column = (place % 212) % 14
-    left = (column != 13).astype(np.float32)
-    right = (column != 0).astype(np.float32)
-    both = np.stack([left, right])
-    return jnp.broadcast_to(jnp.asarray(both)[:, :, None], (2, PAD_ROWS, 128)).astype(bf16)
-
-
-def scatter_rows(rows_ref, pads, edges):
-    on_global = lax.axis_index("stream") == 0
-    inside = lax.broadcasted_iota(jnp.int32, (200, 128), 0)
-
-    @pl.when(on_global)
-    def _():
-        for image in range(IMAGE_DEV):
-            for tile in range(2):
-                start = IMAGE_ROWS * image
-                base = TOP + IMAGE_PAD * image
-                first = jnp.where(inside < 196, rows_ref[tile, start : start + 200], 0.0)
-                second = jnp.where(
-                    inside >= 4, rows_ref[tile, start + 192 : start + 392], 0.0
+    column = np.arange(IMAGE_PAD) % 212 % 14
+    both = np.stack([column != 13, column != 0]).astype(np.float32)
+    return jnp.broadcast_to(jnp.asarray(both)[:, :, None], (2, IMAGE_PAD, 128))
+
+
+def chunk_rows(chunk):
+    return slice(STEP * chunk, STEP * (chunk + 1))
+
+
+def add_up(pieces):
+    pieces = list(pieces)
+    while len(pieces) > 1:
+        odd = [pieces.pop()] if len(pieces) % 2 else []
+        pieces = [pieces[i] + pieces[i + 1] for i in range(0, len(pieces), 2)] + odd
+    return pieces[0]
+
+
+def fold_rows(values):
+    return add_up(values[8 * i : 8 * i + 8] for i in range(values.shape[0] // 8))
+
+
+class Sums:
+    def __init__(self):
+        self.parts = {}
+
+    def add(self, micro, tile, plain, product):
+        for kind, values in ((0, plain), (1, product)):
+            key = (micro, kind, tile)
+            self.parts.setdefault(key, []).append(fold_rows(values))
+
+    def packed(self):
+        return jnp.concatenate([column_sum(add_up(self.parts[key])) for key in sorted(self.parts)])
+
+
+def put_pads(piece, place, tile, pads, edges):
+    here = slice(place, place + piece.shape[0])
+    inner = (place - TOP) % IMAGE_PAD
+    inner = slice(inner, inner + piece.shape[0])
+    pads[0, tile, here] = piece
+    pads[1, tile, here] = piece * edges[0, inner]
+    pads[2, tile, here] = piece * edges[1, inner]
+
+
+def pad_global(load, pads, edges):
+    inside = lax.broadcasted_iota(jnp.int32, (8, 128), 0)
+    for image in range(IMAGE_DEV):
+        base = TOP + IMAGE_PAD * image
+        start = IMAGE_ROWS * image
+        for tile in range(2):
+            middle = load(tile, start + 192, 8)
+            first = load(tile, start, 192)
+            put_pads(first, base, tile, pads, edges)
+            put_pads(jnp.where(inside < 4, middle, 0.0), base + 192, tile, pads, edges)
+            put_pads(jnp.where(inside >= 4, middle, 0.0), base + 208, tile, pads, edges)
+            second = load(tile, start + 200, 192)
+            put_pads(second, base + 216, tile, pads, edges)
+
+
+def small_strips():
+    for image in range(IMAGE_DEV):
+        for crop in range(SMALL_CROPS):
+            for line in range(SMALL_SIDE):
+                start = IMAGE_ROWS * image + 49 * crop + 7 * line
+                yield start, IMAGE_PAD * image + 114 * crop + 14 * line
+
+
+def pad_small(rows_ref, pads):
+    for start, base in small_strips():
+        for tile in range(2):
+            piece = rows_ref[tile, start : start + 7]
+            for kind in range(3):
+                pads[kind, tile, TOP + base : TOP + base + 7] = piece
+
+
+def unpad_small(wide_ref, rows_ref):
+    for start, base in small_strips():
+        for tile in range(2):
+            rows_ref[tile, start : start + 7] = wide_ref[tile, base : base + 7]
+
+
+def unpadded(wide_ref, tile, first, count):
+    pieces = []
+    at = first
+    while at < first + count:
+        image, inner = divmod(at, 49)
+        base = IMAGE_PAD * image
+        stop = 49 * image + (24 if inner < 24 else 25 if inner == 24 else 49)
+        stop = min(stop, first + count)
+        length = 8 * (stop - at)
+        if inner == 24:
+            inside = lax.broadcasted_iota(jnp.int32, (8, 128), 0)
+            pieces.append(
+                jnp.where(
+                    inside < 4,
+                    wide_ref[tile, base + 192 : base + 200],
+                    wide_ref[tile, base + 208 : base + 216],
                 )
-                for place, piece in ((base, first), (base + 208, second)):
-                    here = slice(place, place + 200)
-                    pads[0, tile, here] = piece
-                    pads[1, tile, here] = piece * edges[0, here].astype(f32)
-                    pads[2, tile, here] = piece * edges[1, here].astype(f32)
-
-    @pl.when(jnp.logical_not(on_global))
-    def _():
-        for image in range(IMAGE_DEV):
-            for crop in range(SMALL_CROPS):
-                for line in range(SMALL_SIDE):
-                    start = IMAGE_ROWS * image + 49 * crop + 7 * line
-                    base = TOP + IMAGE_PAD * image + 114 * crop + 14 * line
-                    for tile in range(2):
-                        piece = rows_ref[tile, start : start + 7]
-                        for kind in range(3):
-                            pads[kind, tile, base : base + 7] = piece
-
-
-def compact_rows(wide, image, rows_ref, slot):
-    start = IMAGE_ROWS * image
-    inside = lax.broadcasted_iota(jnp.int32, (8, 128), 0)
-    for tile in range(2):
-        lanes = slice(128 * tile, 128 * tile + 128)
-        rows_ref[slot, tile, start : start + 192] = wide[0:192, lanes]
-        rows_ref[slot, tile, start + 192 : start + 200] = jnp.where(
-            inside < 4, wide[192:200, lanes], wide[208:216, lanes]
-        )
-        rows_ref[slot, tile, start + 200 : start + 392] = wide[216:408, lanes]
-
-
-def compact_small(wide_ref, image, rows_ref, slot):
-    for crop in range(SMALL_CROPS):
-        for line in range(SMALL_SIDE):
-            start = IMAGE_ROWS * image + 49 * crop + 7 * line
-            base = 114 * crop + 14 * line
-            for tile in range(2):
-                rows_ref[slot, tile, start : start + 7] = wide_ref[tile, base : base + 7]
-
-
-def take_result(wide, image, rows_ref, slot, wide_ref):
-    on_global = lax.axis_index("stream") == 0
-
-    @pl.when(on_global)
-    def _():
-        compact_rows(wide, image, rows_ref, slot)
-
-    @pl.when(jnp.logical_not(on_global))
-    def _():
-        wide_ref[0] = wide[:, 0:128]
-        wide_ref[1] = wide[:, 128:256]
-        compact_small(wide_ref, image, rows_ref, slot)
+            )
+        else:
+            start = base + 8 * inner + (0 if inner < 24 else 16)
+            pieces.append(wide_ref[tile, start : start + length])
+        at = stop
+    return pieces[0] if len(pieces) == 1 else jnp.concatenate(pieces)
 
 
 def stack_windows(pads, windows, image, sign):
@@ -240,6 +272,7 @@
 ):
     step = pl.program_id(0)
     count = row_count(size)
+    on_global = lax.axis_index("stream") == 0
 
     @pl.when(step == 0)
     def _():
@@ -252,17 +285,19 @@
     @pl.when(step < BLOCKS)
     def _():
         slot = lax.rem(step, 2)
-        parts = []
         for micro in range(MICRO_BATCHES):
             here = slice(HALF * micro, HALF * (micro + 1))
             act = dot(x_ref[here], weight_ref[...])
-            act_out[here] = act
+            first_rows[slot, 0, here] = act[:, :128]
+            first_rows[slot, 1, here] = act[:, 128:]
+        sums = Sums()
+        for chunk in range(STEPS):
+            here = chunk_rows(chunk)
             for tile in range(2):
-                first_rows[slot, tile, here] = act[:, 128 * tile : 128 * tile + 128]
-            plain = column_sum(act)
-            square = column_sum(act * act)
-            parts += [plain[:, :128], plain[:, 128:], square[:, :128], square[:, 128:]]
-        send_sums(size, step, jnp.concatenate(parts), sent, got, send_sem, recv_sem)
+                act = first_rows[slot, tile, here]
+                act_out[here, 128 * tile : 128 * tile + 128] = act
+                sums.add(chunk // HALF_STEPS, tile, act, act * act)
+        send_sums(size, step, sums.packed(), sent, got, send_sem, recv_sem)
 
     @pl.when((step >= 1) & (step < BLOCKS + 1))
     def _():
@@ -271,39 +306,72 @@
         total = take_sums(size, block, got, send_sem, recv_sem)
         total_out[block, 0] = total
         param = param_ref[block]
+        scales = {}
         for micro in range(MICRO_BATCHES):
-            here = slice(HALF * micro, HALF * (micro + 1))
             for tile in range(2):
                 mean, inverse = moments(total, micro, tile, count)
                 scale = 0.5 * inverse * param[tile : tile + 1]
-                shift = 0.5 * param[2 + tile : 3 + tile] - mean * scale
-                half = first_rows[slot, tile, here] * scale + shift
-                rows_ref[tile, here] = half + half * jnp.tanh(half)
-        scatter_rows(rows_ref, pads, edges)
-        for tile in range(2):
-            turned_out[0, 128 * tile : 128 * tile + 128] = pads[
-                0, tile, TOP : TOP + DEEP_ROWS
-            ].T.astype(bf16)
+                scales[micro, tile] = scale, 0.5 * param[2 + tile : 3 + tile] - mean * scale
+
+        def hidden(tile, start, length):
+            scale, shift = scales[start // HALF, tile]
+            half = first_rows[slot, tile, start : start + length] * scale + shift
+            return half + half * jnp.tanh(half)
+
         same = same_group(BLOCK, LANES)
         for offset in range(9):
             full = dot(conv_ref[offset], fold_ref[...])
             full_ref[LANES * offset : LANES * offset + BLOCK] = jnp.where(
                 same, full, 0.0
             ).astype(bf16)
-        for image in range(IMAGE_DEV):
+
+        def convolve(image, target):
             stack_windows(pads, windows, image, 1)
             here = slice(IMAGE_PAD * image, IMAGE_PAD * (image + 1))
             wide = dot(windows[here], full_ref[...])
-            take_result(wide, image, second_rows, slot, wide_ref)
-        parts = []
-        for micro in range(MICRO_BATCHES):
-            here = slice(HALF * micro, HALF * (micro + 1))
-            acts = [second_rows[slot, tile, here] for tile in range(2)]
-            parts += [column_sum(act) for act in acts]
-            parts += [column_sum(act * act) for act in acts]
-        send_sums(
-            size, BLOCKS + block, jnp.concatenate(parts), sent, got, send_sem, recv_sem
-        )
+            target[0, here] = wide[:, :128]
+            target[1, here] = wide[:, 128:]
+
+        def turn():
+            for tile in range(2):
+                turned_out[0, 128 * tile : 128 * tile + 128] = pads[
+                    0, tile, TOP : TOP + DEEP_ROWS
+                ].T.astype(bf16)
+
+        def send(sums):
+            send_sums(size, BLOCKS + block, sums.packed(), sent, got, send_sem, recv_sem)
+
+        @pl.when(on_global)
+        def _():
+            pad_global(hidden, pads, edges)
+            turn()
+            second = second_rows.at[slot]
+            for image in range(IMAGE_DEV):
+                convolve(image, second)
+            sums = Sums()
+            for chunk in range(STEPS):
+                for tile in range(2):
+                    act = unpadded(second, tile, STEP // 8 * chunk, STEP // 8)
+                    sums.add(chunk // HALF_STEPS, tile, act, act * act)
+            send(sums)
+
+        @pl.when(jnp.logical_not(on_global))
+        def _():
+            for chunk in range(STEPS):
+                for tile in range(2):
+                    rows_ref[tile, chunk_rows(chunk)] = hidden(tile, STEP * chunk, STEP)
+            pad_small(rows_ref, pads)
+            turn()
+            for image in range(IMAGE_DEV):
+                convolve(image, wide_ref)
+            second = second_rows.at[slot]
+            unpad_small(wide_ref, second)
+            sums = Sums()
+            for chunk in range(STEPS):
+                for tile in range(2):
+                    act = second[tile, chunk_rows(chunk)]
+                    sums.add(chunk // HALF_STEPS, tile, act, act * act)
+            send(sums)
 
     @pl.when(step >= 2)
     def _():
@@ -312,17 +380,30 @@
         total = take_sums(size, BLOCKS + block, got, send_sem, recv_sem)
         total_out[block, 1] = total
         param = param_ref[block]
-        for micro in range(MICRO_BATCHES):
-            here = slice(HALF * micro, HALF * (micro + 1))
-            for tile in range(2):
-                lanes = slice(128 * tile, 128 * tile + 128)
-                mean, inverse = moments(total, micro, tile, count)
-                scale = 0.5 * inverse * param[4 + tile : 5 + tile]
-                shift = 0.5 * param[6 + tile : 7 + tile] - mean * scale
-                act = second_rows[slot, tile, here]
-                group_out[here, lanes] = act
-                half = act * scale + shift
-                mixed_out[here, lanes] = (half + half * jnp.tanh(half)).astype(bf16)
+        second = second_rows.at[slot]
+
+        def finish(load):
+            for micro in range(MICRO_BATCHES):
+                for tile in range(2):
+                    lanes = slice(128 * tile, 128 * tile + 128)
+                    mean, inverse = moments(total, micro, tile, count)
+                    scale = 0.5 * inverse * param[4 + tile : 5 + tile]
+                    shift = 0.5 * param[6 + tile : 7 + tile] - mean * scale
+                    for chunk in range(HALF_STEPS * micro, HALF_STEPS * (micro + 1)):
+                        here = chunk_rows(chunk)
+                        act = load(tile, chunk)
+                        group_out[here, lanes] = act
+                        half = act * scale + shift
+                        mixed_out[here, lanes] = (half + half * jnp.tanh(half)).astype(bf16)
+
+        @pl.when(on_global)
+        def _():
+            finish(lambda tile, chunk: unpadded(second, tile, STEP // 8 * chunk, STEP // 8))
+
+        @pl.when(jnp.logical_not(on_global))
+        def _():
+            finish(lambda tile, chunk: second[tile, chunk_rows(chunk)])
+
         pooled_out[...] = dot(pool_ref[...], mixed_out[...])
 
 
@@ -350,7 +431,7 @@
             pl.BlockSpec((9, BLOCK, GROUP_WIDTH), lambda i: (0, at(1)(i), 0)),
             whole((BLOCKS, 8, 128)),
             whole((CROPS, ROWS)),
-            whole((2, PAD_ROWS, 128)),
+            whole((2, IMAGE_PAD, 128)),
             whole((GROUP_WIDTH, LANES)),
         ],
         out_specs=(
@@ -363,11 +444,11 @@
         ),
         scratch_shapes=[
             pltpu.VMEM((2, 2, ROWS, 128), f32),
-            pltpu.VMEM((2, 2, ROWS, 128), f32),
+            pltpu.VMEM((2, 2, CONV_ROWS, 128), f32),
             pltpu.VMEM((2, ROWS, 128), f32),
             pltpu.VMEM((3, 2, PAD_ROWS, 128), f32),
             pltpu.VMEM((CONV_ROWS, 9 * LANES), bf16),
-            pltpu.VMEM((2, IMAGE_PAD, 128), f32),
+            pltpu.VMEM((2, CONV_ROWS, 128), f32),
             pltpu.VMEM((9 * LANES, LANES), bf16),
             pltpu.VMEM((2 * BLOCKS, 8, 128), f32),
             pltpu.VMEM((2 * BLOCKS, size, 8, 128), f32),
@@ -384,6 +465,184 @@
             transcendentals=2 * ROWS * WIDE,
         ),
     )(x, weight, conv, params, pool, edges, fold)
+
+
+def place():
+    me = lax.axis_index("img")
+    return lax.axis_index("stream"), me // 4, lax.rem(me // 2, 2), lax.rem(me, 2)
+
+
+class Reducer:
+    def __init__(self, refs):
+        (
+            self.local,
+            self.core_got,
+            self.plane_got,
+            self.plane_sum,
+            self.z_got,
+            self.final,
+            self.final_got,
+            self.core_sem,
+            self.plane_sem,
+            self.z_sem,
+            self.y_sem,
+        ) = refs
+        self.stream, self.z, self.x, self.core = place()
+        self.mine = pl.ds(pl.multiple_of(64 * self.stream, 64), 64)
+        self.theirs = pl.ds(pl.multiple_of(64 * (1 - self.stream), 64), 64)
+
+    @staticmethod
+    def scratch():
+        return [
+            pltpu.VMEM((2, 2, 2, 4, 2, 128, 128), bf16),
+            pltpu.VMEM((3, 2, 4, 2, 128, 128), bf16),
+            pltpu.VMEM((2, 3, 4, 2, 64, 128), bf16),
+            pltpu.VMEM((2, 4, 2, 64, 128), bf16),
+            pltpu.VMEM((2, 3, 2, 64, 128), bf16),
+            pltpu.VMEM((2, 2, 64, 128), f32),
+            pltpu.VMEM((2, 2, 64, 128), f32),
+            pltpu.SemaphoreType.DMA((2, 2)),
+            pltpu.SemaphoreType.DMA((2, 2, 3)),
+            pltpu.SemaphoreType.DMA((2, 2, 3)),
+            pltpu.SemaphoreType.DMA((2, 2)),
+        ]
+
+    COUNT = 11
+
+    def index(self, k=0, across=0, beside=0):
+        return 4 * (self.z ^ k) + 2 * (self.x ^ across) + (self.core ^ beside)
+
+    def greet(self, barrier):
+        for across in (0, 1):
+            pl.semaphore_signal(
+                barrier,
+                inc=1,
+                device_id=(1 - self.stream, self.index(0, across)),
+                device_id_type=MESH,
+            )
+        return 2
+
+    def core_copy(self, block):
+        hold = lax.rem(block, 2)
+        return pltpu.make_async_remote_copy(
+            src_ref=self.local.at[hold, 1 - self.core],
+            dst_ref=self.core_got.at[lax.rem(block, 3)],
+            send_sem=self.core_sem.at[0, hold],
+            recv_sem=self.core_sem.at[1, hold],
+            device_id=(self.stream, self.index(0, 0, 1)),
+            device_id_type=MESH,
+        )
+
+    def plane_copy(self, block, peer):
+        hold = lax.rem(block, 2)
+        x = self.x if peer == 1 else 1 - self.x
+        rows = self.mine if peer == 0 else self.theirs
+        stream = self.stream if peer == 0 else 1 - self.stream
+        return pltpu.make_async_remote_copy(
+            src_ref=self.core_got.at[lax.rem(block, 3), x, :, :, rows],
+            dst_ref=self.plane_got.at[hold, peer],
+            send_sem=self.plane_sem.at[0, hold, peer],
+            recv_sem=self.plane_sem.at[1, hold, peer],
+            device_id=(stream, self.index(0, 0 if peer == 1 else 1)),
+            device_id_type=MESH,
+        )
+
+    def z_copy(self, block, k):
+        hold = lax.rem(block, 2)
+        return pltpu.make_async_remote_copy(
+            src_ref=self.plane_sum.at[hold, self.z ^ k],
+            dst_ref=self.z_got.at[hold, k - 1],
+            send_sem=self.z_sem.at[0, hold, k - 1],
+            recv_sem=self.z_sem.at[1, hold, k - 1],
+            device_id=(self.stream, self.index(k)),
+            device_id_type=MESH,
+        )
+
+    def y_copy(self, block):
+        hold = lax.rem(block, 2)
+        return pltpu.make_async_remote_copy(
+            src_ref=self.final.at[hold],
+            dst_ref=self.final_got.at[hold],
+            send_sem=self.y_sem.at[0, hold],
+            recv_sem=self.y_sem.at[1, hold],
+            device_id=(1 - self.stream, self.index()),
+            device_id_type=MESH,
+        )
+
+    def finish(self, block, put):
+        hold = lax.rem(block, 2)
+        self.y_copy(block).wait()
+        for tile in range(2):
+            put(tile, self.mine, self.final[hold, tile])
+            put(tile, self.theirs, self.final_got[hold, tile])
+
+    def after_z(self, block):
+        hold = lax.rem(block, 2)
+        for k in (1, 2, 3):
+            self.z_copy(block, k).wait()
+        for tile in range(2):
+            total = self.plane_sum[hold, self.z, tile].astype(f32)
+            for k in range(3):
+                total = total + self.z_got[hold, k, tile].astype(f32)
+            self.final[hold, tile] = total
+        self.y_copy(block).start()
+
+    def after_plane(self, block):
+        hold = lax.rem(block, 2)
+        ring = lax.rem(block, 3)
+        for peer in range(3):
+            self.plane_copy(block, peer).wait()
+        for z in range(4):
+            for tile in range(2):
+                total = self.core_got[ring, self.x, z, tile, self.mine].astype(f32)
+                for peer in range(3):
+                    total = total + self.plane_got[hold, peer, z, tile].astype(f32)
+                self.plane_sum[hold, z, tile] = total.astype(bf16)
+        for k in (1, 2, 3):
+            self.z_copy(block, k).start()
+
+    def after_core(self, block):
+        hold = lax.rem(block, 2)
+        ring = lax.rem(block, 3)
+        self.core_copy(block).wait()
+        for x in range(2):
+            for z in range(4):
+                for tile in range(2):
+                    total = self.core_got[ring, x, z, tile].astype(f32)
+                    total = total + self.local[hold, self.core, x, z, tile].astype(f32)
+                    self.core_got[ring, x, z, tile] = total.astype(bf16)
+        for peer in range(3):
+            self.plane_copy(block, peer).start()
+
+    def advance(self, newest, blocks, put):
+        def live(block):
+            return (block >= 0) & (block < blocks)
+
+        @pl.when(live(newest - 4))
+        def _():
+            self.finish(newest - 4, put)
+
+        @pl.when(live(newest - 3))
+        def _():
+            self.after_z(newest - 3)
+
+        @pl.when(live(newest - 2))
+        def _():
+            self.after_plane(newest - 2)
+
+        @pl.when(live(newest - 1))
+        def _():
+            self.after_core(newest - 1)
+
+    def begin(self, block, grad):
+        hold = lax.rem(block, 2)
+        for chunk in range(SHARDS):
+            z, x, core = chunk // 4, chunk // 2 % 2, chunk % 2
+            for tile in range(2):
+                self.local[hold, core, x, z, tile] = grad[
+                    128 * chunk : 128 * chunk + 128, 128 * tile : 128 * tile + 128
+                ].astype(bf16)
+        self.core_copy(block).start()
 
 
 def whole(shape):
@@ -414,7 +673,7 @@
     residual_out,
     weight_out,
     total_out,
-    normed_ref,
+    act_ref,
     slope_ref,
     pair_sent,
     pair_got,
@@ -424,6 +683,7 @@
     recv_sem,
     pair_send,
     pair_recv,
+    *reduce_refs,
 ):
     step = pl.program_id(0)
     count = row_count(size)
@@ -431,6 +691,7 @@
     me = lax.axis_index("img")
     area = jnp.where(stream == 0, GLOBAL_SIDE**2, SMALL_SIDE**2).astype(f32)
     blocks = OUT_BLOCKS
+    reducer = Reducer(reduce_refs) if reduce_refs else None
 
     def pair_copy(block):
         return pltpu.make_async_remote_copy(
@@ -448,18 +709,27 @@
         pl.semaphore_signal(
             barrier, inc=1, device_id=(1 - stream, me), device_id_type=MESH
         )
-        pl.semaphore_wait(barrier, size)
+        pl.semaphore_wait(barrier, size + (reducer.greet(barrier) if reducer else 0))
+
+    if reducer:
+
+        def put(tile, rows, values):
+            weight_out[rows, 128 * tile : 128 * tile + 128] = values
+
+        reducer.advance(step - 3, blocks, put)
 
     @pl.when(step < blocks)
     def _():
         slot = lax.rem(step, 4)
-        parts = []
         for micro in range(MICRO_BATCHES):
             here = slice(HALF * micro, HALF * (micro + 1))
-            act = dot(scaled_ref[here], weight_ref[...])
-            normed_ref[slot, here] = act
-            parts += lane_halves(column_sum(act)) + lane_halves(column_sum(act * act))
-        send_sums(size, step, jnp.concatenate(parts), sent, got, send_sem, recv_sem)
+            act_ref[slot, here] = dot(scaled_ref[here], weight_ref[...])
+        sums = Sums()
+        for chunk in range(STEPS):
+            for tile in range(2):
+                act = act_ref[slot, chunk_rows(chunk), 128 * tile : 128 * tile + 128]
+                sums.add(chunk // HALF_STEPS, tile, act, act * act)
+        send_sums(size, step, sums.packed(), sent, got, send_sem, recv_sem)
 
     @pl.when((step >= 1) & (step < blocks + 1))
     def _():
@@ -469,22 +739,22 @@
         total_out[block, 0] = total
         param = param_ref[block]
         for micro in range(MICRO_BATCHES):
-            here = slice(HALF * micro, HALF * (micro + 1))
             for tile in range(2):
                 lanes = slice(128 * tile, 128 * tile + 128)
                 mean, inverse = moments(total, micro, tile, count)
-                normed = normed_ref[slot, here, lanes] * inverse - mean * inverse
-                normed_ref[slot, here, lanes] = normed
-                gain = 0.5 * param[tile : tile + 1]
-                shift = 0.5 * param[2 + tile : 3 + tile]
-                half = 0.5 * x_ref[here, lanes].astype(f32) + (normed * gain + shift)
-                bent = jnp.tanh(half)
-                out_out[here, lanes] = (
-                    (half + half * bent) * live_ref[here].astype(f32)
-                ).astype(bf16)
-                slope_ref[lax.rem(block, 3), here, lanes] = (0.5 + 0.5 * bent) * (
-                    1.0 + half * (1.0 - bent)
-                )
+                scale = 0.5 * inverse * param[tile : tile + 1]
+                shift = 0.5 * param[2 + tile : 3 + tile] - mean * scale
+                for chunk in range(HALF_STEPS * micro, HALF_STEPS * (micro + 1)):
+                    here = chunk_rows(chunk)
+                    act = act_ref[slot, here, lanes]
+                    half = 0.5 * x_ref[here, lanes].astype(f32) + (act * scale + shift)
+                    bent = jnp.tanh(half)
+                    out_out[here, lanes] = (
+                        (half + half * bent) * live_ref[here].astype(f32)
+                    ).astype(bf16)
+                    slope_ref[lax.rem(block, 3), here, lanes] = (0.5 + 0.5 * bent) * (
+                        1.0 + half * (1.0 - bent)
+                    )
         embed = dot(pair_ref[...], out_out[...]) / area
         pair_sent[block] = embed[:8].astype(bf16).astype(f32)
         pair_copy(block).start()
@@ -493,66 +763,79 @@
     def _():
         block = step - 2
         slot = lax.rem(block, 4)
+        hold = lax.rem(block, 3)
+        moment = total_out[block, 0]
         pair_copy(block).wait()
         partner = pair_got[block]
         partner = jnp.concatenate([partner, jnp.zeros_like(partner)]).astype(bf16)
-        parts = []
-        for micro in range(MICRO_BATCHES):
-            here = slice(HALF * micro, HALF * (micro + 1))
+        means = {
+            (micro, tile): moments(moment, micro, tile, count)
+            for micro in range(MICRO_BATCHES)
+            for tile in range(2)
+        }
+        sums = Sums()
+        for chunk in range(STEPS):
+            here = chunk_rows(chunk)
             pull = dot(spread_ref[here], partner) * (PAIR_SCALE / area)
-            upstream = cot_ref[here].astype(f32) + pull
-            delta = upstream * slope_ref[lax.rem(block, 3), here]
-            slope_ref[lax.rem(block, 3), here] = delta
-            residual_out[here] = delta.astype(bf16)
-            parts += lane_halves(column_sum(delta))
-            parts += lane_halves(column_sum(delta * normed_ref[slot, here]))
-        send_sums(
-            size, blocks + block, jnp.concatenate(parts), sent, got, send_sem, recv_sem
-        )
-
-    @pl.when(step >= 3)
+            for tile in range(2):
+                lanes = slice(128 * tile, 128 * tile + 128)
+                mean, inverse = means[chunk // HALF_STEPS, tile]
+                upstream = cot_ref[here, lanes].astype(f32) + pull[:, lanes]
+                delta = upstream * slope_ref[hold, here, lanes]
+                slope_ref[hold, here, lanes] = delta
+                residual_out[here, lanes] = delta.astype(bf16)
+                normed = act_ref[slot, here, lanes] * inverse - mean * inverse
+                sums.add(chunk // HALF_STEPS, tile, delta, delta * normed)
+        send_sums(size, blocks + block, sums.packed(), sent, got, send_sem, recv_sem)
+
+    @pl.when((step >= 3) & (step < blocks + 3))
     def _():
         block = step - 3
         slot = lax.rem(block, 4)
+        hold = lax.rem(block, 3)
         moment = total_out[block, 0]
         total = take_sums(size, blocks + block, got, send_sem, recv_sem)
         total_out[block, 1] = total
         param = param_ref[block]
         for micro in range(MICRO_BATCHES):
-            here = slice(HALF * micro, HALF * (micro + 1))
             for tile in range(2):
                 lanes = slice(128 * tile, 128 * tile + 128)
-                delta_out[here, lanes] = norm_back(
-                    slope_ref[lax.rem(block, 3), here, lanes],
-                    normed_ref[slot, here, lanes],
-                    moment,
-                    total,
-                    micro,
-                    tile,
-                    param[tile : tile + 1],
-                    count,
-                ).astype(bf16)
-        weight_out[...] = dot(turned_ref[...], delta_out[...]).astype(bf16)
-
-
-def norm_back(upstream, normed, moment, total, micro, tile, gain, count):
-    _, inverse = moments(moment, micro, tile, count)
+                back = norm_back(moment, total, micro, tile, param[tile : tile + 1], count)
+                for chunk in range(HALF_STEPS * micro, HALF_STEPS * (micro + 1)):
+                    here = chunk_rows(chunk)
+                    delta_out[here, lanes] = back(
+                        slope_ref[hold, here, lanes], act_ref[slot, here, lanes]
+                    ).astype(bf16)
+        grad = dot(turned_ref[...], delta_out[...])
+        if reducer:
+            reducer.begin(block, grad)
+        else:
+            weight_out[...] = grad.astype(bf16)
+
+
+def norm_back(moment, total, micro, tile, gain, count):
+    mean, inverse = moments(moment, micro, tile, count)
     scale = gain * inverse
     plain = total[4 * micro + tile : 4 * micro + tile + 1] / count
-    along = total[4 * micro + 2 + tile : 4 * micro + 3 + tile] / count
-    return scale * upstream - (scale * plain + normed * (scale * along))
+    along = scale * (total[4 * micro + 2 + tile : 4 * micro + 3 + tile] / count)
+    slant = along * inverse
+    level = scale * plain
+    return lambda upstream, act: scale * upstream - (level + (act - mean) * slant)
 
 
 def run_exit(size, scaled, turned, weight, x, cot, params, pair, spread, live):
     blocks = OUT_BLOCKS
+    reduced = size == SHARDS
     return pl.pallas_call(
         functools.partial(exit_kernel, size),
-        grid=(blocks + 3,),
+        grid=(blocks + (7 if reduced else 3),),
         out_shape=(
             jax.ShapeDtypeStruct((ROWS, CHANNELS), bf16),
             jax.ShapeDtypeStruct((ROWS, PADDED), bf16),
             jax.ShapeDtypeStruct((ROWS, PADDED), bf16),
-            jax.ShapeDtypeStruct((PADDED, PADDED), bf16),
+            jax.ShapeDtypeStruct((CHUNK_PAD, PADDED), f32)
+            if reduced
+            else jax.ShapeDtypeStruct((PADDED, PADDED), bf16),
             jax.ShapeDtypeStruct((blocks, 2, 8, 128), f32),
         ),
         in_specs=[
@@ -570,7 +853,7 @@
             columns(ROWS, 1, blocks),
             columns(ROWS, 3, blocks),
             columns(ROWS, 2, blocks),
-            columns(PADDED, 3, blocks),
+            columns(CHUNK_PAD, 7, blocks) if reduced else columns(PADDED, 3, blocks),
             pl.BlockSpec((blocks, 2, 8, 128), lambda i: (0, 0, 0, 0)),
         ),
         scratch_shapes=[
@@ -584,7 +867,8 @@
             pltpu.SemaphoreType.DMA((2 * blocks,)),
             pltpu.SemaphoreType.DMA((blocks,)),
             pltpu.SemaphoreType.DMA((blocks,)),
-        ],
+        ]
+        + (Reducer.scratch() if reduced else []),
         name="exit",
         compiler_params=pltpu.CompilerParams(
             collective_id=2, has_side_effects=True, vmem_limit_bytes=VMEM_LIMIT
@@ -735,13 +1019,19 @@
     )(mixed, gates, spread)
 
 
+BIAS_ROWS = 24
+
+
 def back_kernel(
     size,
+    bias_ref,
     grad_ref,
     group_ref,
+    late_group_ref,
     gates_ref,
     spread_ref,
     act_ref,
+    late_act_ref,
     turned_ref,
     conv_ref,
     x_turned_ref,
@@ -753,59 +1043,100 @@
     weight_out,
     conv_out,
     total_out,
-    normed_two,
+    bias_out,
     delta_two,
-    normed_one,
     delta_one,
-    rows_ref,
     pads,
     windows,
     wide_ref,
     full_ref,
     sent,
     got,
+    bias_got,
     send_sem,
     recv_sem,
+    bias_sem,
+    *reduce_refs,
 ):
     step = pl.program_id(0)
     count = row_count(size)
+    on_global = lax.axis_index("stream") == 0
+    reducer = Reducer(reduce_refs) if reduce_refs else None
+
+    def bend(moment, micro, tile, param, at):
+        mean, inverse = moments(moment, micro, tile, count)
+        gain = 0.5 * param[at + tile : at + tile + 1]
+        shift = 0.5 * param[at + 2 + tile : at + tile + 3]
+
+        def both(act):
+            normed = act * inverse - mean * inverse
+            half = normed * gain + shift
+            bent = jnp.tanh(half)
+            return normed, (0.5 + 0.5 * bent) * (1.0 + half * (1.0 - bent))
+
+        return both
 
     @pl.when(step == 0)
     def _():
         barrier = img_barrier(size)
         pads[...] = jnp.zeros_like(pads)
         full_ref[...] = jnp.zeros_like(full_ref)
-        delta_one[...] = jnp.zeros_like(delta_one)
         windows[CONV_ROWS:] = jnp.zeros_like(windows[CONV_ROWS:])
-        pl.semaphore_wait(barrier, size - 1)
+        greeted = reducer.greet(barrier) if reducer else 0
+        pl.semaphore_wait(barrier, size - 1 + greeted)
+        stream = lax.axis_index("stream")
+        me = lax.axis_index("img")
+        bias_got[me] = bias_ref[...]
+
+        def send(step, carry):
+            pltpu.make_async_remote_copy(
+                src_ref=bias_ref,
+                dst_ref=bias_got.at[me],
+                send_sem=bias_sem.at[0],
+                recv_sem=bias_sem.at[1],
+                device_id=(stream, lax.rem(me + step, size)),
+                device_id_type=MESH,
+            ).start()
+            return carry
+
+        lax.fori_loop(1, size, send, 0)
+
+    @pl.when(step == BLOCKS)
+    def _():
+        others = bias_got.at[pl.ds(0, size - 1)]
+        pltpu.make_async_copy(others, others, bias_sem.at[0]).wait()
+        pltpu.make_async_copy(others, others, bias_sem.at[1]).wait()
+        total = bias_got[0]
+        for peer in range(1, size):
+            total = total + bias_got[peer]
+        bias_out[...] = total
+
+    if reducer:
+
+        def put(tile, rows, values):
+            weight_out[rows, 128 * tile : 128 * tile + 128] = values
+
+        reducer.advance(step - 2, BLOCKS, put)
 
     @pl.when(step < BLOCKS)
     def _():
         slot = lax.rem(step, 2)
         moment = moment_ref[step, 1]
         param = param_ref[step]
-        parts = []
+        sums = Sums()
         for micro in range(MICRO_BATCHES):
-            here = slice(HALF * micro, HALF * (micro + 1))
-            sums = []
-            products = []
-            for tile in range(2):
-                lanes = slice(128 * tile, 128 * tile + 128)
-                mean, inverse = moments(moment, micro, tile, count)
-                normed = group_ref[here, lanes] * inverse - mean * inverse
-                gain = 0.5 * param[4 + tile : 5 + tile]
-                half = normed * gain + 0.5 * param[6 + tile : 7 + tile]
-                bent = jnp.tanh(half)
-                slope = (0.5 + 0.5 * bent) * (1.0 + half * (1.0 - bent))
-                gate = dot(spread_ref[here], gates_ref[0, :, lanes])
-                pooled = dot(spread_ref[here], gates_ref[1, :, lanes])
-                delta = (grad_ref[here, lanes] * gate + pooled) * slope
-                normed_two[slot, tile, here] = normed
-                delta_two[slot, tile, here] = delta
-                sums.append(column_sum(delta))
-                products.append(column_sum(delta * normed))
-            parts += sums + products
-        send_sums(size, step, jnp.concatenate(parts), sent, got, send_sem, recv_sem)
+            bends = [bend(moment, micro, tile, param, 4) for tile in range(2)]
+            for chunk in range(HALF_STEPS * micro, HALF_STEPS * (micro + 1)):
+                here = chunk_rows(chunk)
+                gate = dot(spread_ref[here], gates_ref[0])
+                pooled = dot(spread_ref[here], gates_ref[1])
+                for tile in range(2):
+                    lanes = slice(128 * tile, 128 * tile + 128)
+                    normed, slope = bends[tile](group_ref[here, lanes])
+                    delta = (grad_ref[here, lanes] * gate[:, lanes] + pooled[:, lanes]) * slope
+                    delta_two[slot, tile, here] = delta
+                    sums.add(micro, tile, delta, delta * normed)
+        send_sums(size, step, sums.packed(), sent, got, send_sem, recv_sem)
 
     @pl.when((step >= 1) & (step < BLOCKS + 1))
     def _():
@@ -815,62 +1146,80 @@
         total_out[block, 0] = total
         param = param_ref[block]
         moment = moment_ref[block, 1]
-        for micro in range(MICRO_BATCHES):
-            here = slice(HALF * micro, HALF * (micro + 1))
-            for tile in range(2):
-                rows_ref[tile, here] = norm_back(
-                    delta_two[slot, tile, here],
-                    normed_two[slot, tile, here],
-                    moment,
-                    total,
-                    micro,
-                    tile,
-                    param[4 + tile : 5 + tile],
-                    count,
-                )
-        scatter_rows(rows_ref, pads, edges)
+        backs = {
+            (micro, tile): norm_back(moment, total, micro, tile, param[4 + tile : 5 + tile], count)
+            for micro in range(MICRO_BATCHES)
+            for tile in range(2)
+        }
+
+        def delta_rows(tile, start, length):
+            here = slice(start, start + length)
+            return backs[start // HALF, tile](
+                delta_two[slot, tile, here], late_group_ref[here, 128 * tile : 128 * tile + 128]
+            )
+
         same = same_group(LANES, BLOCK)
         for offset in range(9):
             full = dot(fold_ref[...], conv_ref[offset], ((1,), (1,)))
             full_ref[LANES * offset : LANES * (offset + 1), :BLOCK] = jnp.where(
                 same, full, 0.0
             ).astype(bf16)
-        for image in range(IMAGE_DEV):
+
+        def convolve(image):
             stack_windows(pads, windows, image, -1)
             here = slice(IMAGE_PAD * image, IMAGE_PAD * (image + 1))
             wide = dot(windows[here], full_ref[...])
-            take_result(wide, image, delta_one, slot, wide_ref)
-        same = same_group(LANES, LANES)
+            wide_ref[0, here] = wide[:, :128]
+            wide_ref[1, here] = wide[:, 128:]
+
+        moment_one = moment_ref[block, 0]
+
+        def finish(load):
+            sums = Sums()
+            for micro in range(MICRO_BATCHES):
+                for tile in range(2):
+                    bent = bend(moment_one, micro, tile, param, 0)
+                    for chunk in range(HALF_STEPS * micro, HALF_STEPS * (micro + 1)):
+                        here = chunk_rows(chunk)
+                        normed, slope = bent(act_ref[here, 128 * tile : 128 * tile + 128])
+                        delta = load(tile, chunk) * slope
+                        delta_one[slot, tile, here] = delta
+                        sums.add(micro, tile, delta, delta * normed)
+            send_sums(
+                size, BLOCKS + block, sums.packed(), sent, got, send_sem, recv_sem
+            )
+
+        @pl.when(on_global)
+        def _():
+            pad_global(delta_rows, pads, edges)
+            for image in range(IMAGE_DEV):
+                convolve(image)
+            finish(lambda tile, chunk: unpadded(wide_ref, tile, STEP // 8 * chunk, STEP // 8))
+
+        @pl.when(jnp.logical_not(on_global))
+        def _():
+            rows_ref = delta_one.at[slot]
+            for chunk in range(STEPS):
+                for tile in range(2):
+                    rows_ref[tile, chunk_rows(chunk)] = delta_rows(tile, STEP * chunk, STEP)
+            pad_small(rows_ref, pads)
+            for image in range(IMAGE_DEV):
+                convolve(image)
+            for chunk in range(STEPS):
+                for tile in range(2):
+                    rows_ref[tile, chunk_rows(chunk)] = jnp.zeros((STEP, 128), f32)
+            unpad_small(wide_ref, rows_ref)
+            finish(lambda tile, chunk: rows_ref[tile, chunk_rows(chunk)])
+
         for offset in range(9):
-            lanes = slice(LANES * offset, LANES * (offset + 1))
-            grad = dot(turned_ref[0], windows[:, lanes])
-            grad = jnp.where(same, grad, 0.0).astype(bf16)
-            conv_out[offset] = dot(grad, fold_ref[...])[:BLOCK].astype(bf16)
-        moment = moment_ref[block, 0]
-        parts = []
-        for micro in range(MICRO_BATCHES):
-            here = slice(HALF * micro, HALF * (micro + 1))
-            sums = []
-            products = []
-            for tile in range(2):
-                lanes = slice(128 * tile, 128 * tile + 128)
-                mean, inverse = moments(moment, micro, tile, count)
-                normed = act_ref[here, lanes] * inverse - mean * inverse
-                gain = 0.5 * param[tile : tile + 1]
-                half = normed * gain + 0.5 * param[2 + tile : 3 + tile]
-                bent = jnp.tanh(half)
-                slope = (0.5 + 0.5 * bent) * (1.0 + half * (1.0 - bent))
-                delta = delta_one[slot, tile, here] * slope
-                normed_one[slot, tile, here] = normed
-                delta_one[slot, tile, here] = delta
-                sums.append(column_sum(delta))
-                products.append(column_sum(delta * normed))
-            parts += sums + products
-        send_sums(
-            size, BLOCKS + block, jnp.concatenate(parts), sent, got, send_sem, recv_sem
-        )
-
-    @pl.when(step >= 2)
+            grad = dot(turned_ref[0], windows[:, LANES * offset : LANES * (offset + 1)])
+            pieces = []
+            for group in range(4):
+                here = slice(GROUP_WIDTH * group, GROUP_WIDTH * (group + 1))
+                pieces.append(grad[here, here])
+            conv_out[offset] = jnp.concatenate(pieces).astype(bf16)
+
+    @pl.when((step >= 2) & (step < BLOCKS + 2))
     def _():
         block = step - 2
         slot = lax.rem(block, 2)
@@ -879,68 +1228,76 @@
         param = param_ref[block]
         moment = moment_ref[block, 0]
         for micro in range(MICRO_BATCHES):
-            here = slice(HALF * micro, HALF * (micro + 1))
             for tile in range(2):
-                delta_out[here, 128 * tile : 128 * tile + 128] = norm_back(
-                    delta_one[slot, tile, here],
-                    normed_one[slot, tile, here],
-                    moment,
-                    total,
-                    micro,
-                    tile,
-                    param[tile : tile + 1],
-                    count,
-                ).astype(bf16)
-        weight_out[...] = dot(x_turned_ref[...], delta_out[...]).astype(bf16)
+                lanes = slice(128 * tile, 128 * tile + 128)
+                back = norm_back(moment, total, micro, tile, param[tile : tile + 1], count)
+                for chunk in range(HALF_STEPS * micro, HALF_STEPS * (micro + 1)):
+                    here = chunk_rows(chunk)
+                    delta_out[here, lanes] = back(
+                        delta_one[slot, tile, here], late_act_ref[here, lanes]
+                    ).astype(bf16)
+        grad = dot(x_turned_ref[...], delta_out[...])
+        if reducer:
+            reducer.begin(block, grad)
+        else:
+            weight_out[...] = grad.astype(bf16)
 
 
 def run_back(
-    size, grad, group, gates, spread, act, turned, conv, x_turned, params, moment, edges, fold
+    size, bias, grad, group, gates, spread, act, turned, conv, x_turned, params, moment, edges, fold
 ):
+    reduced = size == SHARDS
     return pl.pallas_call(
         functools.partial(back_kernel, size),
-        grid=(BLOCKS + 2,),
+        grid=(BLOCKS + (6 if reduced else 2),),
         out_shape=(
             jax.ShapeDtypeStruct((ROWS, WIDE), bf16),
-            jax.ShapeDtypeStruct((PADDED, WIDE), bf16),
+            jax.ShapeDtypeStruct((CHUNK_PAD, WIDE), f32)
+            if reduced
+            else jax.ShapeDtypeStruct((PADDED, WIDE), bf16),
             jax.ShapeDtypeStruct((9, CHANNELS, GROUP_WIDTH), bf16),
             jax.ShapeDtypeStruct((BLOCKS, 2, 8, 128), f32),
+            jax.ShapeDtypeStruct((BIAS_ROWS, 128), f32),
         ),
         in_specs=[
+            whole((BIAS_ROWS, 128)),
             columns(ROWS, 0, BLOCKS),
             columns(ROWS, 0, BLOCKS),
+            columns(ROWS, 1, BLOCKS),
             pl.BlockSpec((2, 2 * CROPS, LANES), lambda i: (0, 0, jnp.clip(i, 0, BLOCKS - 1))),
             whole((ROWS, 2 * CROPS)),
             columns(ROWS, 1, BLOCKS),
+            columns(ROWS, 2, BLOCKS),
             pl.BlockSpec((1, LANES, DEEP_ROWS), lambda i: (jnp.clip(i - 1, 0, BLOCKS - 1), 0, 0)),
             pl.BlockSpec((9, BLOCK, GROUP_WIDTH), lambda i: (0, jnp.clip(i - 1, 0, BLOCKS - 1), 0)),
             whole((PADDED, ROWS)),
             whole((BLOCKS, 8, 128)),
             whole((BLOCKS, 2, 8, 128)),
-            whole((2, PAD_ROWS, 128)),
+            whole((2, IMAGE_PAD, 128)),
             whole((LANES, GROUP_WIDTH)),
         ],
         out_specs=(
             columns(ROWS, 2, BLOCKS),
-            columns(PADDED, 2, BLOCKS),
+            columns(CHUNK_PAD, 6, BLOCKS) if reduced else columns(PADDED, 2, BLOCKS),
             pl.BlockSpec((9, BLOCK, GROUP_WIDTH), lambda i: (0, jnp.clip(i - 1, 0, BLOCKS - 1), 0)),
             pl.BlockSpec((BLOCKS, 2, 8, 128), lambda i: (0, 0, 0, 0)),
+            pl.BlockSpec((BIAS_ROWS, 128), lambda i: (0, 0)),
         ),
         scratch_shapes=[
             pltpu.VMEM((2, 2, ROWS, 128), f32),
             pltpu.VMEM((2, 2, ROWS, 128), f32),
-            pltpu.VMEM((2, 2, ROWS, 128), f32),
-            pltpu.VMEM((2, 2, ROWS, 128), f32),
-            pltpu.VMEM((2, ROWS, 128), f32),
             pltpu.VMEM((3, 2, PAD_ROWS, 128), f32),
             pltpu.VMEM((DEEP_ROWS, 9 * LANES), bf16),
-            pltpu.VMEM((2, IMAGE_PAD, 128), f32),
+            pltpu.VMEM((2, CONV_ROWS, 128), f32),
             pltpu.VMEM((9 * LANES, LANES), bf16),
             pltpu.VMEM((2 * BLOCKS, 8, 128), f32),
             pltpu.VMEM((2 * BLOCKS, size, 8, 128), f32),
+            pltpu.VMEM((size, BIAS_ROWS, 128), f32),
             pltpu.SemaphoreType.DMA((2 * BLOCKS,)),
             pltpu.SemaphoreType.DMA((2 * BLOCKS,)),
-        ],
+            pltpu.SemaphoreType.DMA((2,)),
+        ]
+        + (Reducer.scratch() if reduced else []),
         name="back",
         compiler_params=pltpu.CompilerParams(
             collective_id=3, has_side_effects=True, vmem_limit_bytes=VMEM_LIMIT
@@ -950,7 +1307,322 @@
             bytes_accessed=90 * 2**20,
             transcendentals=2 * ROWS * WIDE,
         ),
-    )(grad, group, gates, spread, act, turned, conv, x_turned, params, moment, edges, fold)
+    )(bias, grad, group, group, gates, spread, act, act, turned, conv, x_turned, params, moment, edges, fold)
+
+
+CONV_LINES = 1152
+
+
+def gather_kernel(
+    entry_ref,
+    conv_ref,
+    x_ref,
+    entry_out,
+    conv_out,
+    chunk_out,
+    turned_out,
+    x_rows,
+    chunk_rows_ref,
+    turned_rows,
+    send_sem,
+    recv_sem,
+    local_sem,
+    store_sem,
+):
+    stream, z, x, core = place()
+    pieces = (entry_ref, conv_ref)
+    wholes = (entry_out, conv_out)
+    quarters = (CHUNK_PAD // 4, CONV_LINES // 4)
+    waiting = []
+
+    def shard(k, across=0, beside=0):
+        return 4 * (z ^ k) + 2 * (x ^ across) + (core ^ beside)
+
+    def region(array, index, first, count):
+        rows = quarters[array]
+        return wholes[array].at[index, pl.ds(pl.multiple_of(rows * first, 16), rows * count)]
+
+    def device(name, k=0):
+        if name == "y":
+            return (1 - stream, shard(0))
+        return (stream, {"z": shard(k), "x": shard(0, 1), "core": shard(0, 0, 1)}[name])
+
+    def push(slot, to, index, first, count, k=0, own=False):
+        for array in range(2):
+            target = region(array, index, first, count)
+            source = target
+            if own:
+                rows = quarters[array]
+                source = pieces[array].at[
+                    pl.ds(pl.multiple_of(rows * first, 16), rows * count)
+                ]
+            pltpu.make_async_remote_copy(
+                src_ref=source,
+                dst_ref=target,
+                send_sem=send_sem.at[array, slot],
+                recv_sem=recv_sem.at[array, slot],
+                device_id=device(to, k),
+                device_id_type=MESH,
+            ).start()
+            waiting.append((array, slot, target))
+
+    def arrive(slot, index, first, count):
+        for array in range(2):
+            target = region(array, index, first, count)
+            pltpu.make_async_copy(target, target, recv_sem.at[array, slot]).wait()
+
+    barrier = pltpu.get_barrier_semaphore()
+    for name, k in (("z", 1), ("z", 2), ("z", 3), ("x", 0), ("y", 0), ("core", 0)):
+        pl.semaphore_signal(barrier, inc=1, device_id=device(name, k), device_id_type=MESH)
+    load = pltpu.make_async_copy(x_ref, x_rows, local_sem.at[2])
+    load.start()
+    keep = [
+        pltpu.make_async_copy(pieces[array], wholes[array].at[shard(0)], local_sem.at[array])
+        for array in range(2)
+    ]
+    for copy in keep:
+        copy.start()
+    pl.semaphore_wait(barrier, 6)
+
+    push(6, "x", shard(0), stream, 3, own=True)
+    for k in (1, 2, 3):
+        push(k - 1, "z", shard(0), 2 * stream, 2, k, own=True)
+    push(17, "core", shard(0), 0, 4, own=True)
+
+    stores = []
+
+    def prepare(pair):
+        if pair == 0:
+            load.wait()
+        slot = pair % 2
+        if pair >= 2:
+            for copy in stores[pair - 2]:
+                copy.wait()
+        depth = 384
+        first = (PAIR * pair) // 128
+        source = 128 * first - PAIR * pair
+        values = x_rows[:, 128 * first : 128 * first + depth]
+        there = lax.broadcasted_iota(jnp.int32, (depth, LANES), 0) + source
+        pick = one_hot(there == pair_lane((depth, LANES), 1))
+        chunk_rows_ref[slot] = dot(values, pick).astype(bf16)
+        there = lax.broadcasted_iota(jnp.int32, (LANES, depth), 1) + source
+        pick = one_hot(there == pair_lane((LANES, depth), 0))
+        turned_rows[slot] = dot(pick, values, ((1,), (1,))).astype(bf16)
+        lanes = slice(LANES * pair, LANES * (pair + 1))
+        copies = (
+            pltpu.make_async_copy(chunk_rows_ref.at[slot], chunk_out.at[:, lanes], store_sem.at[0, pair]),
+            pltpu.make_async_copy(turned_rows.at[slot], turned_out.at[lanes], store_sem.at[1, pair]),
+        )
+        for copy in copies:
+            copy.start()
+        stores.append(copies)
+
+    def from_z(k):
+        arrive(k - 1, shard(k), 2 * stream, 2)
+        push(6 + k, "x", shard(k), 2 * stream, 2)
+        push(2 + k, "y", shard(k), 2 * stream, 2)
+        push(17 + k, "core", shard(k), 2 * stream, 2)
+
+    def from_y(k):
+        arrive(2 + k, shard(k), 2 - 2 * stream, 2)
+        push(9 + k, "x", shard(k), 2 - stream, 1)
+        push(20 + k, "core", shard(k), 2 - 2 * stream, 2)
+
+    def from_x(k):
+        if k == 0:
+            arrive(6, shard(0, 1), stream, 3)
+            push(13, "y", shard(0, 1), 3 * stream, 1)
+            push(24, "core", shard(0, 1), stream, 3)
+        else:
+            arrive(6 + k, shard(k, 1), 2 * stream, 2)
+            push(13 + k, "y", shard(k, 1), 3 * stream, 1)
+            push(24 + k, "core", shard(k, 1), 2 * stream, 2)
+
+    def last_x(k):
+        arrive(9 + k, shard(k, 1), 2 - stream, 1)
+        push(27 + k, "core", shard(k, 1), 2 - stream, 1)
+
+    def last_y(k):
+        arrive(13 + k, shard(k, 1), 3 - 3 * stream, 1)
+        push(31 + k, "core", shard(k, 1), 3 - 3 * stream, 1)
+
+    prepare(0)
+    prepare(1)
+    from_z(1)
+    prepare(2)
+    from_z(2)
+    from_x(0)
+    prepare(3)
+    from_z(3)
+    from_y(1)
+    prepare(4)
+    from_x(1)
+    from_y(2)
+    prepare(5)
+    from_x(2)
+    from_y(3)
+    prepare(6)
+    from_x(3)
+    last_y(0)
+    last_x(1)
+    prepare(7)
+    last_y(1)
+    last_x(2)
+    last_y(2)
+    last_x(3)
+    last_y(3)
+
+    arrive(17, shard(0, 0, 1), 0, 4)
+    for k in (1, 2, 3):
+        arrive(17 + k, shard(k, 0, 1), 2 * stream, 2)
+        arrive(20 + k, shard(k, 0, 1), 2 - 2 * stream, 2)
+    arrive(24, shard(0, 1, 1), stream, 3)
+    for k in (1, 2, 3):
+        arrive(24 + k, shard(k, 1, 1), 2 * stream, 2)
+        arrive(27 + k, shard(k, 1, 1), 2 - stream, 1)
+    for k in range(4):
+        arrive(31 + k, shard(k, 1, 1), 3 - 3 * stream, 1)
+    for array, slot, target in waiting:
+        pltpu.make_async_copy(target, target, send_sem.at[array, slot]).wait()
+    for copy in keep:
+        copy.wait()
+    for pair in (6, 7):
+        for copy in stores[pair]:
+            copy.wait()
+
+
+def run_gather(entry, conv, x):
+    return pl.pallas_call(
+        gather_kernel,
+        out_shape=(
+            jax.ShapeDtypeStruct((SHARDS, CHUNK_PAD, WIDE), bf16),
+            jax.ShapeDtypeStruct((SHARDS, CONV_LINES, 128), bf16),
+            jax.ShapeDtypeStruct((ROWS, PADDED), bf16),
+            jax.ShapeDtypeStruct((PADDED, ROWS), bf16),
+        ),
+        in_specs=[pl.BlockSpec(memory_space=HBM)] * 3,
+        out_specs=(pl.BlockSpec(memory_space=HBM),) * 4,
+        scratch_shapes=[
+            pltpu.VMEM((ROWS, PADDED), bf16),
+            pltpu.VMEM((2, ROWS, LANES), bf16),
+            pltpu.VMEM((2, LANES, ROWS), bf16),
+            pltpu.SemaphoreType.DMA((2, 35)),
+            pltpu.SemaphoreType.DMA((2, 35)),
+            pltpu.SemaphoreType.DMA((3,)),
+            pltpu.SemaphoreType.DMA((2, OUT_BLOCKS)),
+        ],
+        name="gather",
+        compiler_params=pltpu.CompilerParams(
+            collective_id=4, has_side_effects=True, vmem_limit_bytes=VMEM_LIMIT
+        ),
+        cost_estimate=pl.CostEstimate(
+            flops=4 * ROWS * 384 * PADDED, bytes_accessed=200 * 2**20, transcendentals=0
+        ),
+    )(entry, conv, x)
+
+
+CONV_BLOCKS = 5
+
+
+def input_kernel(delta_ref, weight_ref, residual_ref, live_ref, *refs):
+    block = pl.program_id(0)
+    if len(refs) == 1:
+        (grad_out,) = refs
+    else:
+        conv_ref, grad_out, conv_out, load_sem, *reduce_refs = refs
+        reducer = Reducer(reduce_refs)
+
+        def load(at):
+            hold = lax.rem(at, 2)
+            return pltpu.make_async_copy(
+                conv_ref.at[at], reducer.local.at[hold], load_sem.at[hold]
+            )
+
+        @pl.when(block == 0)
+        def _():
+            load(0).start()
+            barrier = pltpu.get_barrier_semaphore()
+            greeted = reducer.greet(barrier)
+            peers = [(0, 0, 1), (0, 1, 0), (1, 0, 0), (2, 0, 0), (3, 0, 0)]
+            for peer in peers:
+                pl.semaphore_signal(
+                    barrier,
+                    inc=1,
+                    device_id=(reducer.stream, reducer.index(*peer)),
+                    device_id_type=MESH,
+                )
+            pl.semaphore_wait(barrier, len(peers) + greeted)
+
+        def put(tile, rows, values):
+            conv_out[block - 4, tile, rows] = values
+
+        reducer.advance(block, CONV_BLOCKS, put)
+
+        @pl.when(block < CONV_BLOCKS)
+        def _():
+            load(block).wait()
+            reducer.core_copy(block).start()
+
+        @pl.when(block < CONV_BLOCKS - 1)
+        def _():
+            load(block + 1).start()
+
+    @pl.when(block < OUT_BLOCKS)
+    def _():
+        spans = 4
+        first = jnp.minimum((LANES * block) // CHUNK, SHARDS - spans)
+        depth = spans * CHUNK_PAD
+        row = lax.broadcasted_iota(jnp.int32, (LANES, depth), 0) + LANES * block
+        lane = lax.broadcasted_iota(jnp.int32, (LANES, depth), 1)
+        channel = CHUNK * (first + lane // CHUNK_PAD) + lane % CHUNK_PAD
+        pick = one_hot((channel == row) & (lane % CHUNK_PAD < CHUNK))
+        rows = pl.ds(pl.multiple_of(CHUNK_PAD * first, CHUNK_PAD), depth)
+        weight = dot(pick, weight_ref[rows]).astype(bf16)
+        for micro in range(MICRO_BATCHES):
+            here = slice(HALF * micro, HALF * (micro + 1))
+            grad = dot(delta_ref[here], weight, ((1,), (1,)))
+            for tile in range(2):
+                lanes = slice(128 * tile, 128 * tile + 128)
+                grad_out[here, lanes] = (
+                    (grad[:, lanes] + residual_ref[here, lanes].astype(f32))
+                    * live_ref[here].astype(f32)
+                ).astype(bf16)
+
+
+def run_input(delta, weight, residual, live, conv=None):
+    reduced = conv is not None
+    out_shape = jax.ShapeDtypeStruct((ROWS, CHANNELS), bf16)
+    out_specs = columns(ROWS, 0, OUT_BLOCKS)
+    in_specs = [
+        whole((ROWS, WIDE)),
+        whole((PADDED, WIDE)),
+        columns(ROWS, 0, OUT_BLOCKS),
+        whole((ROWS, 128)),
+    ]
+    args = [delta, weight, residual, live]
+    if reduced:
+        shape = (CONV_BLOCKS, 2, 128, 128)
+        out_shape = (out_shape, jax.ShapeDtypeStruct(shape, f32))
+        out_specs = (out_specs, pl.BlockSpec(shape, lambda i: (0, 0, 0, 0)))
+        in_specs.append(pl.BlockSpec(memory_space=HBM))
+        args.append(conv)
+    return pl.pallas_call(
+        input_kernel,
+        grid=(CONV_BLOCKS + 4 if reduced else OUT_BLOCKS,),
+        out_shape=out_shape,
+        in_specs=in_specs,
+        out_specs=out_specs,
+        scratch_shapes=[pltpu.SemaphoreType.DMA((2,))] + Reducer.scratch() if reduced else [],
+        name="input",
+        compiler_params=pltpu.CompilerParams(
+            vmem_limit_bytes=VMEM_LIMIT,
+            collective_id=5 if reduced else None,
+            has_side_effects=reduced,
+        ),
+        cost_estimate=pl.CostEstimate(
+            flops=2 * ROWS * WIDE * PADDED, bytes_accessed=35 * 2**20, transcendentals=0
+        ),
+    )(*args)
 
 
 def split(values):
@@ -1058,18 +1730,18 @@
     x = jnp.pad(jnp.where(live[:, None], block_in[0], 0), pad_out)
     cot = jnp.pad(jnp.where(live[:, None], out_cotangent[0], 0), pad_out)
 
+    lines = CONV_LINES - 18
     if size == SHARDS:
-        entry_piece = wide_lanes(entry_weight.reshape(CHUNK, CHANNELS)).reshape(-1)
-        entry_mat = gather(entry_piece, WIDE, size)
+        entry_piece = wide_lanes(entry_weight.reshape(CHUNK, CHANNELS))
+        entry_piece = jnp.pad(entry_piece, ((0, CHUNK_PAD - CHUNK), (0, 0)))
+        piece = group_weight.reshape(lines, GROUP_WIDTH)
+        piece = jnp.pad(piece, ((0, CONV_LINES - lines), (0, 128 - GROUP_WIDTH)))
+        entry_mat, conv, x_chunked, x_turned = run_gather(entry_piece, piece, x)
+        entry_mat = entry_mat.reshape(PADDED, WIDE)
+        conv = conv[:, :lines, :GROUP_WIDTH]
     else:
+        x_chunked, x_turned = run_prepare(x)
         entry_mat = wide_lanes(gather(entry_weight, CHANNELS, size)[:, :CHANNELS])
-    lines = group_weight.shape[0] // GROUP_WIDTH if size == SHARDS else 0
-    if lines:
-        lines_pad = -(-lines // 16) * 16
-        piece = group_weight.reshape(lines, GROUP_WIDTH)
-        piece = jnp.pad(piece, ((0, lines_pad - lines), (0, 128 - GROUP_WIDTH)))
-        conv = lax.all_gather(piece, "img", axis=0, tiled=False)[:, :lines, :GROUP_WIDTH]
-    else:
         conv = lax.all_gather(group_weight, "img", axis=0, tiled=True)
     conv = conv.reshape(9, CHANNELS, GROUP_WIDTH)
     squeeze_mat = gather(squeeze_weight, SQUEEZE, size)[:, :SQUEEZE]
@@ -1090,7 +1762,6 @@
     fold = np.zeros((LANES, GROUP_WIDTH), np.float32)
     fold[np.arange(BLOCK), np.arange(BLOCK) % GROUP_WIDTH] = 1
     fold = jnp.asarray(fold, bf16)
-    x_chunked, x_turned = run_prepare(x)
     act, turned, group, mixed, pooled, moment = run_entry(
         size, x_chunked, entry_mat, conv, params, pool, edges, fold.T
     )
@@ -1124,7 +1795,10 @@
     block_out, exit_delta, residual, exit_grad, exit_total = run_exit(
         size, scaled, scaled_turned, exit_mat, x, cot, exit_params, pair, pair.T, live_lanes
     )
-    exit_shard = scatter(exit_grad, CHANNELS, size)
+    if size == SHARDS:
+        exit_shard = exit_grad[:CHUNK, :CHANNELS].reshape(-1)
+    else:
+        exit_shard = scatter(exit_grad, CHANNELS, size)
     scaled_grad, gate_grad = run_gate(exit_delta, exit_mat, mixed, pool)
 
     used = crop_ids < IMAGE_DEV * per_image
@@ -1143,28 +1817,29 @@
     excite_shard = scatter(excite_grad.astype(bf16), SQUEEZE, size)
     squeeze_shard = scatter(squeeze_grad.astype(bf16), SQUEEZE, size)
     gates = jnp.stack([gate_terms, split(wide_lanes(pooled_grad))])
-    entry_delta, entry_grad, conv_grad, totals = run_back(
-        size, scaled_grad, group, gates, spread, act, turned, conv, x_turned, params,
+    bias_rows = jnp.concatenate(
+        [
+            jnp.pad(jnp.sum(squeeze_delta, axis=0), (0, 512 - SQUEEZE)),
+            jnp.pad(jnp.sum(excite_delta, axis=0), (0, 20 * 128 - CHANNELS)),
+        ]
+    ).reshape(BIAS_ROWS, 128)
+    entry_delta, entry_grad, conv_grad, totals, bias_totals = run_back(
+        size, bias_rows, scaled_grad, group, gates, spread, act, turned, conv, x_turned, params,
         moment, edges, fold,
     )
-    input_grad = unchunked(dot(entry_delta, entry_mat, ((1,), (1,))))
-    input_grad = input_grad + residual[:, :CHANNELS].astype(f32)
-    input_grad = jnp.where(live[:, None], input_grad, 0.0).astype(bf16)
-
     if size == SHARDS:
-        part = lax.psum_scatter(entry_grad, "img", scatter_dimension=0, tiled=True)
-        part = swap_sum(part)
-        entry_shard = narrow_lanes(part[:CHUNK]).reshape(-1)
-    else:
-        entry_shard = scatter(narrow_lanes(entry_grad), CHANNELS, size)
-    if lines:
+        entry_shard = narrow_lanes(entry_grad[:CHUNK]).reshape(-1)
+        conv_lines = 256 * CONV_BLOCKS
         conv_grad = conv_grad.reshape(SHARDS, lines, GROUP_WIDTH)
         conv_grad = jnp.pad(
-            conv_grad, ((0, 0), (0, lines_pad - lines), (0, 128 - GROUP_WIDTH))
-        ).reshape(-1, 128)
-        conv_part = lax.psum_scatter(conv_grad, "img", scatter_dimension=0, tiled=True)
-        conv_shard = swap_sum(conv_part)[:lines, :GROUP_WIDTH].reshape(-1)
+            conv_grad, ((0, 0), (0, conv_lines - lines), (0, 128 - GROUP_WIDTH))
+        ).reshape(4, 2, 2, CONV_BLOCKS, 2, 128, 128)
+        conv_grad = conv_grad.transpose(3, 2, 1, 0, 4, 5, 6)
+        input_grad, conv_part = run_input(entry_delta, entry_mat, residual, live_lanes, conv_grad)
+        conv_shard = conv_part.reshape(conv_lines, 128)[:lines, :GROUP_WIDTH].reshape(-1)
     else:
+        input_grad = run_input(entry_delta, entry_mat, residual, live_lanes)
+        entry_shard = scatter(narrow_lanes(entry_grad), CHANNELS, size)
         conv_part = lax.psum_scatter(
             conv_grad.reshape(-1), "img", scatter_dimension=0, tiled=True
         )
@@ -1178,20 +1853,25 @@
     group_gain_grad, group_shift_grad = [narrow_lanes(v) for v in folded(totals[:, 0])]
     entry_gain_grad, entry_shift_grad = [narrow_lanes(v) for v in folded(totals[:, 1])]
     exit_gain_grad, exit_shift_grad = [v[:CHANNELS] for v in folded(exit_total[:, 1])]
-    bias_sums = lax.psum(
-        (jnp.sum(squeeze_delta, axis=0), jnp.sum(excite_delta, axis=0)), ("stream", "img")
+    bias_totals = bias_totals.reshape(-1)
+    kept = jnp.concatenate(
+        [
+            jnp.stack(
+                [
+                    entry_gain_grad,
+                    entry_shift_grad,
+                    group_gain_grad,
+                    group_shift_grad,
+                    exit_gain_grad,
+                    exit_shift_grad,
+                    bias_totals[512 : 512 + CHANNELS],
+                ]
+            ),
+            jnp.pad(bias_totals[:SQUEEZE], (0, CHANNELS - SQUEEZE))[None],
+        ]
     )
-    smalls = lax.psum(
-        (
-            entry_gain_grad,
-            entry_shift_grad,
-            group_gain_grad,
-            group_shift_grad,
-            exit_gain_grad,
-            exit_shift_grad,
-        ),
-        "stream",
-    )
+    smalls = swap_sum(kept)
+
     return (
         block_out[None],
         input_grad[None],
@@ -1202,9 +1882,9 @@
         smalls[2],
         smalls[3],
         shards[2],
-        bias_sums[0],
+        smalls[7, :SQUEEZE],
         shards[3],
-        bias_sums[1],
+        smalls[6],
         shards[4],
         smalls[4],
         smalls[5],

time: 954 us -> 677 us (0.71)
  waiting for transfers between devices: 322 us -> 2.84 us
  Pallas kernels: 381 us -> 523 us
  blocking collectives: 46.2 us -> 0 us
  matrix products: 41.5 us -> 19.9 us
  local copies, waits for them, and re-layouts: 95.6 us -> 81.9 us
  other arithmetic: 36.5 us -> 25.9 us
    pallas_call x3 -> x4, Pallas kernels: 238 us -> 399 us  [the longest x1 150 us: run_back(): pl.pallas_call(functools.partial(back_kernel, size), grid=(BLOCKS + (6 if...]
    all_gather x4 -> x3, waiting for transfers between devices: 118 us -> 0.02 us  [gather(): return lax.all_gather(piece, 'img', axis=0, tiled=True)]
    reduce_scatter x2 -> x0, waiting for transfers between devices: 111 us -> none  [the longest x1 111 us: local(): part = lax.psum_scatter(entry_grad, 'img', scatter_dimension=0, tiled=True)]
    reduce_scatter x3 -> x2, waiting for transfers between devices: 66.7 us -> 0.02 us  [scatter(): part = lax.psum_scatter(grads, 'img', scatter_dimension=0, tiled=True)]
    psum x2 -> x0, blocking collectives: 46.2 us -> none  [the longest x1 38.2 us: local(): lax.psum((jnp.sum(squeeze_delta, axis=0), jnp.sum(excite_delta, axis=0)),...]
    dot_general x1 -> x0, matrix products: 21.8 us -> none  [dot(): return lax.dot_general(a, b, (dims, ((), ())), preferred_element_type=f32)]
    pallas_call x1, Pallas kernels: 94.3 us -> 75 us  [run_entry(): pl.pallas_call(functools.partial(entry_kernel, size), grid=(BLOCKS + 2,),...]
    all_gather x1 -> x0, waiting for transfers between devices: 16 us -> none  [local(): lax.all_gather(piece, 'img', axis=0, tiled=False)[:, :lines, :GROUP_WIDTH]]
  transfers between devices with their start and end apart: 15 -> 8, of which waited for: 6 -> 2; matrix products, arithmetic and copies ran while one was open for 16% -> 16% of each run, Pallas kernels for 30% -> 57%
where the time goes in v2:
time: 677 us; the launch traced here: 673 us
  Pallas kernels  523 us (77%)
  local copies, waits for them, and re-layouts  81.9 us (12%)
  other arithmetic  25.9 us (4%)
  matrix products  19.9 us (3%)
  between operations  15 us (2%)
    pallas_call x1, Pallas kernels, run_back(): pl.pallas_call(functools.partial(back_kernel, size), grid=(BLOCKS + (6 if...  150 us
    pallas_call x1, Pallas kernels, run_exit(): pl.pallas_call(functools.partial(exit_kernel, size), grid=(blocks + (7 if...  106 us
    pallas_call x1, Pallas kernels, run_gather(): pl.pallas_call(gather_kernel, out_shape=(jax.ShapeDtypeStruct((SHARDS, CH...  86.3 us
    pallas_call x1, Pallas kernels, run_entry(): pl.pallas_call(functools.partial(entry_kernel, size), grid=(BLOCKS + 2,),...  75 us
    pallas_call x1, Pallas kernels, run_input(): pl.pallas_call(input_kernel, grid=(CONV_BLOCKS + 4 if reduced else OUT_BL...  56.3 us
    pallas_call x1, Pallas kernels, run_gate(): pl.pallas_call(gate_kernel, grid=(BLOCKS,), out_shape=(jax.ShapeDtypeStru...  30.5 us
    pallas_call x1, Pallas kernels, run_scale(): pl.pallas_call(scale_kernel, grid=(BLOCKS + OUT_BLOCKS,), out_shape=(jax....  18.3 us
    dot_general x5, matrix products, small_dot(): lax.dot_general(a, b.astype(f32), (dims, ((), ())), precision=lax.Precisi...  17.6 us
  transfers between devices with their start and end apart: 8, of which 2 were waited for; matrix products, arithmetic and copies ran while one was open for 16% of the time, Pallas kernels for 57%

profile of v2, /device:TPU:0, one launch (start us, length us, event | category | flops | bytes accessed | tf_op | source)
XLA Modules:
  0.0 672.7 jit_solution(14664166492031753184)
XLA Ops:
  20.2 6.0 bitcast_select_fusion
  26.2 3.4 pad.103.cot_ref
  29.6 3.5 pad.92.x_ref
  33.1 86.3 %gather.1 = (bf16[16,128,2304]{2,1,0:T(8,128)(2,1)}, bf16[16,1152,128]{2,1,0:T(8,128)(2,1)}, bf16[1568,2048]{1,0:T(8,128)(2,1)}, bf16[2048,1568]{1,0:T(8,128)(2,1)}) custom-call(bf16[128,2304]{1,0:T(8,128)(2,1)} %pad.90.entry_ref, bf16[1152,128]{1,0:T(8,128)(2,1)} %pad.91.conv_ref, bf16[1568,2048]{1,0:T(8,128)(2,1)} %pad.92.x_ref), custom_call_target="tpu_custom_call" | custom-call | flops 4932501504 | bytes 209715200 | tf_op jit(solution)/shard_map/gather/pallas_call | solution.py:1495
  119.4 4.8 slice.124
  124.2 6.0 reshape.304.conv_ref
  132.6 75.0 %entry.1 = (f32[1568,2304]{1,0:T(8,128)}, bf16[9,256,1792]{2,1,0:T(8,128)(2,1)}, f32[1568,2304]{1,0:T(8,128)}, bf16[1568,2304]{1,0:T(8,128)(2,1)}, f32[16,2304]{1,0:T(8,128)}, /*index=5*/f32[9,2,8,128]{3,2,1,0:T(8,128)}) custom-call(bf16[1568,2048]{1,0:T(8,128)(2,1)} %get-tuple-element.41.x_ref, bf16[2048,2304]{1,0:T(8,128)(2,1)} %bitcast.149, ...), custom_call_target="tpu_custom_call" | custom-call | flops 31444697088 | bytes 73400320 | tf_op jit(solution)/shard_map/entry/pallas_call | solution.py:417
  213.9 3.3 fusion.33
  220.0 4.0 mul.75
  224.6 3.4 fusion.9
  229.3 18.3 %scale.1 = (bf16[1568,2048]{1,0:T(8,128)(2,1)}, bf16[2048,1568]{1,0:T(8,128)(2,1)}) custom-call(bf16[1568,2304]{1,0:T(8,128)(2,1)} %get-tuple-element.44.mixed_ref, bf16[32,2304]{1,0:T(8,128)(2,1)} %get-tuple-element.77.gates_ref, bf16[1568,32]{1,0:T(8,128)(2,1)} %add_convert_fusion.spread_ref), custom_call_target="tpu_custom_call" | custom-call | flops 6576668672 | bytes 31457280 | tf_op jit(solution)/shard_map/scale/pallas_call | solution.py:997
  248.7 106.4 %exit.1 = (bf16[1568,2016]{1,0:T(8,128)(2,1)}, bf16[1568,2048]{1,0:T(8,128)(2,1)}, bf16[1568,2048]{1,0:T(8,128)(2,1)}, f32[128,2048]{1,0:T(8,128)}, f32[8,2,8,128]{3,2,1,0:T(8,128)}) custom-call(bf16[1568,2048]{1,0:T(8,128)(2,1)} %get-tuple-element.46.scaled_ref, bf16[2048,1568]{1,0:T(8,128)(2,1)} %get-tuple-element.47.turned_ref, ...), custom_call_target="tpu_custom_call" | custom-call | flops 26306674688 | bytes 73400320 | tf_op jit(solution)/shard_map/exit/pallas_call | solution.py:829
  355.1 30.5 %gate.1 = (f32[1568,2304]{1,0:T(8,128)}, f32[16,2304]{1,0:T(8,128)}) custom-call(bf16[1568,2048]{1,0:T(8,128)(2,1)} %get-tuple-element.49.delta_ref, bf16[2048,2048]{1,0:T(8,128)(2,1)} %all-gather.8.cloned.1.call-done.weight_ref, bf16[1568,2304]{1,0:T(8,128)(2,1)} %get-tuple-element.44.mixed_ref, bf16[16,1568]{1,0:T(8,128)(2,1)} %get-tuple-element.98.pool_ref), custom_call_target="tpu_custom_call" | custom-call | flops 14797504512 | bytes 41943040 | tf_op jit(solution)/shard_map/gate/pallas_call | solution.py:899
  388.3 4.5 convolution_convert_fusion
  398.3 3.1 reshape_reshape.27
  401.4 4.0 multiply_reduce_fusion
  408.3 4.7 convolution_convert_fusion.1
  413.9 150.3 %back.1 = (bf16[1568,2304]{1,0:T(8,128)(2,1)}, f32[128,2304]{1,0:T(8,128)}, bf16[9,2016,56]{2,1,0:T(8,128)(2,1)}, f32[9,2,8,128]{3,2,1,0:T(8,128)}, f32[24,128]{1,0:T(8,128)}) custom-call(f32[24,128]{1,0:T(8,128)} %fusion.34.bias_ref, f32[1568,2304]{1,0:T(8,128)} %get-tuple-element.51.grad_ref, f32[1568,2304]{1,0:T(8,128)} %get-tuple-element.52.group_ref.late_group_ref, ...), custom_call_target="tpu_custom_call" | custom-call | flops 48091889664 | bytes 94371840 | tf_op jit(solution)/shard_map/back/pallas_call | solution.py:1250
  568.4 5.4 reshape.308
  573.8 3.7 pad.109.clone
  577.5 3.5 copy.148
  581.0 56.3 %input.1 = (bf16[1568,2016]{1,0:T(8,128)(2,1)}, f32[5,2,128,128]{3,2,1,0:T(8,128)}) custom-call(bf16[1568,2304]{1,0:T(8,128)(2,1)} %get-tuple-element.57.delta_ref, bf16[2048,2304]{1,0:T(8,128)(2,1)} %bitcast.150, bf16[1568,2048]{1,0:T(8,128)(2,1)} %get-tuple-element.58.residual_ref, bf16[1568,128]{1,0:T(8,128)(2,1)} %broadcast_in_dim.82.live_ref, ...), custom_call_target="tpu_custom_call" | custom-call | flops 14797504512 | bytes 36700160 | tf_op jit(solution)/shard_map/input/pallas_call | solution.py:1609
  637.3 2.8 reshape.301
  656.1 6.9 %copy.155 = bf16[1,1568,2016]{2,1,0:T(8,128)(2,1)} copy(bf16[1,1568,2016]{2,1,0:T(8,128)(2,1)} %bitcast.110) | data formatting | bytes 12644352
  (193 shorter events, 61.8 us)
Async XLA Ops:
  7.2 7.7 %copy-start.10 = (s32[4,3]{1,0:T(4,128)S(1)}, s32[4,3]{1,0:T(4,128)}, u32[]{:S(2)}) copy-start(s32[4,3]{1,0:T(4,128)} %param.20) | copy-start | bytes 148
  7.2 8.3 %copy-start.17 = (f32[2016]{0:T(1024)S(1)}, f32[2016]{0:T(1024)}, u32[]{:S(2)}) copy-start(f32[2016]{0:T(1024)} %param.32) | copy-start | bytes 24196
  7.2 8.3 %copy-start.18 = (f32[2016]{0:T(1024)S(1)}, f32[2016]{0:T(1024)}, u32[]{:S(2)}) copy-start(f32[2016]{0:T(1024)} %param.33) | copy-start | bytes 24196
  7.2 8.3 %copy-start.13 = (f32[2016]{0:T(1024)S(1)}, f32[2016]{0:T(1024)}, u32[]{:S(2)}) copy-start(f32[2016]{0:T(1024)} %param.22) | copy-start | bytes 24196
  7.2 8.4 %copy-start.14 = (f32[2016]{0:T(1024)S(1)}, f32[2016]{0:T(1024)}, u32[]{:S(2)}) copy-start(f32[2016]{0:T(1024)} %param.23) | copy-start | bytes 24196
  7.2 8.5 %copy-start.15 = (f32[2016]{0:T(1024)S(1)}, f32[2016]{0:T(1024)}, u32[]{:S(2)}) copy-start(f32[2016]{0:T(1024)} %param.25) | copy-start | bytes 24196
  7.3 8.6 %copy-start.16 = (f32[2016]{0:T(1024)S(1)}, f32[2016]{0:T(1024)}, u32[]{:S(2)}) copy-start(f32[2016]{0:T(1024)} %param.26) | copy-start | bytes 24196
  7.3 8.7 %copy-start.4 = (bf16[63504]{0:T(1024)(128)(2,1)S(1)}, bf16[63504]{0:T(1024)(128)(2,1)}, u32[]{:S(2)}) copy-start(bf16[63504]{0:T(1024)(128)(2,1)} %param.24) | copy-start | bytes 381028
  7.3 10.0 %copy-start.2 = (bf16[254016]{0:T(1024)(128)(2,1)S(1)}, bf16[254016]{0:T(1024)(128)(2,1)}, u32[]{:S(2)}) copy-start(bf16[254016]{0:T(1024)(128)(2,1)} %param.21) | copy-start | bytes 1524100
  7.3 206.6 %all-gather.4.cloned.1.call-start = ((), (), s32[]{:S(2)}) async-start(), calls=%async_computation.2 | async-start | bytes 2228224 | tf_op jit(solution)/shard_map/all_gather | solution.py:1656
  9.3 215.3 %all-gather.6.cloned.1.call-start = ((), (), s32[]{:S(2)}) async-start(), calls=%async_computation.3 | async-start | bytes 2228224 | tf_op jit(solution)/shard_map/all_gather | solution.py:1656
  11.4 236.3 %all-gather.8.cloned.1.call-start = ((), (), s32[]{:S(2)}) async-start(), calls=%async_computation.4 | async-start | bytes 8912896 | tf_op jit(solution)/shard_map/all_gather | solution.py:1656
  14.0 632.4 %reduce-scatter.5.cloned.1.call-start = ((), (), s32[]{:S(2)}) async-start(), calls=%async_computation.6 | async-start | bytes 2228224 | tf_op jit(solution)/shard_map/reduce_scatter | solution.py:1663
  132.6 81.3 %copy-start.22 = (f32[504]{0:T(512)S(1)}, f32[504]{0:T(512)}, u32[]{:S(2)}) copy-start(f32[504]{0:T(512)} %param.28) | copy-start | bytes 6052
  209.2 8.0 %copy-start.8 = (f32[4,4]{0,1:T(4,128)}, f32[4,4]{0,1:T(4,128)S(1)}, u32[]{:S(2)}) copy-start(f32[4,4]{0,1:T(4,128)S(1)} %fusion.42) | copy-start | bytes 196
  229.3 18.3 %copy-start.11 = (bf16[1568]{0:T(1024)(128)(2,1)S(1)}, bf16[1568]{0:T(1024)(128)(2,1)}, u32[]{:S(2)}) copy-start(bf16[1568]{0:T(1024)(128)(2,1)} %fusion.43) | copy-start | bytes 9412
  355.0 31.4 %copy-start.21 = (pred[16]{0:T(512)(128)(4,1)S(1)}, pred[16]{0:T(512)(128)(4,1)}, u32[]{:S(2)}) copy-start(pred[16]{0:T(512)(128)(4,1)} %iota_compare_fusion.7) | copy-start | bytes 52
  392.8 256.3 %reduce-scatter.3.cloned.1.call-start = ((), (), s32[]{:S(2)}) async-start(), calls=%async_computation.5 | async-start | bytes 2228224 | tf_op jit(solution)/shard_map/reduce_scatter | solution.py:1663
  413.8 150.3 %copy-start.12 = (f32[8,2,8,128]{3,2,1,0:T(8,128)S(1)}, f32[8,2,8,128]{3,2,1,0:T(8,128)}, u32[]{:S(2)}) copy-start(f32[8,2,8,128]{3,2,1,0:T(8,128)} %get-tuple-element.63) | copy-start | bytes 196612
  413.9 151.7 %copy-start.20 = (pred[2016]{0:T(1024)(128)(4,1)S(1)}, pred[2016]{0:T(1024)(128)(4,1)}, u32[]{:S(2)}) copy-start(pred[2016]{0:T(1024)(128)(4,1)} %constant.62.clone.1) | copy-start | bytes 6052
  566.5 79.9 %collective-permute-start = (f32[8,2016]{1,0:T(8,128)S(1)}, f32[8,2016]{1,0:T(8,128)S(1)}, u32[]{:S(2)}, u32[]{:S(2)}) collective-permute-start(f32[8,2016]{1,0:T(8,128)S(1)} %concatenate.30), channel_id=1, source_target_pairs={{0,16},{16,0},{1,17},{17,1},{2,18},{18,2},{3,19},{19,3},{4,20},{20... | collective-permute-start | bytes 193544 | tf_op jit(solution)/shard_map/ppermute | solution.py:1671
  581.0 59.1 %copy-start.1 = (f32[128,2304]{1,0:T(8,128)S(1)}, f32[128,2304]{1,0:T(8,128)}, u32[]{:S(2)}) copy-start(f32[128,2304]{1,0:T(8,128)} %get-tuple-element.61) | copy-start | bytes 3538948
  646.4 5.2 collective-permute-start.2
  649.1 5.2 collective-permute-start.1
  (9 other events, 54.6 us)
Sparse Core Ops, SparseCore 0:
  10.9 68.6 all-gather.3
  82.3 43.4 all-gather.5
  128.5 92.5 all-gather.7
  393.0 62.5 reduce-scatter.4
  460.1 72.0 reduce-scatter.2

commit v3 on v2

--- a/solution.py
+++ b/solution.py
@@ -473,7 +473,8 @@
 
 
 class Reducer:
-    def __init__(self, refs):
+    def __init__(self, refs, inside, rest=None):
+        self.inside, self.rest = inside, rest
         (
             self.local,
             self.core_got,
@@ -486,6 +487,7 @@
             self.plane_sem,
             self.z_sem,
             self.y_sem,
+            self.local_sem,
         ) = refs
         self.stream, self.z, self.x, self.core = place()
         self.mine = pl.ds(pl.multiple_of(64 * self.stream, 64), 64)
@@ -505,9 +507,10 @@
             pltpu.SemaphoreType.DMA((2, 2, 3)),
             pltpu.SemaphoreType.DMA((2, 2, 3)),
             pltpu.SemaphoreType.DMA((2, 2)),
+            pltpu.SemaphoreType.DMA((2,)),
         ]
 
-    COUNT = 11
+    SHAPE = (2, 2, 4, 2, 128, 128)
 
     def index(self, k=0, across=0, beside=0):
         return 4 * (self.z ^ k) + 2 * (self.x ^ across) + (self.core ^ beside)
@@ -614,9 +617,19 @@
         for peer in range(3):
             self.plane_copy(block, peer).start()
 
-    def advance(self, newest, blocks, put):
+    def rest_copy(self, block):
+        hold = lax.rem(block, 2)
+        return pltpu.make_async_copy(
+            self.local.at[hold], self.rest.at[block - self.inside], self.local_sem.at[hold]
+        )
+
+    def load_copy(self, source, at, block):
+        hold = lax.rem(block, 2)
+        return pltpu.make_async_copy(source.at[at], self.local.at[hold], self.local_sem.at[hold])
+
+    def advance(self, newest, put, blocks=0):
         def live(block):
-            return (block >= 0) & (block < blocks)
+            return (block >= 0) & (block < self.inside)
 
         @pl.when(live(newest - 4))
         def _():
@@ -633,6 +646,12 @@
         @pl.when(live(newest - 1))
         def _():
             self.after_core(newest - 1)
+
+        if self.rest is not None:
+
+            @pl.when((newest > self.inside) & (newest <= blocks))
+            def _():
+                self.rest_copy(newest - 1).wait()
 
     def begin(self, block, grad):
         hold = lax.rem(block, 2)
@@ -642,7 +661,63 @@
                 self.local[hold, core, x, z, tile] = grad[
                     128 * chunk : 128 * chunk + 128, 128 * tile : 128 * tile + 128
                 ].astype(bf16)
-        self.core_copy(block).start()
+
+        @pl.when(block < self.inside)
+        def _():
+            self.core_copy(block).start()
+
+        if self.rest is not None:
+
+            @pl.when(block >= self.inside)
+            def _():
+                self.rest_copy(block).start()
+
+    def neighbours(self):
+        barrier = pltpu.get_barrier_semaphore()
+        greeted = self.greet(barrier)
+        peers = [(0, 0, 1), (0, 1, 0), (1, 0, 0), (2, 0, 0), (3, 0, 0)]
+        for peer in peers:
+            pl.semaphore_signal(
+                barrier, inc=1, device_id=(self.stream, self.index(*peer)), device_id_type=MESH
+            )
+        pl.semaphore_wait(barrier, len(peers) + greeted)
+
+
+def feed(reducer, step, sources, part_out):
+    starts = []
+    total = 0
+    for source, count in sources:
+        starts.append((source, total, total + count))
+        total += count
+
+    def start_load(block):
+        for source, first, last in starts:
+
+            @pl.when((block >= first) & (block < last))
+            def _():
+                reducer.load_copy(source, block - first, block).start()
+
+    @pl.when(step == 0)
+    def _():
+        start_load(step)
+        reducer.neighbours()
+
+    def put(tile, rows, values):
+        part_out[step - 4, tile, rows] = values
+
+    reducer.advance(step, put)
+
+    @pl.when(step < total)
+    def _():
+        reducer.load_copy(sources[0][0], 0, step).wait()
+        reducer.core_copy(step).start()
+
+    start_load(step + 1)
+
+
+BACK_INSIDE = 6
+BACK_REST = BLOCKS - BACK_INSIDE
+CONV_BLOCKS = 3
 
 
 def whole(shape):
@@ -683,7 +758,6 @@
     recv_sem,
     pair_send,
     pair_recv,
-    *reduce_refs,
 ):
     step = pl.program_id(0)
     count = row_count(size)
@@ -691,7 +765,10 @@
     me = lax.axis_index("img")
     area = jnp.where(stream == 0, GLOBAL_SIDE**2, SMALL_SIDE**2).astype(f32)
     blocks = OUT_BLOCKS
-    reducer = Reducer(reduce_refs) if reduce_refs else None
+
+    def used_lanes(block):
+        lane = lax.broadcasted_iota(jnp.int32, (STEP, 128), 1) + LANES * block
+        return [lane + 128 * tile < CHANNELS for tile in range(2)]
 
     def pair_copy(block):
         return pltpu.make_async_remote_copy(
@@ -709,14 +786,7 @@
         pl.semaphore_signal(
             barrier, inc=1, device_id=(1 - stream, me), device_id_type=MESH
         )
-        pl.semaphore_wait(barrier, size + (reducer.greet(barrier) if reducer else 0))
-
-    if reducer:
-
-        def put(tile, rows, values):
-            weight_out[rows, 128 * tile : 128 * tile + 128] = values
-
-        reducer.advance(step - 3, blocks, put)
+        pl.semaphore_wait(barrier, size)
 
     @pl.when(step < blocks)
     def _():
@@ -738,6 +808,7 @@
         total = take_sums(size, block, got, send_sem, recv_sem)
         total_out[block, 0] = total
         param = param_ref[block]
+        inside = used_lanes(block)
         for micro in range(MICRO_BATCHES):
             for tile in range(2):
                 lanes = slice(128 * tile, 128 * tile + 128)
@@ -747,7 +818,8 @@
                 for chunk in range(HALF_STEPS * micro, HALF_STEPS * (micro + 1)):
                     here = chunk_rows(chunk)
                     act = act_ref[slot, here, lanes]
-                    half = 0.5 * x_ref[here, lanes].astype(f32) + (act * scale + shift)
+                    source = jnp.where(inside[tile], x_ref[here, lanes].astype(f32), 0.0)
+                    half = 0.5 * source + (act * scale + shift)
                     bent = jnp.tanh(half)
                     out_out[here, lanes] = (
                         (half + half * bent) * live_ref[here].astype(f32)
@@ -773,14 +845,17 @@
             for micro in range(MICRO_BATCHES)
             for tile in range(2)
         }
+        inside = used_lanes(block)
         sums = Sums()
         for chunk in range(STEPS):
             here = chunk_rows(chunk)
+            live = live_ref[here].astype(f32)
             pull = dot(spread_ref[here], partner) * (PAIR_SCALE / area)
             for tile in range(2):
                 lanes = slice(128 * tile, 128 * tile + 128)
                 mean, inverse = means[chunk // HALF_STEPS, tile]
-                upstream = cot_ref[here, lanes].astype(f32) + pull[:, lanes]
+                upstream = jnp.where(inside[tile], cot_ref[here, lanes].astype(f32), 0.0)
+                upstream = upstream * live + pull[:, lanes]
                 delta = upstream * slope_ref[hold, here, lanes]
                 slope_ref[hold, here, lanes] = delta
                 residual_out[here, lanes] = delta.astype(bf16)
@@ -788,7 +863,7 @@
                 sums.add(chunk // HALF_STEPS, tile, delta, delta * normed)
         send_sums(size, blocks + block, sums.packed(), sent, got, send_sem, recv_sem)
 
-    @pl.when((step >= 3) & (step < blocks + 3))
+    @pl.when(step >= 3)
     def _():
         block = step - 3
         slot = lax.rem(block, 4)
@@ -806,11 +881,7 @@
                     delta_out[here, lanes] = back(
                         slope_ref[hold, here, lanes], act_ref[slot, here, lanes]
                     ).astype(bf16)
-        grad = dot(turned_ref[...], delta_out[...])
-        if reducer:
-            reducer.begin(block, grad)
-        else:
-            weight_out[...] = grad.astype(bf16)
+        weight_out[...] = dot(turned_ref[...], delta_out[...]).astype(bf16)
 
 
 def norm_back(moment, total, micro, tile, gain, count):
@@ -825,17 +896,14 @@
 
 def run_exit(size, scaled, turned, weight, x, cot, params, pair, spread, live):
     blocks = OUT_BLOCKS
-    reduced = size == SHARDS
     return pl.pallas_call(
         functools.partial(exit_kernel, size),
-        grid=(blocks + (7 if reduced else 3),),
+        grid=(blocks + 3,),
         out_shape=(
             jax.ShapeDtypeStruct((ROWS, CHANNELS), bf16),
             jax.ShapeDtypeStruct((ROWS, PADDED), bf16),
             jax.ShapeDtypeStruct((ROWS, PADDED), bf16),
-            jax.ShapeDtypeStruct((CHUNK_PAD, PADDED), f32)
-            if reduced
-            else jax.ShapeDtypeStruct((PADDED, PADDED), bf16),
+            jax.ShapeDtypeStruct((PADDED, PADDED), bf16),
             jax.ShapeDtypeStruct((blocks, 2, 8, 128), f32),
         ),
         in_specs=[
@@ -853,7 +921,7 @@
             columns(ROWS, 1, blocks),
             columns(ROWS, 3, blocks),
             columns(ROWS, 2, blocks),
-            columns(CHUNK_PAD, 7, blocks) if reduced else columns(PADDED, 3, blocks),
+            columns(PADDED, 3, blocks),
             pl.BlockSpec((blocks, 2, 8, 128), lambda i: (0, 0, 0, 0)),
         ),
         scratch_shapes=[
@@ -867,8 +935,7 @@
             pltpu.SemaphoreType.DMA((2 * blocks,)),
             pltpu.SemaphoreType.DMA((blocks,)),
             pltpu.SemaphoreType.DMA((blocks,)),
-        ]
-        + (Reducer.scratch() if reduced else []),
+        ],
         name="exit",
         compiler_params=pltpu.CompilerParams(
             collective_id=2, has_side_effects=True, vmem_limit_bytes=VMEM_LIMIT
@@ -960,14 +1027,114 @@
     )(x)
 
 
-def scale_kernel(mixed_ref, gates_ref, spread_ref, scaled_out, turned_out, scaled):
+QUARTERS = CHANNELS // SQUEEZE
+INNER = 512
+
+
+def split(values):
+    high = values.astype(bf16)
+    low = (values - high.astype(f32)).astype(bf16)
+    return jnp.concatenate([high, low], axis=-2)
+
+
+def join(terms):
+    half = terms.shape[0] // 2
+    return terms[:half] + terms[half:]
+
+
+def wide_place(channel):
+    return channel + (LANES - BLOCK) * (channel // BLOCK)
+
+
+def pair_source(pair):
+    return min(128 * (wide_place(PAIR * pair) // 128), WIDE - 512)
+
+
+def pair_from_wide(pair, shape, dim):
+    inside = pair_lane(shape, dim)
+    where = wide_place(PAIR * pair + inside) - pair_source(pair)
+    there = lax.broadcasted_iota(jnp.int32, shape, 1 - dim)
+    return one_hot((there == where) & (inside >= 0))
+
+
+def inner_source(pair):
+    return min(128 * ((PAIR // QUARTERS) * pair // 128), INNER - LANES)
+
+
+def pair_from_inner(pair, quarter):
+    shape = (LANES, LANES)
+    inside = pair_lane(shape, 1)
+    inner = lax.broadcasted_iota(jnp.int32, shape, 0) + inner_source(pair)
+    return one_hot((PAIR * pair + inside == QUARTERS * inner + quarter) & (inside >= 0))
+
+
+def quarters_of(block):
+    first = BLOCK * block // SQUEEZE
+    last = (BLOCK * block + BLOCK - 1) // SQUEEZE
+    return range(first, last + 1)
+
+
+def scale_kernel(
+    mixed_ref,
+    spread_ref,
+    pooled_ref,
+    squeeze_ref,
+    excite_ref,
+    squeeze_bias_ref,
+    excite_bias_ref,
+    scaled_out,
+    turned_out,
+    gates_out,
+    pooled_out,
+    inner_out,
+    rows_out,
+    quarter_out,
+    scaled,
+):
     step = pl.program_id(0)
+    area = jnp.where(lax.axis_index("stream") == 0, GLOBAL_SIDE**2, SMALL_SIDE**2).astype(f32)
+
+    @pl.when(step == 0)
+    def _():
+        for pair in range(OUT_BLOCKS):
+            lanes = slice(pair_source(pair), pair_source(pair) + 512)
+            pick = pair_from_wide(pair, (512, LANES), 1)
+            picked = join(dot(split(pooled_ref[:, lanes]), pick)) / area
+            pooled_out[:, LANES * pair : LANES * (pair + 1)] = picked
+        inner = join(dot(split(pooled_out[...]), squeeze_ref[...])) + squeeze_bias_ref[...]
+        inner_out[...] = inner
+        half = 0.5 * inner
+        terms = split(half + half * jnp.tanh(half))
+        for pair in range(OUT_BLOCKS):
+            source = terms[:, inner_source(pair) : inner_source(pair) + LANES]
+            for quarter in range(QUARTERS):
+                rows_out[
+                    CROPS * quarter : CROPS * (quarter + 1), LANES * pair : LANES * (pair + 1)
+                ] = join(dot(source, pair_from_inner(pair, quarter)))
+        excite = join(dot(split(rows_out[...]), excite_ref[...]))
+        for quarter in range(QUARTERS):
+            here = slice(CROPS * quarter, CROPS * (quarter + 1))
+            half = 0.5 * (excite[here] + excite_bias_ref[quarter : quarter + 1])
+            quarter_out[here] = 0.5 + 0.5 * jnp.tanh(half)
+        for block in range(BLOCKS):
+            total = 0.0
+            for quarter in quarters_of(block):
+                shape = (INNER, LANES)
+                channel = SQUEEZE * quarter + lax.broadcasted_iota(jnp.int32, shape, 0)
+                lane = lax.broadcasted_iota(jnp.int32, shape, 1)
+                inside = lax.broadcasted_iota(jnp.int32, shape, 0) < SQUEEZE
+                pick = one_hot((channel == BLOCK * block + lane) & (lane < BLOCK) & inside)
+                here = slice(CROPS * quarter, CROPS * (quarter + 1))
+                total = total + dot(split(quarter_out[here]), pick)
+            gates_out[:, LANES * block : LANES * (block + 1)] = total.astype(bf16)
 
     @pl.when(step < BLOCKS)
     def _():
-        gate = dot(spread_ref[...], gates_ref[...])
         lanes = pl.ds(pl.multiple_of(LANES * step, LANES), LANES)
-        scaled[:, lanes] = (mixed_ref[...].astype(f32) * gate).astype(bf16)
+        for chunk in range(STEPS):
+            here = chunk_rows(chunk)
+            gate = dot(spread_ref[here], gates_out[:, lanes])
+            scaled[here, lanes] = (mixed_ref[here].astype(f32) * gate).astype(bf16)
 
     @pl.when(step >= BLOCKS)
     def _():
@@ -990,36 +1157,147 @@
         )
 
 
-def run_scale(mixed, gates, spread):
+def run_scale(mixed, spread, pooled, squeeze, excite, squeeze_bias, excite_bias):
     def pair(i):
         return jnp.maximum(i - BLOCKS, 0)
 
+    def kept(shape):
+        return pl.BlockSpec(shape, lambda i: (0, 0))
+
+    kinds = (
+        ((2 * CROPS, WIDE), bf16),
+        ((CROPS, PADDED), f32),
+        ((CROPS, INNER), f32),
+        ((QUARTERS * CROPS, PADDED), f32),
+        ((QUARTERS * CROPS, INNER), f32),
+    )
     return pl.pallas_call(
         scale_kernel,
         grid=(BLOCKS + OUT_BLOCKS,),
         out_shape=(
             jax.ShapeDtypeStruct((ROWS, PADDED), bf16),
             jax.ShapeDtypeStruct((PADDED, ROWS), bf16),
-        ),
+        )
+        + tuple(jax.ShapeDtypeStruct(*kind) for kind in kinds),
         in_specs=[
             columns(ROWS, 0, BLOCKS),
-            columns(2 * CROPS, 0, BLOCKS),
             whole((ROWS, 2 * CROPS)),
+            whole((CROPS, WIDE)),
+            whole((PADDED, INNER)),
+            whole((PADDED, INNER)),
+            whole((1, INNER)),
+            whole((QUARTERS, INNER)),
         ],
         out_specs=(
             pl.BlockSpec((ROWS, LANES), lambda i: (0, pair(i))),
             pl.BlockSpec((LANES, ROWS), lambda i: (pair(i), 0)),
-        ),
+        )
+        + tuple(kept(shape) for shape, _ in kinds),
         scratch_shapes=[pltpu.VMEM((ROWS, WIDE), bf16)],
         name="scale",
         compiler_params=pltpu.CompilerParams(vmem_limit_bytes=VMEM_LIMIT),
         cost_estimate=pl.CostEstimate(
             flops=4 * ROWS * 512 * PADDED, bytes_accessed=30 * 2**20, transcendentals=0
         ),
-    )(mixed, gates, spread)
-
-
-BIAS_ROWS = 24
+    )(mixed, spread, pooled, squeeze, excite, squeeze_bias, excite_bias)
+
+
+def outer(left, right):
+    left_high = left.astype(bf16)
+    left_low = (left - left_high.astype(f32)).astype(bf16)
+    right_high = right.astype(bf16)
+    right_low = (right - right_high.astype(f32)).astype(bf16)
+    left = jnp.concatenate([left_high, left_high, left_low])
+    right = jnp.concatenate([right_high, right_low, right_high])
+    return dot(left, right, ((0,), (0,)))
+
+
+def squeeze_kernel(
+    gate_grad_ref,
+    pooled_ref,
+    inner_ref,
+    rows_ref,
+    quarter_ref,
+    squeeze_ref,
+    excite_ref,
+    gates_out,
+    grads_out,
+    bias_out,
+    quarter_delta,
+    inner_delta,
+    pooled_delta,
+):
+    area = jnp.where(lax.axis_index("stream") == 0, GLOBAL_SIDE**2, SMALL_SIDE**2).astype(f32)
+    bias_out[...] = jnp.zeros_like(bias_out)
+    for quarter in range(QUARTERS):
+        first = min(LANES * (SQUEEZE * quarter // BLOCK), WIDE - 1024)
+        shape = (1024, INNER)
+        inner = lax.broadcasted_iota(jnp.int32, shape, 1)
+        where = wide_place(SQUEEZE * quarter + inner) - first
+        there = lax.broadcasted_iota(jnp.int32, shape, 0)
+        pick = one_hot((there == where) & (inner < SQUEEZE))
+        grad = join(dot(split(gate_grad_ref[:, first : first + 1024]), pick))
+        here = slice(CROPS * quarter, CROPS * (quarter + 1))
+        gate = quarter_ref[here]
+        delta = grad * gate * (1.0 - gate)
+        quarter_delta[here] = delta
+        bias_out[1 + quarter : 2 + quarter] = column_sum(delta)
+    back = join(dot(split(quarter_delta[...]), excite_ref[...], ((1,), (1,))))
+    inner_delta[...] = jnp.zeros_like(inner_delta)
+    for pair in range(OUT_BLOCKS):
+        lanes = slice(inner_source(pair), inner_source(pair) + LANES)
+        total = 0.0
+        for quarter in range(QUARTERS):
+            terms = split(
+                back[CROPS * quarter : CROPS * (quarter + 1), LANES * pair : LANES * (pair + 1)]
+            )
+            total = total + dot(terms, pair_from_inner(pair, quarter), ((1,), (1,)))
+        inner_delta[:, lanes] += join(total)
+    half = 0.5 * inner_ref[...]
+    bent = jnp.tanh(half)
+    delta = inner_delta[...] * ((0.5 + 0.5 * bent) * (1.0 + half * (1.0 - bent)))
+    bias_out[0:1] = column_sum(delta)
+    pooled_delta[...] = join(dot(split(delta), squeeze_ref[...], ((1,), (1,)))) / area
+    for block in range(BLOCKS):
+        first = min(BLOCK * block // CHUNK, SHARDS - 3)
+        shape = (3 * CHUNK_PAD, LANES)
+        place_in = lax.broadcasted_iota(jnp.int32, shape, 0)
+        lane = lax.broadcasted_iota(jnp.int32, shape, 1)
+        channel = CHUNK * (first + place_in // CHUNK_PAD) + place_in % CHUNK_PAD
+        pick = (channel == BLOCK * block + lane) & (lane < BLOCK) & (place_in % CHUNK_PAD < CHUNK)
+        source = pooled_delta[:, CHUNK_PAD * first : CHUNK_PAD * (first + 3)]
+        gates_out[:, LANES * block : LANES * (block + 1)] = dot(
+            split(source), one_hot(pick)
+        ).astype(bf16)
+    grads_out[:, INNER:] = outer(rows_ref[...], quarter_delta[...]).astype(bf16)
+    grads_out[:, :INNER] = outer(pooled_ref[...], delta).astype(bf16)
+
+
+def run_squeeze(gate_grad, pooled, inner, rows, quarter, squeeze, excite):
+    vmem = pl.BlockSpec(memory_space=pltpu.VMEM)
+    return pl.pallas_call(
+        squeeze_kernel,
+        out_shape=(
+            jax.ShapeDtypeStruct((2 * CROPS, WIDE), bf16),
+            jax.ShapeDtypeStruct((PADDED, 2 * INNER), bf16),
+            jax.ShapeDtypeStruct((8, INNER), f32),
+        ),
+        in_specs=[vmem] * 7,
+        out_specs=(vmem,) * 3,
+        scratch_shapes=[
+            pltpu.VMEM((QUARTERS * CROPS, INNER), f32),
+            pltpu.VMEM((CROPS, INNER), f32),
+            pltpu.VMEM((CROPS, PADDED), f32),
+        ],
+        name="squeeze",
+        compiler_params=pltpu.CompilerParams(vmem_limit_bytes=VMEM_LIMIT),
+        cost_estimate=pl.CostEstimate(
+            flops=2 * 2**30, bytes_accessed=20 * 2**20, transcendentals=0
+        ),
+    )(gate_grad, pooled, inner, rows, quarter, squeeze, excite)
+
+
+BIAS_ROWS = 32
 
 
 def back_kernel(
@@ -1029,6 +1307,7 @@
     group_ref,
     late_group_ref,
     gates_ref,
+    pooled_ref,
     spread_ref,
     act_ref,
     late_act_ref,
@@ -1044,6 +1323,11 @@
     conv_out,
     total_out,
     bias_out,
+    *refs,
+):
+    if size == SHARDS:
+        rest_out, *refs = refs
+    (
     delta_two,
     delta_one,
     pads,
@@ -1056,12 +1340,14 @@
     send_sem,
     recv_sem,
     bias_sem,
+    even_ref,
+    odd_ref,
     *reduce_refs,
-):
+    ) = refs
     step = pl.program_id(0)
     count = row_count(size)
     on_global = lax.axis_index("stream") == 0
-    reducer = Reducer(reduce_refs) if reduce_refs else None
+    reducer = Reducer(reduce_refs, BACK_INSIDE, rest_out) if reduce_refs else None
 
     def bend(moment, micro, tile, param, at):
         mean, inverse = moments(moment, micro, tile, count)
@@ -1116,7 +1402,7 @@
         def put(tile, rows, values):
             weight_out[rows, 128 * tile : 128 * tile + 128] = values
 
-        reducer.advance(step - 2, BLOCKS, put)
+        reducer.advance(step - 2, put, BLOCKS)
 
     @pl.when(step < BLOCKS)
     def _():
@@ -1128,8 +1414,8 @@
             bends = [bend(moment, micro, tile, param, 4) for tile in range(2)]
             for chunk in range(HALF_STEPS * micro, HALF_STEPS * (micro + 1)):
                 here = chunk_rows(chunk)
-                gate = dot(spread_ref[here], gates_ref[0])
-                pooled = dot(spread_ref[here], gates_ref[1])
+                gate = dot(spread_ref[here], gates_ref[...])
+                pooled = dot(spread_ref[here], pooled_ref[...])
                 for tile in range(2):
                     lanes = slice(128 * tile, 128 * tile + 128)
                     normed, slope = bends[tile](group_ref[here, lanes])
@@ -1217,7 +1503,11 @@
             for group in range(4):
                 here = slice(GROUP_WIDTH * group, GROUP_WIDTH * (group + 1))
                 pieces.append(grad[here, here])
-            conv_out[offset] = jnp.concatenate(pieces).astype(bf16)
+            even_ref[:, :GROUP_WIDTH] = jnp.concatenate(pieces)
+            lines = [even_ref[pl.ds(start, BLOCK // 2, 2), :GROUP_WIDTH] for start in range(2)]
+            odd_ref[:, :GROUP_WIDTH] = lines[0]
+            odd_ref[:, GROUP_WIDTH : 2 * GROUP_WIDTH] = lines[1]
+            conv_out[offset] = odd_ref[:, : 2 * GROUP_WIDTH].astype(bf16)
 
     @pl.when((step >= 2) & (step < BLOCKS + 2))
     def _():
@@ -1244,27 +1534,29 @@
 
 
 def run_back(
-    size, bias, grad, group, gates, spread, act, turned, conv, x_turned, params, moment, edges, fold
+    size, bias, grad, group, gates, pooled, spread, act, turned, conv, x_turned, params, moment, edges, fold
 ):
     reduced = size == SHARDS
     return pl.pallas_call(
         functools.partial(back_kernel, size),
-        grid=(BLOCKS + (6 if reduced else 2),),
+        grid=(max(BLOCKS + 2, BACK_INSIDE + 6) if reduced else BLOCKS + 2,),
         out_shape=(
             jax.ShapeDtypeStruct((ROWS, WIDE), bf16),
-            jax.ShapeDtypeStruct((CHUNK_PAD, WIDE), f32)
+            jax.ShapeDtypeStruct((CHUNK_PAD, LANES * BACK_INSIDE), f32)
             if reduced
             else jax.ShapeDtypeStruct((PADDED, WIDE), bf16),
-            jax.ShapeDtypeStruct((9, CHANNELS, GROUP_WIDTH), bf16),
+            jax.ShapeDtypeStruct((9, CHANNELS // 2, 2 * GROUP_WIDTH), bf16),
             jax.ShapeDtypeStruct((BLOCKS, 2, 8, 128), f32),
             jax.ShapeDtypeStruct((BIAS_ROWS, 128), f32),
-        ),
+        )
+        + ((jax.ShapeDtypeStruct((BACK_REST,) + Reducer.SHAPE, bf16),) if reduced else ()),
         in_specs=[
             whole((BIAS_ROWS, 128)),
             columns(ROWS, 0, BLOCKS),
             columns(ROWS, 0, BLOCKS),
             columns(ROWS, 1, BLOCKS),
-            pl.BlockSpec((2, 2 * CROPS, LANES), lambda i: (0, 0, jnp.clip(i, 0, BLOCKS - 1))),
+            columns(2 * CROPS, 0, BLOCKS),
+            columns(2 * CROPS, 0, BLOCKS),
             whole((ROWS, 2 * CROPS)),
             columns(ROWS, 1, BLOCKS),
             columns(ROWS, 2, BLOCKS),
@@ -1278,11 +1570,14 @@
         ],
         out_specs=(
             columns(ROWS, 2, BLOCKS),
-            columns(CHUNK_PAD, 6, BLOCKS) if reduced else columns(PADDED, 2, BLOCKS),
-            pl.BlockSpec((9, BLOCK, GROUP_WIDTH), lambda i: (0, jnp.clip(i - 1, 0, BLOCKS - 1), 0)),
+            columns(CHUNK_PAD, 6, BACK_INSIDE) if reduced else columns(PADDED, 2, BLOCKS),
+            pl.BlockSpec(
+                (9, BLOCK // 2, 2 * GROUP_WIDTH), lambda i: (0, jnp.clip(i - 1, 0, BLOCKS - 1), 0)
+            ),
             pl.BlockSpec((BLOCKS, 2, 8, 128), lambda i: (0, 0, 0, 0)),
             pl.BlockSpec((BIAS_ROWS, 128), lambda i: (0, 0)),
-        ),
+        )
+        + ((pl.BlockSpec(memory_space=HBM),) if reduced else ()),
         scratch_shapes=[
             pltpu.VMEM((2, 2, ROWS, 128), f32),
             pltpu.VMEM((2, 2, ROWS, 128), f32),
@@ -1296,6 +1591,8 @@
             pltpu.SemaphoreType.DMA((2 * BLOCKS,)),
             pltpu.SemaphoreType.DMA((2 * BLOCKS,)),
             pltpu.SemaphoreType.DMA((2,)),
+            pltpu.VMEM((BLOCK, 128), f32),
+            pltpu.VMEM((BLOCK // 2, 128), f32),
         ]
         + (Reducer.scratch() if reduced else []),
         name="back",
@@ -1307,7 +1604,7 @@
             bytes_accessed=90 * 2**20,
             transcendentals=2 * ROWS * WIDE,
         ),
-    )(bias, grad, group, group, gates, spread, act, act, turned, conv, x_turned, params, moment, edges, fold)
+    )(bias, grad, group, group, gates, pooled, spread, act, act, turned, conv, x_turned, params, moment, edges, fold)
 
 
 CONV_LINES = 1152
@@ -1317,6 +1614,8 @@
     entry_ref,
     conv_ref,
     x_ref,
+    live_ref,
+    lane_ref,
     entry_out,
     conv_out,
     chunk_out,
@@ -1398,16 +1697,21 @@
         if pair >= 2:
             for copy in stores[pair - 2]:
                 copy.wait()
-        depth = 384
         first = (PAIR * pair) // 128
+        depth = min(384, CHANNELS - 128 * first)
         source = 128 * first - PAIR * pair
         values = x_rows[:, 128 * first : 128 * first + depth]
         there = lax.broadcasted_iota(jnp.int32, (depth, LANES), 0) + source
         pick = one_hot(there == pair_lane((depth, LANES), 1))
-        chunk_rows_ref[slot] = dot(values, pick).astype(bf16)
+        picked = dot(values, pick)
+        for tile in range(2):
+            lanes = slice(128 * tile, 128 * tile + 128)
+            chunk_rows_ref[slot, :, lanes] = (
+                picked[:, lanes] * live_ref[...].astype(f32)
+            ).astype(bf16)
         there = lax.broadcasted_iota(jnp.int32, (LANES, depth), 1) + source
         pick = one_hot(there == pair_lane((LANES, depth), 0))
-        turned_rows[slot] = dot(pick, values, ((1,), (1,))).astype(bf16)
+        turned_rows[slot] = (dot(pick, values, ((1,), (1,))) * lane_ref[...]).astype(bf16)
         lanes = slice(LANES * pair, LANES * (pair + 1))
         copies = (
             pltpu.make_async_copy(chunk_rows_ref.at[slot], chunk_out.at[:, lanes], store_sem.at[0, pair]),
@@ -1491,7 +1795,7 @@
             copy.wait()
 
 
-def run_gather(entry, conv, x):
+def run_gather(entry, conv, x, live, lane):
     return pl.pallas_call(
         gather_kernel,
         out_shape=(
@@ -1500,10 +1804,11 @@
             jax.ShapeDtypeStruct((ROWS, PADDED), bf16),
             jax.ShapeDtypeStruct((PADDED, ROWS), bf16),
         ),
-        in_specs=[pl.BlockSpec(memory_space=HBM)] * 3,
+        in_specs=[pl.BlockSpec(memory_space=HBM)] * 3
+        + [pl.BlockSpec(memory_space=pltpu.VMEM)] * 2,
         out_specs=(pl.BlockSpec(memory_space=HBM),) * 4,
         scratch_shapes=[
-            pltpu.VMEM((ROWS, PADDED), bf16),
+            pltpu.VMEM((ROWS, CHANNELS), bf16),
             pltpu.VMEM((2, ROWS, LANES), bf16),
             pltpu.VMEM((2, LANES, ROWS), bf16),
             pltpu.SemaphoreType.DMA((2, 35)),
@@ -1518,10 +1823,7 @@
         cost_estimate=pl.CostEstimate(
             flops=4 * ROWS * 384 * PADDED, bytes_accessed=200 * 2**20, transcendentals=0
         ),
-    )(entry, conv, x)
-
-
-CONV_BLOCKS = 5
+    )(entry, conv, x, live, lane)
 
 
 def input_kernel(delta_ref, weight_ref, residual_ref, live_ref, *refs):
@@ -1529,43 +1831,9 @@
     if len(refs) == 1:
         (grad_out,) = refs
     else:
-        conv_ref, grad_out, conv_out, load_sem, *reduce_refs = refs
-        reducer = Reducer(reduce_refs)
-
-        def load(at):
-            hold = lax.rem(at, 2)
-            return pltpu.make_async_copy(
-                conv_ref.at[at], reducer.local.at[hold], load_sem.at[hold]
-            )
-
-        @pl.when(block == 0)
-        def _():
-            load(0).start()
-            barrier = pltpu.get_barrier_semaphore()
-            greeted = reducer.greet(barrier)
-            peers = [(0, 0, 1), (0, 1, 0), (1, 0, 0), (2, 0, 0), (3, 0, 0)]
-            for peer in peers:
-                pl.semaphore_signal(
-                    barrier,
-                    inc=1,
-                    device_id=(reducer.stream, reducer.index(*peer)),
-                    device_id_type=MESH,
-                )
-            pl.semaphore_wait(barrier, len(peers) + greeted)
-
-        def put(tile, rows, values):
-            conv_out[block - 4, tile, rows] = values
-
-        reducer.advance(block, CONV_BLOCKS, put)
-
-        @pl.when(block < CONV_BLOCKS)
-        def _():
-            load(block).wait()
-            reducer.core_copy(block).start()
-
-        @pl.when(block < CONV_BLOCKS - 1)
-        def _():
-            load(block + 1).start()
+        rest_ref, conv_ref, grad_out, part_out, *reduce_refs = refs
+        sources = [(rest_ref, BACK_REST), (conv_ref, CONV_BLOCKS)]
+        feed(Reducer(reduce_refs, BACK_REST + CONV_BLOCKS), block, sources, part_out)
 
     @pl.when(block < OUT_BLOCKS)
     def _():
@@ -1589,8 +1857,8 @@
                 ).astype(bf16)
 
 
-def run_input(delta, weight, residual, live, conv=None):
-    reduced = conv is not None
+def run_input(delta, weight, residual, live, *rest):
+    reduced = bool(rest)
     out_shape = jax.ShapeDtypeStruct((ROWS, CHANNELS), bf16)
     out_specs = columns(ROWS, 0, OUT_BLOCKS)
     in_specs = [
@@ -1601,18 +1869,18 @@
     ]
     args = [delta, weight, residual, live]
     if reduced:
-        shape = (CONV_BLOCKS, 2, 128, 128)
+        shape = (BACK_REST + CONV_BLOCKS, 2, 128, 128)
         out_shape = (out_shape, jax.ShapeDtypeStruct(shape, f32))
         out_specs = (out_specs, pl.BlockSpec(shape, lambda i: (0, 0, 0, 0)))
-        in_specs.append(pl.BlockSpec(memory_space=HBM))
-        args.append(conv)
+        in_specs += [pl.BlockSpec(memory_space=HBM)] * 2
+        args += rest
     return pl.pallas_call(
         input_kernel,
-        grid=(CONV_BLOCKS + 4 if reduced else OUT_BLOCKS,),
+        grid=(BACK_REST + CONV_BLOCKS + 4 if reduced else OUT_BLOCKS,),
         out_shape=out_shape,
         in_specs=in_specs,
         out_specs=out_specs,
-        scratch_shapes=[pltpu.SemaphoreType.DMA((2,))] + Reducer.scratch() if reduced else [],
+        scratch_shapes=Reducer.scratch() if reduced else [],
         name="input",
         compiler_params=pltpu.CompilerParams(
             vmem_limit_bytes=VMEM_LIMIT,
@@ -1623,17 +1891,6 @@
             flops=2 * ROWS * WIDE * PADDED, bytes_accessed=35 * 2**20, transcendentals=0
         ),
     )(*args)
-
-
-def split(values):
-    high = values.astype(bf16)
-    low = (values - high.astype(f32)).astype(bf16)
-    return jnp.concatenate([high, low], axis=-2)
-
-
-def silu_slope(values):
-    sig_vals = jax.nn.sigmoid(values)
-    return sig_vals * (1.0 + values * (1.0 - sig_vals))
 
 
 def wide_lanes(values):
@@ -1659,17 +1916,23 @@
 
 
 def scatter(grads, width, size):
-    if size == SHARDS:
-        part = lax.psum_scatter(grads, "img", scatter_dimension=0, tiled=True)
-        part = swap_sum(part)
-        return part[:CHUNK, :width].reshape(-1)
-    grads = grads.reshape(SHARDS, CHUNK_PAD, -1)[:, :CHUNK, :width].reshape(-1)
-    return swap_sum(lax.psum_scatter(grads, "img", scatter_dimension=0, tiled=True))
+    if size != SHARDS:
+        grads = grads.reshape(SHARDS, CHUNK_PAD, -1)[:, :CHUNK, :width].reshape(-1)
+    return lax.psum_scatter(grads, "img", scatter_dimension=0, tiled=True)
+
+
+def shard_of(part, width, size):
+    part = swap_sum(part)
+    return part[:CHUNK, :width].reshape(-1) if size == SHARDS else part
 
 
 def swap_sum(part):
     other = lax.ppermute(part, "stream", [(0, 1), (1, 0)])
     return part.astype(f32) + other.astype(f32)
+
+
+def beside_blocks(first, blocks):
+    return jnp.concatenate([first, blocks.transpose(2, 0, 1, 3).reshape(128, -1)], axis=1)
 
 
 def chunked(values):
@@ -1726,9 +1989,8 @@
     live_lanes = jnp.broadcast_to(live[:, None], (ROWS, 128)).astype(bf16)
     edges = edge_masks()
 
-    pad_out = ((0, 0), (0, PADDED - CHANNELS))
-    x = jnp.pad(jnp.where(live[:, None], block_in[0], 0), pad_out)
-    cot = jnp.pad(jnp.where(live[:, None], out_cotangent[0], 0), pad_out)
+    x = block_in[0]
+    cot = out_cotangent[0]
 
     lines = CONV_LINES - 18
     if size == SHARDS:
@@ -1736,21 +1998,25 @@
         entry_piece = jnp.pad(entry_piece, ((0, CHUNK_PAD - CHUNK), (0, 0)))
         piece = group_weight.reshape(lines, GROUP_WIDTH)
         piece = jnp.pad(piece, ((0, CONV_LINES - lines), (0, 128 - GROUP_WIDTH)))
-        entry_mat, conv, x_chunked, x_turned = run_gather(entry_piece, piece, x)
+        entry_mat, conv, x_chunked, x_turned = run_gather(
+            entry_piece, piece, x, live_lanes, live[None].astype(f32)
+        )
         entry_mat = entry_mat.reshape(PADDED, WIDE)
         conv = conv[:, :lines, :GROUP_WIDTH]
     else:
-        x_chunked, x_turned = run_prepare(x)
+        x_padded = jnp.where(live[:, None], x, 0)
+        x_padded = jnp.pad(x_padded, ((0, 0), (0, PADDED - CHANNELS)))
+        x_chunked, x_turned = run_prepare(x_padded)
         entry_mat = wide_lanes(gather(entry_weight, CHANNELS, size)[:, :CHANNELS])
         conv = lax.all_gather(group_weight, "img", axis=0, tiled=True)
     conv = conv.reshape(9, CHANNELS, GROUP_WIDTH)
-    squeeze_mat = gather(squeeze_weight, SQUEEZE, size)[:, :SQUEEZE]
-    excite_mat = gather(excite_weight, SQUEEZE, size)[:, :SQUEEZE]
+    squeeze_mat = gather(squeeze_weight, SQUEEZE, size)
+    excite_mat = gather(excite_weight, SQUEEZE, size)
     exit_mat = gather(exit_weight, CHANNELS, size)
 
     def rows_of(*vectors):
-        kept = [wide_lanes(vector).reshape(BLOCKS, 2, 128) for vector in vectors]
-        return jnp.concatenate(kept, axis=1)
+        kept = wide_lanes(jnp.stack(vectors)).reshape(len(vectors), BLOCKS, 2, 128)
+        return kept.transpose(1, 0, 2, 3).reshape(BLOCKS, 2 * len(vectors), 128)
 
     params = rows_of(entry_gain, entry_shift, group_gain, group_shift)
     exit_params = [
@@ -1766,80 +2032,61 @@
         size, x_chunked, entry_mat, conv, params, pool, edges, fold.T
     )
 
-    def small_dot(a, b, dims=((1,), (0,))):
-        return lax.dot_general(
-            a, b.astype(f32), (dims, ((), ())), precision=lax.Precision.HIGHEST
-        )
-
-    quarters = CHANNELS // SQUEEZE
-    quarter = jnp.eye(quarters, dtype=f32)
-
-    def to_rows(values):
-        spread_out = values[None, :, :, None] * quarter[:, None, None, :]
-        return chunked(spread_out.reshape(quarters * CROPS, CHANNELS))
-
-    def to_quarters(values):
-        return values.reshape(CROPS, quarters, SQUEEZE).transpose(1, 0, 2).reshape(-1, SQUEEZE)
-
-    pooled = chunked(narrow_lanes(pooled) / area.astype(f32))
-    squeeze_in = small_dot(pooled, squeeze_mat) + squeeze_bias
-    squeezed = jax.nn.silu(squeeze_in)
-    squeezed_rows = to_rows(squeezed)
-    excite_in = small_dot(squeezed_rows, excite_mat).reshape(quarters, CROPS, SQUEEZE)
-    excite_in = excite_in.transpose(1, 0, 2).reshape(CROPS, CHANNELS)
-    gate = jax.nn.sigmoid(excite_in + excite_bias)
+    inner_pad = INNER - SQUEEZE
     spread = jnp.concatenate([pool.T, pool.T], axis=1)
-    gate_terms = split(wide_lanes(gate))
-    scaled, scaled_turned = run_scale(mixed, gate_terms, spread)
+    scaled, scaled_turned, gates, pooled, inner, inner_rows, quarter = run_scale(
+        mixed,
+        spread,
+        pooled,
+        squeeze_mat,
+        excite_mat,
+        jnp.pad(squeeze_bias, (0, inner_pad))[None],
+        jnp.pad(excite_bias.reshape(QUARTERS, SQUEEZE), ((0, 0), (0, inner_pad))),
+    )
 
     block_out, exit_delta, residual, exit_grad, exit_total = run_exit(
         size, scaled, scaled_turned, exit_mat, x, cot, exit_params, pair, pair.T, live_lanes
     )
-    if size == SHARDS:
-        exit_shard = exit_grad[:CHUNK, :CHANNELS].reshape(-1)
-    else:
-        exit_shard = scatter(exit_grad, CHANNELS, size)
+    exit_part = scatter(exit_grad, CHANNELS, size)
     scaled_grad, gate_grad = run_gate(exit_delta, exit_mat, mixed, pool)
 
-    used = crop_ids < IMAGE_DEV * per_image
-    gate_grad = jnp.where(used[:, None], narrow_lanes(gate_grad), 0.0)
-    excite_delta = gate_grad * gate * (1.0 - gate)
-    excite_quarters = to_quarters(excite_delta)
-    back_rows = unchunked(small_dot(excite_quarters, excite_mat, ((1,), (1,))))
-    back_rows = back_rows.reshape(quarters, CROPS, SQUEEZE, quarters)
-    squeeze_delta = jnp.sum(back_rows * quarter[:, None, None, :], axis=(0, 3))
-    squeeze_delta = squeeze_delta * silu_slope(squeeze_in)
-    pooled_grad = unchunked(small_dot(squeeze_delta, squeeze_mat, ((1,), (1,))))
-    pooled_grad = pooled_grad / area.astype(f32)
-    beside = ((0, 0), (0, 512 - SQUEEZE))
-    excite_grad = small_dot(squeezed_rows, jnp.pad(excite_quarters, beside), ((0,), (0,)))
-    squeeze_grad = small_dot(pooled, jnp.pad(squeeze_delta, beside), ((0,), (0,)))
-    excite_shard = scatter(excite_grad.astype(bf16), SQUEEZE, size)
-    squeeze_shard = scatter(squeeze_grad.astype(bf16), SQUEEZE, size)
-    gates = jnp.stack([gate_terms, split(wide_lanes(pooled_grad))])
-    bias_rows = jnp.concatenate(
-        [
-            jnp.pad(jnp.sum(squeeze_delta, axis=0), (0, 512 - SQUEEZE)),
-            jnp.pad(jnp.sum(excite_delta, axis=0), (0, 20 * 128 - CHANNELS)),
-        ]
-    ).reshape(BIAS_ROWS, 128)
-    entry_delta, entry_grad, conv_grad, totals, bias_totals = run_back(
-        size, bias_rows, scaled_grad, group, gates, spread, act, turned, conv, x_turned, params,
+    pooled_gates, inner_grads, bias_rows = run_squeeze(
+        gate_grad, pooled, inner, inner_rows, quarter, squeeze_mat, excite_mat
+    )
+    bias_rows = bias_rows.reshape(BIAS_ROWS, 128)
+    entry_delta, entry_grad, conv_grad, totals, bias_totals, *entry_rest = run_back(
+        size, bias_rows, scaled_grad, group, gates, pooled_gates, spread, act, turned, conv, x_turned, params,
         moment, edges, fold,
     )
+    entry_delta, exit_part, inner_grads = lax.optimization_barrier(
+        (entry_delta, exit_part, inner_grads)
+    )
+    exit_shard = shard_of(exit_part, CHANNELS, size)
     if size == SHARDS:
-        entry_shard = narrow_lanes(entry_grad[:CHUNK]).reshape(-1)
+        inner_part = swap_sum(scatter(inner_grads, 2 * INNER, size))[:CHUNK]
+        squeeze_shard = inner_part[:, :SQUEEZE].reshape(-1)
+        excite_shard = inner_part[:, INNER : INNER + SQUEEZE].reshape(-1)
+    else:
+        squeeze_shard = shard_of(scatter(inner_grads[:, :INNER], SQUEEZE, size), SQUEEZE, size)
+        excite_shard = shard_of(scatter(inner_grads[:, INNER:], SQUEEZE, size), SQUEEZE, size)
+    if size == SHARDS:
         conv_lines = 256 * CONV_BLOCKS
-        conv_grad = conv_grad.reshape(SHARDS, lines, GROUP_WIDTH)
+        conv_grad = conv_grad.reshape(SHARDS, lines // 2, 2 * GROUP_WIDTH)
         conv_grad = jnp.pad(
-            conv_grad, ((0, 0), (0, conv_lines - lines), (0, 128 - GROUP_WIDTH))
+            conv_grad,
+            ((0, 0), (0, conv_lines - lines // 2), (0, 128 - 2 * GROUP_WIDTH)),
         ).reshape(4, 2, 2, CONV_BLOCKS, 2, 128, 128)
         conv_grad = conv_grad.transpose(3, 2, 1, 0, 4, 5, 6)
-        input_grad, conv_part = run_input(entry_delta, entry_mat, residual, live_lanes, conv_grad)
-        conv_shard = conv_part.reshape(conv_lines, 128)[:lines, :GROUP_WIDTH].reshape(-1)
+        input_grad, parts = run_input(
+            entry_delta, entry_mat, residual, live_lanes, entry_rest[0], conv_grad
+        )
+        entry_grad = beside_blocks(entry_grad, parts[:BACK_REST])
+        entry_shard = narrow_lanes(entry_grad[:CHUNK]).reshape(-1)
+        conv_part = parts[BACK_REST:].reshape(conv_lines, 128)
+        conv_shard = conv_part[: lines // 2, : 2 * GROUP_WIDTH].reshape(-1)
     else:
         input_grad = run_input(entry_delta, entry_mat, residual, live_lanes)
-        entry_shard = scatter(narrow_lanes(entry_grad), CHANNELS, size)
+        entry_shard = swap_sum(scatter(narrow_lanes(entry_grad), CHANNELS, size))
         conv_part = lax.psum_scatter(
             conv_grad.reshape(-1), "img", scatter_dimension=0, tiled=True
         )
@@ -1853,7 +2100,7 @@
     group_gain_grad, group_shift_grad = [narrow_lanes(v) for v in folded(totals[:, 0])]
     entry_gain_grad, entry_shift_grad = [narrow_lanes(v) for v in folded(totals[:, 1])]
     exit_gain_grad, exit_shift_grad = [v[:CHANNELS] for v in folded(exit_total[:, 1])]
-    bias_totals = bias_totals.reshape(-1)
+    bias_totals = bias_totals.reshape(8, INNER)[: 1 + QUARTERS, :SQUEEZE]
     kept = jnp.concatenate(
         [
             jnp.stack(
@@ -1864,10 +2111,10 @@
                     group_shift_grad,
                     exit_gain_grad,
                     exit_shift_grad,
-                    bias_totals[512 : 512 + CHANNELS],
+                    bias_totals[1:].reshape(-1),
                 ]
             ),
-            jnp.pad(bias_totals[:SQUEEZE], (0, CHANNELS - SQUEEZE))[None],
+            jnp.pad(bias_totals[0], (0, CHANNELS - SQUEEZE))[None],
         ]
     )
     smalls = swap_sum(kept)

time: 677 us -> 604 us (0.89)
  matrix products: 19.9 us -> 0 us
  local copies, waits for them, and re-layouts: 81.9 us -> 64 us
  other arithmetic: 25.9 us -> 8.04 us
  Pallas kernels: 523 us -> 508 us
    pallas_call x3 -> x4, Pallas kernels: 313 us -> 292 us  [the longest x1 134 us: run_back(): pl.pallas_call(functools.partial(back_kernel, size), grid=(max(BLOCKS + 2...]
    dot_general x5 -> x0, matrix products: 17.6 us -> none  [small_dot(): lax.dot_general(a, b.astype(f32), (dims, ((), ())), precision=lax.Precisi...]
    pad x6 -> x4, local copies, waits for them, and re-layouts: 11.1 us -> 2.67 us  [the longest x1 1.26 us: local(): jnp.pad(squeeze_bias, (0, inner_pad))[None]]
    reshape x14 -> x10, local copies, waits for them, and re-layouts: 17.3 us -> 11.4 us  [the longest x1 2.08 us: local(): conv_grad = jnp.pad(conv_grad, ((0, 0), (0, conv_lines - lines // 2), (0,...]
  transfers between devices with their start and end apart: 8 -> 8, of which waited for: 2 -> 1; matrix products, arithmetic and copies ran while one was open for 16% -> 10% of each run, Pallas kernels for 57% -> 73%
where the time goes in v3:
time: 604 us; the launch traced here: 600 us
  Pallas kernels  508 us (84%)
  local copies, waits for them, and re-layouts  64 us (11%)
  between operations  14.4 us (2%)
  other arithmetic  8.04 us (1%)
    pallas_call x1, Pallas kernels, run_back(): pl.pallas_call(functools.partial(back_kernel, size), grid=(max(BLOCKS + 2...  134 us
    pallas_call x1, Pallas kernels, run_gather(): pl.pallas_call(gather_kernel, out_shape=(jax.ShapeDtypeStruct((SHARDS, CH...  87.4 us
    pallas_call x1, Pallas kernels, run_input(): pl.pallas_call(input_kernel, grid=(BACK_REST + CONV_BLOCKS + 4 if reduced...  80 us
    pallas_call x1, Pallas kernels, run_entry(): pl.pallas_call(functools.partial(entry_kernel, size), grid=(BLOCKS + 2,),...  74.5 us
    pallas_call x1, Pallas kernels, run_exit(): pl.pallas_call(functools.partial(exit_kernel, size), grid=(blocks + 3,),...  68.6 us
    pallas_call x1, Pallas kernels, run_gate(): pl.pallas_call(gate_kernel, grid=(BLOCKS,), out_shape=(jax.ShapeDtypeStru...  30.7 us
    pallas_call x1, Pallas kernels, run_scale(): pl.pallas_call(scale_kernel, grid=(BLOCKS + OUT_BLOCKS,), out_shape=(jax....  23.3 us
  transfers between devices with their start and end apart: 8, of which 1 were waited for; matrix products, arithmetic and copies ran while one was open for 10% of the time, Pallas kernels for 73%

profile of v3, /device:TPU:0, one launch (start us, length us, event | category | flops | bytes accessed | tf_op | source)
XLA Modules:
  0.0 600.4 jit_solution(8698069343689319692)
XLA Ops:
  11.0 1.8 reshape.209
  23.1 1.4 reshape.202
  25.2 2.2 reshape_reshape.9
  31.1 87.4 %gather.1 = (bf16[16,128,2304]{2,1,0:T(8,128)(2,1)}, bf16[16,1152,128]{2,1,0:T(8,128)(2,1)}, bf16[1568,2048]{1,0:T(8,128)(2,1)}, bf16[2048,1568]{1,0:T(8,128)(2,1)}) custom-call(bf16[128,2304]{1,0:T(8,128)(2,1)} %pad.51.entry_ref, bf16[1152,128]{1,0:T(8,128)(2,1)} %pad.52.conv_ref, bf16[1568,2016]{1,0:T(8,128)(2,1)} %bitcast.92, ...), custom_call_target="tpu_custom_call" | custom-call | flops 4932501504 | bytes 209715200 | tf_op jit(solution)/shard_map/gather/pallas_call | solution.py:1799
  118.5 4.8 slice.117
  123.3 6.2 %reshape.226.conv_ref = bf16[9,2016,56]{2,1,0:T(8,128)(2,1)} reshape(bf16[16,1134,56]{2,1,0:T(8,128)(2,1)} %slice.117) | data formatting | bytes 4064256 | tf_op jit(solution)/shard_map/reshape | solution.py:2012
  130.3 2.4 fusion.2
  135.3 74.5 %entry.1 = (f32[1568,2304]{1,0:T(8,128)}, bf16[9,256,1792]{2,1,0:T(8,128)(2,1)}, f32[1568,2304]{1,0:T(8,128)}, bf16[1568,2304]{1,0:T(8,128)(2,1)}, f32[16,2304]{1,0:T(8,128)}, /*index=5*/f32[9,2,8,128]{3,2,1,0:T(8,128)}) custom-call(bf16[1568,2048]{1,0:T(8,128)(2,1)} %get-tuple-element.53.x_ref, bf16[2048,2304]{1,0:T(8,128)(2,1)} %bitcast.95, ...), custom_call_target="tpu_custom_call" | custom-call | flops 31444697088 | bytes 73400320 | tf_op jit(solution)/shard_map/entry/pallas_call | solution.py:417
  209.9 23.3 %scale.1 = (bf16[1568,2048]{1,0:T(8,128)(2,1)}, bf16[2048,1568]{1,0:T(8,128)(2,1)}, bf16[32,2304]{1,0:T(8,128)(2,1)}, f32[16,2048]{1,0:T(8,128)}, f32[16,512]{1,...) custom-call(bf16[1568,2304]{1,0:T(8,128)(2,1)} %get-tuple-element.56.mixed_ref, ...), custom_call_target="tpu_custom_call" | custom-call | flops 6576668672 | bytes 31457280 | tf_op jit(solution)/shard_map/scale/pallas_call | solution.py:1174
  233.2 68.6 %exit.1 = (bf16[1568,2016]{1,0:T(8,128)(2,1)}, bf16[1568,2048]{1,0:T(8,128)(2,1)}, bf16[1568,2048]{1,0:T(8,128)(2,1)}, bf16[2048,2048]{1,0:T(8,128)(2,1)}, f32[8,2,8,128]{3,2,1,0:T(8,128)}) custom-call(bf16[1568,2048]{1,0:T(8,128)(2,1)} %get-tuple-element.58.scaled_ref, bf16[2048,1568]{1,0:T(8,128)(2,1)} %get-tuple-element.59.turned_ref, ...), custom_call_target="tpu_custom_call" | custom-call | flops 26306674688 | bytes 73400320 | tf_op jit(solution)/shard_map/exit/pallas_call | solution.py:899
  302.0 30.7 %gate.1 = (f32[1568,2304]{1,0:T(8,128)}, f32[16,2304]{1,0:T(8,128)}) custom-call(bf16[1568,2048]{1,0:T(8,128)(2,1)} %get-tuple-element.61.delta_ref, bf16[2048,2048]{1,0:T(8,128)(2,1)} %all-gather.8.cloned.1.call-done.weight_ref, bf16[1568,2304]{1,0:T(8,128)(2,1)} %get-tuple-element.56.mixed_ref, bf16[16,1568]{1,0:T(8,128)(2,1)} %get-tuple-element.116.pool_ref), custom_call_target="tpu_custom_call" | custom-call | flops 14797504512 | bytes 41943040 | tf_op jit(solution)/shard_map/gate/pallas_call | solution.py:966
  332.7 9.5 %squeeze.57 = (bf16[32,2304]{1,0:T(8,128)(2,1)}, bf16[2048,1024]{1,0:T(8,128)(2,1)}, f32[8,512]{1,0:T(8,128)}) custom-call(f32[16,2304]{1,0:T(8,128)} %get-tuple-element.62.gate_grad_ref, f32[16,2048]{1,0:T(8,128)} %get-tuple-element.63.pooled_ref, f32[16,512]{1,0:T(8,128)} %get-tuple-element.64.inner_ref, f32[64,2048]{1,0:T(8,128)} %get-tuple-element.65.rows_ref, ...), custom_call_target="tpu_custom_call" | custom-call | flops 2147483648 | bytes 20971520 | tf_op jit(solution)/shard_map/squeeze/pallas_call | solution.py:1278
  343.5 133.8 %back.1 = (bf16[1568,2304]{1,0:T(8,128)(2,1)}, f32[128,1536]{1,0:T(8,128)}, bf16[9,1008,112]{2,1,0:T(8,128)(2,1)}, f32[9,2,8,128]{3,2,1,0:T(8,128)}, f32[32,128]...) custom-call(f32[32,128]{1,0:T(8,128)} %reshape.215.bias_ref, f32[1568,2304]{1,0:T(8,128)} %get-tuple-element.68.grad_ref, ...), custom_call_target="tpu_custom_call" | custom-call | flops 48091889664 | bytes 94371840 | tf_op jit(solution)/shard_map/back/pallas_call | solution.py:1540
  480.2 2.0 reshape.216
  482.9 2.1 copy.77
  486.3 1.7 collective-permute-start.2
  487.9 80.0 %input.1 = (bf16[1568,2016]{1,0:T(8,128)(2,1)}, f32[6,2,128,128]{3,2,1,0:T(8,128)}) custom-call(bf16[1568,2304]{1,0:T(8,128)(2,1)} %get-tuple-element.79.delta_ref, bf16[2048,2304]{1,0:T(8,128)(2,1)} %bitcast.96, bf16[1568,2048]{1,0:T(8,128)(2,1)} %get-tuple-element.80.residual_ref, bf16[1568,128]{1,0:T(8,128)(2,1)} %broadcast_in_dim.18.live_ref, ...), custom_call_target="tpu_custom_call" | custom-call | flops 14797504512 | bytes 36700160 | tf_op jit(solution)/shard_map/input/pallas_call | solution.py:1877
  571.0 1.7 copy.65
  572.7 1.9 reshape_reshape.11
  575.7 1.3 convert_add_fusion
  577.1 1.6 reshape.225
  578.6 2.6 collective-permute-done.1
  584.1 6.9 %copy.84 = bf16[1,1568,2016]{2,1,0:T(8,128)(2,1)} copy(bf16[1,1568,2016]{2,1,0:T(8,128)(2,1)} %bitcast.62) | data formatting | bytes 12644352
  591.0 2.7 copy.85
  (109 shorter events, 35.0 us)
Async XLA Ops:
  7.2 202.6 %all-gather.4.cloned.1.call-start = ((), (), s32[]{:S(2)}) async-start(), calls=%async_computation.2 | async-start | bytes 2228224 | tf_op jit(solution)/shard_map/all_gather | solution.py:1913
  9.1 200.8 %all-gather.6.cloned.1.call-start = ((), (), s32[]{:S(2)}) async-start(), calls=%async_computation.3 | async-start | bytes 2228224 | tf_op jit(solution)/shard_map/all_gather | solution.py:1913
  11.0 222.3 %all-gather.8.cloned.1.call-start = ((), (), s32[]{:S(2)}) async-start(), calls=%async_computation.4 | async-start | bytes 8912896 | tf_op jit(solution)/shard_map/all_gather | solution.py:1913
  13.6 463.7 %reduce-scatter.3.cloned.1.call-start = ((), (), s32[]{:S(2)}) async-start(), calls=%async_computation.5 | async-start | bytes 8912896 | tf_op jit(solution)/shard_map/reduce_scatter | solution.py:1921
  123.3 11.1 %copy-start.2 = (f32[2,424]{1,0:T(2,128)S(1)}, f32[2,424]{1,0:T(2,128)}, u32[]{:S(2)}) copy-start(f32[2,424]{1,0:T(2,128)} %constant.54.clone) | copy-start | bytes 10180
  301.9 272.7 %reduce-scatter.5.cloned.1.call-start = ((), (), s32[]{:S(2)}) async-start(), calls=%async_computation.6 | async-start | bytes 4456448 | tf_op jit(solution)/shard_map/reduce_scatter | solution.py:1921
  343.5 134.7 %copy-start.1 = (f32[8,2,8,128]{3,2,1,0:T(8,128)S(1)}, f32[8,2,8,128]{3,2,1,0:T(8,128)}, u32[]{:S(2)}) copy-start(f32[8,2,8,128]{3,2,1,0:T(8,128)} %get-tuple-element.87) | copy-start | bytes 196612
  479.8 5.3 collective-permute-start
  486.3 89.4 %collective-permute-start.2 = (bf16[128,2048]{1,0:T(8,128)(2,1)}, bf16[128,2048]{1,0:T(8,128)(2,1)}, u32[]{:S(2)}, u32[]{:S(2)}) collective-permute-start(bf16[128,2048]{1,0:T(8,128)(2,1)} %reduce-scatter.3.cloned.1.call-done), channel_id=1, source_target_pairs={{0,16},{16,0},{1,17},{17,1},{2,18},{18,2},{3,19},{19,3},{4,20},{20... | collective-permute-start | bytes 1572872 | tf_op jit(solution)/shard_map/ppermute | solution.py:1930
  487.9 82.5 %copy-start = (f32[128,1536]{1,0:T(8,128)S(1)}, f32[128,1536]{1,0:T(8,128)}, u32[]{:S(2)}) copy-start(f32[128,1536]{1,0:T(8,128)} %get-tuple-element.84) | copy-start | bytes 2359300
  574.6 6.6 %collective-permute-start.1 = (bf16[128,1024]{1,0:T(8,128)(2,1)}, bf16[128,1024]{1,0:T(8,128)(2,1)S(1)}, u32[]{:S(2)}, u32[]{:S(2)}) collective-permute-start(bf16[128,1024]{1,0:T(8,128)(2,1)} %reduce-scatter.5.cloned.1.call-done), channel_id=1, source_target_pairs={{0,16},{16,0},{1,17},{17,1},{2,18},{18,2},{3,19},{19,3},{4,20},{20... | collective-permute-start | bytes 786440 | tf_op jit(solution)/shard_map/ppermute | solution.py:1930
  583.2 7.8 %slice-start = ((s8[6422528]{0:T(1024)(128)(4,1)}), s8[2228224]{0:T(1024)(128)(4,1)S(1)}, s32[]{:S(2)}) async-start(s8[6422528]{0:T(1024)(128)(4,1)} %bitcast.63), calls=%async_computation.7 | async-start | bytes 4456448
  584.1 6.9 %slice-start.1 = ((s8[6422528]{0:T(1024)(128)(4,1)}), s8[4194304]{0:T(1024)(128)(4,1)S(1)}, s32[]{:S(2)}) async-start(s8[6422528]{0:T(1024)(128)(4,1)} %bitcast.63), calls=%async_computation.8 | async-start | bytes 8388608
Sparse Core Ops, SparseCore 0:
  10.7 67.8 all-gather.3
  81.4 43.5 all-gather.5
  127.7 92.0 all-gather.7
  302.0 127.6 reduce-scatter.2
  477.5 87.6 reduce-scatter.4

commit v4 on v3

--- a/solution.py
+++ b/solution.py
@@ -73,34 +73,44 @@
     return barrier
 
 
-def send_sums(size, slot, packed, sent, got, send_sem, recv_sem):
-    stream = lax.axis_index("stream")
-    me = lax.axis_index("img")
-    sent[slot] = packed
-    got[slot, me] = packed
-
-    def send(step, carry):
-        pltpu.make_async_remote_copy(
-            src_ref=sent.at[slot],
-            dst_ref=got.at[slot, me],
-            send_sem=send_sem.at[slot],
-            recv_sem=recv_sem.at[slot],
-            device_id=(stream, lax.rem(me + step, size)),
-            device_id_type=MESH,
-        ).start()
-        return carry
-
-    lax.fori_loop(1, size, send, 0)
-
-
-def take_sums(size, slot, got, send_sem, recv_sem):
-    others = got.at[slot, pl.ds(0, size - 1)]
-    pltpu.make_async_copy(others, others, recv_sem.at[slot]).wait()
-    pltpu.make_async_copy(others, others, send_sem.at[slot]).wait()
-    total = got[slot, 0]
-    for peer in range(1, size):
-        total = total + got[slot, peer]
-    return total
+class Exchange:
+    def __init__(self, size, sent, got, send_sem, recv_sem):
+        self.size, self.sent, self.got = size, sent, got
+        self.send_sem, self.recv_sem = send_sem, recv_sem
+
+    @staticmethod
+    def scratch(steps, size):
+        return [
+            pltpu.VMEM((steps, 2, 8, 128), f32),
+            pltpu.VMEM((steps, 2, size, 8, 128), f32),
+            pltpu.SemaphoreType.DMA((steps, 2)),
+            pltpu.SemaphoreType.DMA((steps, 2)),
+        ]
+
+    def put(self, slot, kind, packed):
+        stream = lax.axis_index("stream")
+        me = lax.axis_index("img")
+        self.sent[slot, kind] = packed
+        self.got[slot, kind, me] = packed
+
+        def start(step, carry):
+            pltpu.make_async_remote_copy(
+                src_ref=self.sent.at[slot, kind],
+                dst_ref=self.got.at[slot, kind, me],
+                send_sem=self.send_sem.at[slot, kind],
+                recv_sem=self.recv_sem.at[slot, kind],
+                device_id=(stream, lax.rem(me + step, self.size)),
+                device_id_type=MESH,
+            ).start()
+            return carry
+
+        lax.fori_loop(1, self.size, start, 0)
+
+    def total(self, slot, kind):
+        others = self.got.at[slot, kind, pl.ds(0, self.size - 1)]
+        pltpu.make_async_copy(others, others, self.recv_sem.at[slot, kind]).wait()
+        pltpu.make_async_copy(others, others, self.send_sem.at[slot, kind]).wait()
+        return add_up(self.got[slot, kind, peer] for peer in range(self.size))
 
 
 def row_count(size):
@@ -265,11 +275,9 @@
     windows,
     wide_ref,
     full_ref,
-    sent,
-    got,
-    send_sem,
-    recv_sem,
+    *exchange_refs,
 ):
+    exchange = Exchange(size, *exchange_refs)
     step = pl.program_id(0)
     count = row_count(size)
     on_global = lax.axis_index("stream") == 0
@@ -297,13 +305,13 @@
                 act = first_rows[slot, tile, here]
                 act_out[here, 128 * tile : 128 * tile + 128] = act
                 sums.add(chunk // HALF_STEPS, tile, act, act * act)
-        send_sums(size, step, sums.packed(), sent, got, send_sem, recv_sem)
+        exchange.put(step, 0, sums.packed())
 
     @pl.when((step >= 1) & (step < BLOCKS + 1))
     def _():
         block = step - 1
         slot = lax.rem(block, 2)
-        total = take_sums(size, block, got, send_sem, recv_sem)
+        total = exchange.total(step - 1, 0)
         total_out[block, 0] = total
         param = param_ref[block]
         scales = {}
@@ -337,9 +345,6 @@
                 turned_out[0, 128 * tile : 128 * tile + 128] = pads[
                     0, tile, TOP : TOP + DEEP_ROWS
                 ].T.astype(bf16)
-
-        def send(sums):
-            send_sums(size, BLOCKS + block, sums.packed(), sent, got, send_sem, recv_sem)
 
         @pl.when(on_global)
         def _():
@@ -353,7 +358,7 @@
                 for tile in range(2):
                     act = unpadded(second, tile, STEP // 8 * chunk, STEP // 8)
                     sums.add(chunk // HALF_STEPS, tile, act, act * act)
-            send(sums)
+            exchange.put(step, 1, sums.packed())
 
         @pl.when(jnp.logical_not(on_global))
         def _():
@@ -371,13 +376,13 @@
                 for tile in range(2):
                     act = second[tile, chunk_rows(chunk)]
                     sums.add(chunk // HALF_STEPS, tile, act, act * act)
-            send(sums)
+            exchange.put(step, 1, sums.packed())
 
     @pl.when(step >= 2)
     def _():
         block = step - 2
         slot = lax.rem(block, 2)
-        total = take_sums(size, BLOCKS + block, got, send_sem, recv_sem)
+        total = exchange.total(step - 1, 1)
         total_out[block, 1] = total
         param = param_ref[block]
         second = second_rows.at[slot]
@@ -428,11 +433,11 @@
         in_specs=[
             whole((ROWS, PADDED)),
             pl.BlockSpec((PADDED, LANES), lambda i: (0, at(0)(i))),
-            pl.BlockSpec((9, BLOCK, GROUP_WIDTH), lambda i: (0, at(1)(i), 0)),
+            pl.BlockSpec((9, BLOCK, 128), lambda i: (0, at(1)(i), 0)),
             whole((BLOCKS, 8, 128)),
             whole((CROPS, ROWS)),
             whole((2, IMAGE_PAD, 128)),
-            whole((GROUP_WIDTH, LANES)),
+            whole((128, LANES)),
         ],
         out_specs=(
             pl.BlockSpec((ROWS, LANES), lambda i: (0, at(0)(i))),
@@ -450,11 +455,8 @@
             pltpu.VMEM((CONV_ROWS, 9 * LANES), bf16),
             pltpu.VMEM((2, CONV_ROWS, 128), f32),
             pltpu.VMEM((9 * LANES, LANES), bf16),
-            pltpu.VMEM((2 * BLOCKS, 8, 128), f32),
-            pltpu.VMEM((2 * BLOCKS, size, 8, 128), f32),
-            pltpu.SemaphoreType.DMA((2 * BLOCKS,)),
-            pltpu.SemaphoreType.DMA((2 * BLOCKS,)),
-        ],
+        ]
+        + Exchange.scratch(BLOCKS + 1, size),
         name="entry",
         compiler_params=pltpu.CompilerParams(
             collective_id=1, has_side_effects=True, vmem_limit_bytes=VMEM_LIMIT
@@ -752,13 +754,11 @@
     slope_ref,
     pair_sent,
     pair_got,
-    sent,
-    got,
-    send_sem,
-    recv_sem,
     pair_send,
     pair_recv,
+    *exchange_refs,
 ):
+    exchange = Exchange(size, *exchange_refs)
     step = pl.program_id(0)
     count = row_count(size)
     stream = lax.axis_index("stream")
@@ -799,13 +799,13 @@
             for tile in range(2):
                 act = act_ref[slot, chunk_rows(chunk), 128 * tile : 128 * tile + 128]
                 sums.add(chunk // HALF_STEPS, tile, act, act * act)
-        send_sums(size, step, sums.packed(), sent, got, send_sem, recv_sem)
+        exchange.put(step, 0, sums.packed())
 
     @pl.when((step >= 1) & (step < blocks + 1))
     def _():
         block = step - 1
         slot = lax.rem(block, 4)
-        total = take_sums(size, block, got, send_sem, recv_sem)
+        total = exchange.total(step - 1, 0)
         total_out[block, 0] = total
         param = param_ref[block]
         inside = used_lanes(block)
@@ -861,15 +861,14 @@
                 residual_out[here, lanes] = delta.astype(bf16)
                 normed = act_ref[slot, here, lanes] * inverse - mean * inverse
                 sums.add(chunk // HALF_STEPS, tile, delta, delta * normed)
-        send_sums(size, blocks + block, sums.packed(), sent, got, send_sem, recv_sem)
-
+        exchange.put(step, 1, sums.packed())
     @pl.when(step >= 3)
     def _():
         block = step - 3
         slot = lax.rem(block, 4)
         hold = lax.rem(block, 3)
         moment = total_out[block, 0]
-        total = take_sums(size, blocks + block, got, send_sem, recv_sem)
+        total = exchange.total(step - 1, 1)
         total_out[block, 1] = total
         param = param_ref[block]
         for micro in range(MICRO_BATCHES):
@@ -929,13 +928,10 @@
             pltpu.VMEM((3, ROWS, LANES), f32),
             pltpu.VMEM((blocks, 8, LANES), f32),
             pltpu.VMEM((blocks, 8, LANES), f32),
-            pltpu.VMEM((2 * blocks, 8, 128), f32),
-            pltpu.VMEM((2 * blocks, size, 8, 128), f32),
-            pltpu.SemaphoreType.DMA((2 * blocks,)),
-            pltpu.SemaphoreType.DMA((2 * blocks,)),
             pltpu.SemaphoreType.DMA((blocks,)),
             pltpu.SemaphoreType.DMA((blocks,)),
-        ],
+        ]
+        + Exchange.scratch(blocks + 2, size),
         name="exit",
         compiler_params=pltpu.CompilerParams(
             collective_id=2, has_side_effects=True, vmem_limit_bytes=VMEM_LIMIT
@@ -948,8 +944,11 @@
     )(scaled, turned, weight, x, cot, params, pair, spread, live)
 
 
-def gate_kernel(delta_ref, weight_ref, mixed_ref, pool_ref, scaled_out, gate_out):
+def gate_kernel(
+    delta_ref, weight_ref, mixed_ref, pool_ref, block_ref, scaled_out, gate_out, block_out
+):
     block = pl.program_id(0)
+    block_out[...] = block_ref[...]
     first = jnp.minimum((BLOCK * block) // CHUNK, SHARDS - 3)
     row = lax.broadcasted_iota(jnp.int32, (LANES, 3 * CHUNK_PAD), 0)
     lane = lax.broadcasted_iota(jnp.int32, (LANES, 3 * CHUNK_PAD), 1)
@@ -962,27 +961,33 @@
     gate_out[...] = dot(pool_ref[...], (grad * mixed_ref[...].astype(f32)).astype(bf16))
 
 
-def run_gate(delta, weight, mixed, pool):
+def run_gate(delta, weight, mixed, pool, block):
     return pl.pallas_call(
         gate_kernel,
         grid=(BLOCKS,),
         out_shape=(
             jax.ShapeDtypeStruct((ROWS, WIDE), f32),
             jax.ShapeDtypeStruct((CROPS, WIDE), f32),
+            jax.ShapeDtypeStruct((ROWS, CHANNELS), bf16),
         ),
         in_specs=[
             whole((ROWS, PADDED)),
             whole((PADDED, PADDED)),
             columns(ROWS, 0, BLOCKS),
             whole((CROPS, ROWS)),
+            columns(ROWS, 0, OUT_BLOCKS),
         ],
-        out_specs=(columns(ROWS, 0, BLOCKS), columns(CROPS, 0, BLOCKS)),
+        out_specs=(
+            columns(ROWS, 0, BLOCKS),
+            columns(CROPS, 0, BLOCKS),
+            columns(ROWS, 0, OUT_BLOCKS),
+        ),
         name="gate",
         compiler_params=pltpu.CompilerParams(vmem_limit_bytes=VMEM_LIMIT),
         cost_estimate=pl.CostEstimate(
             flops=2 * ROWS * WIDE * PADDED, bytes_accessed=40 * 2**20, transcendentals=0
         ),
-    )(delta, weight, mixed, pool)
+    )(delta, weight, mixed, pool, block)
 
 
 def pair_lane(shape, dim):
@@ -1334,16 +1339,14 @@
     windows,
     wide_ref,
     full_ref,
-    sent,
-    got,
-    bias_got,
-    send_sem,
-    recv_sem,
-    bias_sem,
-    even_ref,
-    odd_ref,
-    *reduce_refs,
+        bias_got,
+        bias_sem,
+        even_ref,
+        odd_ref,
+        *refs,
     ) = refs
+    exchange = Exchange(size, *refs[:4])
+    reduce_refs = refs[4:]
     step = pl.program_id(0)
     count = row_count(size)
     on_global = lax.axis_index("stream") == 0
@@ -1422,13 +1425,13 @@
                     delta = (grad_ref[here, lanes] * gate[:, lanes] + pooled[:, lanes]) * slope
                     delta_two[slot, tile, here] = delta
                     sums.add(micro, tile, delta, delta * normed)
-        send_sums(size, step, sums.packed(), sent, got, send_sem, recv_sem)
+        exchange.put(step, 0, sums.packed())
 
     @pl.when((step >= 1) & (step < BLOCKS + 1))
     def _():
         block = step - 1
         slot = lax.rem(block, 2)
-        total = take_sums(size, block, got, send_sem, recv_sem)
+        total = exchange.total(step - 1, 0)
         total_out[block, 0] = total
         param = param_ref[block]
         moment = moment_ref[block, 1]
@@ -1471,9 +1474,7 @@
                         delta = load(tile, chunk) * slope
                         delta_one[slot, tile, here] = delta
                         sums.add(micro, tile, delta, delta * normed)
-            send_sums(
-                size, BLOCKS + block, sums.packed(), sent, got, send_sem, recv_sem
-            )
+            exchange.put(step, 1, sums.packed())
 
         @pl.when(on_global)
         def _():
@@ -1513,7 +1514,7 @@
     def _():
         block = step - 2
         slot = lax.rem(block, 2)
-        total = take_sums(size, BLOCKS + block, got, send_sem, recv_sem)
+        total = exchange.total(step - 1, 1)
         total_out[block, 1] = total
         param = param_ref[block]
         moment = moment_ref[block, 0]
@@ -1561,12 +1562,12 @@
             columns(ROWS, 1, BLOCKS),
             columns(ROWS, 2, BLOCKS),
             pl.BlockSpec((1, LANES, DEEP_ROWS), lambda i: (jnp.clip(i - 1, 0, BLOCKS - 1), 0, 0)),
-            pl.BlockSpec((9, BLOCK, GROUP_WIDTH), lambda i: (0, jnp.clip(i - 1, 0, BLOCKS - 1), 0)),
+            pl.BlockSpec((9, BLOCK, 128), lambda i: (0, jnp.clip(i - 1, 0, BLOCKS - 1), 0)),
             whole((PADDED, ROWS)),
             whole((BLOCKS, 8, 128)),
             whole((BLOCKS, 2, 8, 128)),
             whole((2, IMAGE_PAD, 128)),
-            whole((LANES, GROUP_WIDTH)),
+            whole((LANES, 128)),
         ],
         out_specs=(
             columns(ROWS, 2, BLOCKS),
@@ -1585,15 +1586,12 @@
             pltpu.VMEM((DEEP_ROWS, 9 * LANES), bf16),
             pltpu.VMEM((2, CONV_ROWS, 128), f32),
             pltpu.VMEM((9 * LANES, LANES), bf16),
-            pltpu.VMEM((2 * BLOCKS, 8, 128), f32),
-            pltpu.VMEM((2 * BLOCKS, size, 8, 128), f32),
             pltpu.VMEM((size, BIAS_ROWS, 128), f32),
-            pltpu.SemaphoreType.DMA((2 * BLOCKS,)),
-            pltpu.SemaphoreType.DMA((2 * BLOCKS,)),
             pltpu.SemaphoreType.DMA((2,)),
             pltpu.VMEM((BLOCK, 128), f32),
             pltpu.VMEM((BLOCK // 2, 128), f32),
         ]
+        + Exchange.scratch(BLOCKS + 1, size)
         + (Reducer.scratch() if reduced else []),
         name="back",
         compiler_params=pltpu.CompilerParams(
@@ -1614,23 +1612,36 @@
     entry_ref,
     conv_ref,
     x_ref,
-    live_ref,
-    lane_ref,
-    entry_out,
-    conv_out,
-    chunk_out,
-    turned_out,
-    x_rows,
-    chunk_rows_ref,
-    turned_rows,
-    send_sem,
-    recv_sem,
-    local_sem,
-    store_sem,
+    target_ref,
+    *refs,
 ):
+    vectors, exit_vectors = refs[:4], refs[4:6]
+    (
+        entry_out,
+        lines_out,
+        chunk_out,
+        turned_out,
+        live_out,
+        pool_out,
+        spread_out,
+        pair_out,
+        pull_out,
+        param_out,
+        exit_param_out,
+        conv_rows,
+        shifted,
+        lines,
+        x_rows,
+        chunk_rows_ref,
+        turned_rows,
+        send_sem,
+        recv_sem,
+        local_sem,
+        store_sem,
+    ) = refs[6:]
     stream, z, x, core = place()
     pieces = (entry_ref, conv_ref)
-    wholes = (entry_out, conv_out)
+    wholes = (entry_out, conv_rows)
     quarters = (CHUNK_PAD // 4, CONV_LINES // 4)
     waiting = []
 
@@ -1646,8 +1657,8 @@
             return (1 - stream, shard(0))
         return (stream, {"z": shard(k), "x": shard(0, 1), "core": shard(0, 0, 1)}[name])
 
-    def push(slot, to, index, first, count, k=0, own=False):
-        for array in range(2):
+    def push(arrays, slot, to, index, first, count, k=0, own=False):
+        for array in arrays:
             target = region(array, index, first, count)
             source = target
             if own:
@@ -1665,8 +1676,8 @@
             ).start()
             waiting.append((array, slot, target))
 
-    def arrive(slot, index, first, count):
-        for array in range(2):
+    def arrive(arrays, slot, index, first, count):
+        for array in arrays:
             target = region(array, index, first, count)
             pltpu.make_async_copy(target, target, recv_sem.at[array, slot]).wait()
 
@@ -1683,11 +1694,58 @@
         copy.start()
     pl.semaphore_wait(barrier, 6)
 
-    push(6, "x", shard(0), stream, 3, own=True)
-    for k in (1, 2, 3):
-        push(k - 1, "z", shard(0), 2 * stream, 2, k, own=True)
-    push(17, "core", shard(0), 0, 4, own=True)
-
+    entry, conv = (0,), (1,)
+    for array in (conv, entry):
+        push(array, 6, "x", shard(0), stream, 3, own=True)
+        for k in (1, 2, 3):
+            push(array, k - 1, "z", shard(0), 2 * stream, 2, k, own=True)
+        push(array, 17, "core", shard(0), 0, 4, own=True)
+
+    on_global = stream == 0
+
+    def rows_of(shape, dim):
+        row = lax.broadcasted_iota(jnp.int32, shape, dim)
+        image = row // IMAGE_ROWS
+        within = row - IMAGE_ROWS * image
+        live = within < jnp.where(on_global, IMAGE_ROWS, SMALL_ROWS)
+        return image, within, live
+
+    def members(shape, dim):
+        image, within, live = rows_of(shape, dim)
+        crop = jnp.where(on_global, within // GLOBAL_SIDE**2, within // SMALL_SIDE**2)
+        slot = lax.rem(lax.broadcasted_iota(jnp.int32, shape, 1 - dim), CROPS)
+        target = jnp.zeros(shape, jnp.int32)
+        for at in range(IMAGE_DEV):
+            for small in range(SMALL_CROPS):
+                target = jnp.where(
+                    (image == at) & (crop == small), target_ref[at, small], target
+                )
+        target = jnp.where(on_global, crop, target)
+        crops = jnp.where(on_global, GLOBAL_CROPS, SMALL_CROPS)
+        pool = one_hot(live & (crops * image + crop == slot))
+        return pool, one_hot(live & (GLOBAL_CROPS * image + target == slot))
+
+    for at, ref in enumerate(vectors):
+        values = ref[...]
+        for block in range(BLOCKS):
+            start = BLOCK * block
+            param_out[block, 2 * at : 2 * at + 1] = values[:, start : start + 128]
+            param_out[block, 2 * at + 1 : 2 * at + 2] = jnp.concatenate(
+                [values[:, start + 128 : start + BLOCK], jnp.zeros((1, LANES - BLOCK), f32)], axis=1
+            )
+    exit_param_out[...] = jnp.zeros_like(exit_param_out)
+    for at, ref in enumerate(exit_vectors):
+        for tile in range(PADDED // 128):
+            width = min(128, CHANNELS - 128 * tile)
+            exit_param_out[tile // 2, 2 * at + tile % 2, :width] = ref[
+                0, 128 * tile : 128 * tile + width
+            ]
+    pool_out[...], pair_out[...] = members((CROPS, ROWS), 1)
+    spread, pull = members((ROWS, 2 * CROPS), 0)
+    spread_out[...] = spread
+    pull_out[...] = pull[:, :CROPS]
+    live_out[...] = one_hot(rows_of((ROWS, 128), 0)[2])
+    live_lane = jnp.where(rows_of((1, ROWS), 1)[2], 1.0, 0.0)
     stores = []
 
     def prepare(pair):
@@ -1707,11 +1765,11 @@
         for tile in range(2):
             lanes = slice(128 * tile, 128 * tile + 128)
             chunk_rows_ref[slot, :, lanes] = (
-                picked[:, lanes] * live_ref[...].astype(f32)
+                picked[:, lanes] * live_out[...].astype(f32)
             ).astype(bf16)
         there = lax.broadcasted_iota(jnp.int32, (LANES, depth), 1) + source
         pick = one_hot(there == pair_lane((LANES, depth), 0))
-        turned_rows[slot] = (dot(pick, values, ((1,), (1,))) * lane_ref[...]).astype(bf16)
+        turned_rows[slot] = (dot(pick, values, ((1,), (1,))) * live_lane).astype(bf16)
         lanes = slice(LANES * pair, LANES * (pair + 1))
         copies = (
             pltpu.make_async_copy(chunk_rows_ref.at[slot], chunk_out.at[:, lanes], store_sem.at[0, pair]),
@@ -1721,99 +1779,137 @@
             copy.start()
         stores.append(copies)
 
-    def from_z(k):
-        arrive(k - 1, shard(k), 2 * stream, 2)
-        push(6 + k, "x", shard(k), 2 * stream, 2)
-        push(2 + k, "y", shard(k), 2 * stream, 2)
-        push(17 + k, "core", shard(k), 2 * stream, 2)
-
-    def from_y(k):
-        arrive(2 + k, shard(k), 2 - 2 * stream, 2)
-        push(9 + k, "x", shard(k), 2 - stream, 1)
-        push(20 + k, "core", shard(k), 2 - 2 * stream, 2)
-
-    def from_x(k):
+    def from_z(a, k):
+        arrive(a, k - 1, shard(k), 2 * stream, 2)
+        push(a, 6 + k, "x", shard(k), 2 * stream, 2)
+        push(a, 2 + k, "y", shard(k), 2 * stream, 2)
+        push(a, 17 + k, "core", shard(k), 2 * stream, 2)
+
+    def from_y(a, k):
+        arrive(a, 2 + k, shard(k), 2 - 2 * stream, 2)
+        push(a, 9 + k, "x", shard(k), 2 - stream, 1)
+        push(a, 20 + k, "core", shard(k), 2 - 2 * stream, 2)
+
+    def from_x(a, k):
         if k == 0:
-            arrive(6, shard(0, 1), stream, 3)
-            push(13, "y", shard(0, 1), 3 * stream, 1)
-            push(24, "core", shard(0, 1), stream, 3)
+            arrive(a, 6, shard(0, 1), stream, 3)
+            push(a, 13, "y", shard(0, 1), 3 * stream, 1)
+            push(a, 24, "core", shard(0, 1), stream, 3)
         else:
-            arrive(6 + k, shard(k, 1), 2 * stream, 2)
-            push(13 + k, "y", shard(k, 1), 3 * stream, 1)
-            push(24 + k, "core", shard(k, 1), 2 * stream, 2)
-
-    def last_x(k):
-        arrive(9 + k, shard(k, 1), 2 - stream, 1)
-        push(27 + k, "core", shard(k, 1), 2 - stream, 1)
-
-    def last_y(k):
-        arrive(13 + k, shard(k, 1), 3 - 3 * stream, 1)
-        push(31 + k, "core", shard(k, 1), 3 - 3 * stream, 1)
-
-    prepare(0)
-    prepare(1)
-    from_z(1)
-    prepare(2)
-    from_z(2)
-    from_x(0)
-    prepare(3)
-    from_z(3)
-    from_y(1)
-    prepare(4)
-    from_x(1)
-    from_y(2)
-    prepare(5)
-    from_x(2)
-    from_y(3)
-    prepare(6)
-    from_x(3)
-    last_y(0)
-    last_x(1)
-    prepare(7)
-    last_y(1)
-    last_x(2)
-    last_y(2)
-    last_x(3)
-    last_y(3)
-
-    arrive(17, shard(0, 0, 1), 0, 4)
-    for k in (1, 2, 3):
-        arrive(17 + k, shard(k, 0, 1), 2 * stream, 2)
-        arrive(20 + k, shard(k, 0, 1), 2 - 2 * stream, 2)
-    arrive(24, shard(0, 1, 1), stream, 3)
-    for k in (1, 2, 3):
-        arrive(24 + k, shard(k, 1, 1), 2 * stream, 2)
-        arrive(27 + k, shard(k, 1, 1), 2 - stream, 1)
-    for k in range(4):
-        arrive(31 + k, shard(k, 1, 1), 3 - 3 * stream, 1)
+            arrive(a, 6 + k, shard(k, 1), 2 * stream, 2)
+            push(a, 13 + k, "y", shard(k, 1), 3 * stream, 1)
+            push(a, 24 + k, "core", shard(k, 1), 2 * stream, 2)
+
+    def last_x(a, k):
+        arrive(a, 9 + k, shard(k, 1), 2 - stream, 1)
+        push(a, 27 + k, "core", shard(k, 1), 2 - stream, 1)
+
+    def last_y(a, k):
+        arrive(a, 13 + k, shard(k, 1), 3 - 3 * stream, 1)
+        push(a, 31 + k, "core", shard(k, 1), 3 - 3 * stream, 1)
+
+    def last_core(a):
+        arrive(a, 17, shard(0, 0, 1), 0, 4)
+        for k in (1, 2, 3):
+            arrive(a, 17 + k, shard(k, 0, 1), 2 * stream, 2)
+            arrive(a, 20 + k, shard(k, 0, 1), 2 - 2 * stream, 2)
+        arrive(a, 24, shard(0, 1, 1), stream, 3)
+        for k in (1, 2, 3):
+            arrive(a, 24 + k, shard(k, 1, 1), 2 * stream, 2)
+            arrive(a, 27 + k, shard(k, 1, 1), 2 - stream, 1)
+        for k in range(4):
+            arrive(a, 31 + k, shard(k, 1, 1), 3 - 3 * stream, 1)
+
+    def forward(a, between):
+        between = iter(between)
+
+        def pause():
+            for work in between:
+                work()
+                break
+
+        pause()
+        from_z(a, 1)
+        pause()
+        from_z(a, 2)
+        from_x(a, 0)
+        pause()
+        from_z(a, 3)
+        from_y(a, 1)
+        pause()
+        from_x(a, 1)
+        from_y(a, 2)
+        pause()
+        from_x(a, 2)
+        from_y(a, 3)
+        pause()
+        from_x(a, 3)
+        last_y(a, 0)
+        last_x(a, 1)
+        pause()
+        last_y(a, 1)
+        last_x(a, 2)
+        last_y(a, 2)
+        last_x(a, 3)
+        last_y(a, 3)
+
+    def straighten():
+        last_core(conv)
+        keep[1].wait()
+        for at in range(SHARDS):
+            start = LINES * at
+            shifted[start : start + CONV_LINES] = conv_rows[at].astype(f32)
+        lines[...] = shifted[: SHARDS * LINES].astype(bf16)
+        store_lines.start()
+
+    store_lines = pltpu.make_async_copy(lines, lines_out, local_sem.at[3])
+    prepares = [functools.partial(prepare, pair) for pair in range(OUT_BLOCKS)]
+    forward(conv, prepares[:3])
+    forward(entry, prepares[3:6] + [straighten] + prepares[6:])
+    last_core(entry)
     for array, slot, target in waiting:
         pltpu.make_async_copy(target, target, send_sem.at[array, slot]).wait()
-    for copy in keep:
-        copy.wait()
+    keep[0].wait()
+    store_lines.wait()
     for pair in (6, 7):
         for copy in stores[pair]:
             copy.wait()
 
 
-def run_gather(entry, conv, x, live, lane):
+LINES = 1134
+
+
+def run_gather(entry, conv, x, target, *vectors):
     return pl.pallas_call(
         gather_kernel,
         out_shape=(
             jax.ShapeDtypeStruct((SHARDS, CHUNK_PAD, WIDE), bf16),
-            jax.ShapeDtypeStruct((SHARDS, CONV_LINES, 128), bf16),
+            jax.ShapeDtypeStruct((SHARDS * LINES, 128), bf16),
             jax.ShapeDtypeStruct((ROWS, PADDED), bf16),
             jax.ShapeDtypeStruct((PADDED, ROWS), bf16),
+            jax.ShapeDtypeStruct((ROWS, 128), bf16),
+            jax.ShapeDtypeStruct((CROPS, ROWS), bf16),
+            jax.ShapeDtypeStruct((ROWS, 2 * CROPS), bf16),
+            jax.ShapeDtypeStruct((CROPS, ROWS), bf16),
+            jax.ShapeDtypeStruct((ROWS, CROPS), bf16),
+            jax.ShapeDtypeStruct((BLOCKS, 8, 128), f32),
+            jax.ShapeDtypeStruct((OUT_BLOCKS, 8, 128), f32),
         ),
         in_specs=[pl.BlockSpec(memory_space=HBM)] * 3
-        + [pl.BlockSpec(memory_space=pltpu.VMEM)] * 2,
-        out_specs=(pl.BlockSpec(memory_space=HBM),) * 4,
+        + [pl.BlockSpec(memory_space=pltpu.SMEM)]
+        + [pl.BlockSpec(memory_space=pltpu.VMEM)] * 6,
+        out_specs=(pl.BlockSpec(memory_space=HBM),) * 4
+        + (pl.BlockSpec(memory_space=pltpu.VMEM),) * 7,
         scratch_shapes=[
+            pltpu.VMEM((SHARDS, CONV_LINES, 128), bf16),
+            pltpu.VMEM((SHARDS * LINES + 32, 128), f32),
+            pltpu.VMEM((SHARDS * LINES, 128), bf16),
             pltpu.VMEM((ROWS, CHANNELS), bf16),
             pltpu.VMEM((2, ROWS, LANES), bf16),
             pltpu.VMEM((2, LANES, ROWS), bf16),
             pltpu.SemaphoreType.DMA((2, 35)),
             pltpu.SemaphoreType.DMA((2, 35)),
-            pltpu.SemaphoreType.DMA((3,)),
+            pltpu.SemaphoreType.DMA((4,)),
             pltpu.SemaphoreType.DMA((2, OUT_BLOCKS)),
         ],
         name="gather",
@@ -1823,7 +1919,7 @@
         cost_estimate=pl.CostEstimate(
             flops=4 * ROWS * 384 * PADDED, bytes_accessed=200 * 2**20, transcendentals=0
         ),
-    )(entry, conv, x, live, lane)
+    )(entry, conv, x, target, *vectors)
 
 
 def input_kernel(delta_ref, weight_ref, residual_ref, live_ref, *refs):
@@ -1948,6 +2044,28 @@
     return values.reshape(lead + (CHANNELS,))
 
 
+def row_masks(on_global, pair_target):
+    positions = jnp.arange(ROWS, dtype=jnp.int32)
+    image_of = positions // IMAGE_ROWS
+    within = positions % IMAGE_ROWS
+    live = within < jnp.where(on_global, IMAGE_ROWS, SMALL_ROWS)
+    area = jnp.where(on_global, GLOBAL_SIDE**2, SMALL_SIDE**2)
+    crop_of = within // area
+    crop_ids = jnp.arange(CROPS, dtype=jnp.int32)
+    per_image = jnp.where(on_global, GLOBAL_CROPS, SMALL_CROPS)
+    pool_full = live[None] & ((image_of * per_image + crop_of)[None] == crop_ids[:, None])
+    pool = pool_full.astype(bf16)
+    target_rows = jnp.zeros((ROWS,), jnp.int32)
+    for slot in range(SMALL_CROPS):
+        target_rows = jnp.where(
+            crop_of == slot, jnp.repeat(pair_target[:, slot], IMAGE_ROWS), target_rows
+        )
+    pair_of = image_of * GLOBAL_CROPS + jnp.where(on_global, crop_of, target_rows)
+    pair = (live[None] & (pair_of[None] == crop_ids[:, None])).astype(bf16)
+    live_lanes = jnp.broadcast_to(live[:, None], (ROWS, 128)).astype(bf16)
+    return live, live_lanes, pool, pair
+
+
 def local(
     block_in,
     out_cotangent,
@@ -1969,63 +2087,50 @@
     size = lax.axis_size("img")
     stream = lax.axis_index("stream")
     on_global = stream == 0
-    positions = jnp.arange(ROWS, dtype=jnp.int32)
-    image_of = positions // IMAGE_ROWS
-    within = positions % IMAGE_ROWS
-    live = within < jnp.where(on_global, IMAGE_ROWS, SMALL_ROWS)
-    area = jnp.where(on_global, GLOBAL_SIDE**2, SMALL_SIDE**2)
-    crop_of = within // area
-    crop_ids = jnp.arange(CROPS, dtype=jnp.int32)
-    per_image = jnp.where(on_global, GLOBAL_CROPS, SMALL_CROPS)
-    pool_full = live[None] & ((image_of * per_image + crop_of)[None] == crop_ids[:, None])
-    pool = pool_full.astype(bf16)
-    target_rows = jnp.zeros((ROWS,), jnp.int32)
-    for slot in range(SMALL_CROPS):
-        target_rows = jnp.where(
-            crop_of == slot, jnp.repeat(pair_target[:, slot], IMAGE_ROWS), target_rows
-        )
-    pair_of = image_of * GLOBAL_CROPS + jnp.where(on_global, crop_of, target_rows)
-    pair = (live[None] & (pair_of[None] == crop_ids[:, None])).astype(bf16)
-    live_lanes = jnp.broadcast_to(live[:, None], (ROWS, 128)).astype(bf16)
     edges = edge_masks()
 
     x = block_in[0]
     cot = out_cotangent[0]
 
-    lines = CONV_LINES - 18
+    lines = LINES
     if size == SHARDS:
         entry_piece = wide_lanes(entry_weight.reshape(CHUNK, CHANNELS))
         entry_piece = jnp.pad(entry_piece, ((0, CHUNK_PAD - CHUNK), (0, 0)))
         piece = group_weight.reshape(lines, GROUP_WIDTH)
         piece = jnp.pad(piece, ((0, CONV_LINES - lines), (0, 128 - GROUP_WIDTH)))
-        entry_mat, conv, x_chunked, x_turned = run_gather(
-            entry_piece, piece, x, live_lanes, live[None].astype(f32)
+        vectors = (entry_gain, entry_shift, group_gain, group_shift, exit_gain, exit_shift)
+        gathered = run_gather(
+            entry_piece, piece, x, pair_target, *(vector[None] for vector in vectors)
         )
+        entry_mat, conv, x_chunked, x_turned, live_lanes, pool, spread, pair, pull = gathered[:9]
+        params, exit_params = gathered[9:]
         entry_mat = entry_mat.reshape(PADDED, WIDE)
-        conv = conv[:, :lines, :GROUP_WIDTH]
+        conv = conv.reshape(9, CHANNELS, 128)
     else:
+        def rows_of(*vectors):
+            kept = wide_lanes(jnp.stack(vectors)).reshape(len(vectors), BLOCKS, 2, 128)
+            return kept.transpose(1, 0, 2, 3).reshape(BLOCKS, 2 * len(vectors), 128)
+
+        params = rows_of(entry_gain, entry_shift, group_gain, group_shift)
+        exit_params = [
+            jnp.pad(vector, (0, PADDED - CHANNELS)).reshape(OUT_BLOCKS, 2, 128)
+            for vector in (exit_gain, exit_shift)
+        ]
+        exit_params = jnp.concatenate(exit_params * 2, axis=1)
+        live, live_lanes, pool, pair = row_masks(on_global, pair_target)
+        spread, pull = jnp.concatenate([pool.T, pool.T], axis=1), pair.T
         x_padded = jnp.where(live[:, None], x, 0)
         x_padded = jnp.pad(x_padded, ((0, 0), (0, PADDED - CHANNELS)))
         x_chunked, x_turned = run_prepare(x_padded)
         entry_mat = wide_lanes(gather(entry_weight, CHANNELS, size)[:, :CHANNELS])
         conv = lax.all_gather(group_weight, "img", axis=0, tiled=True)
-    conv = conv.reshape(9, CHANNELS, GROUP_WIDTH)
+        conv = conv.reshape(9, CHANNELS, GROUP_WIDTH)
+        conv = jnp.pad(conv, ((0, 0), (0, 0), (0, 128 - GROUP_WIDTH)))
     squeeze_mat = gather(squeeze_weight, SQUEEZE, size)
     excite_mat = gather(excite_weight, SQUEEZE, size)
     exit_mat = gather(exit_weight, CHANNELS, size)
 
-    def rows_of(*vectors):
-        kept = wide_lanes(jnp.stack(vectors)).reshape(len(vectors), BLOCKS, 2, 128)
-        return kept.transpose(1, 0, 2, 3).reshape(BLOCKS, 2 * len(vectors), 128)
-
-    params = rows_of(entry_gain, entry_shift, group_gain, group_shift)
-    exit_params = [
-        jnp.pad(vector, (0, PADDED - CHANNELS)).reshape(OUT_BLOCKS, 2, 128)
-        for vector in (exit_gain, exit_shift)
-    ]
-    exit_params = jnp.concatenate(exit_params * 2, axis=1)
-
-    fold = np.zeros((LANES, GROUP_WIDTH), np.float32)
+    fold = np.zeros((LANES, 128), np.float32)
     fold[np.arange(BLOCK), np.arange(BLOCK) % GROUP_WIDTH] = 1
     fold = jnp.asarray(fold, bf16)
     act, turned, group, mixed, pooled, moment = run_entry(
@@ -2033,7 +2138,6 @@
     )
 
     inner_pad = INNER - SQUEEZE
-    spread = jnp.concatenate([pool.T, pool.T], axis=1)
     scaled, scaled_turned, gates, pooled, inner, inner_rows, quarter = run_scale(
         mixed,
         spread,
@@ -2045,10 +2149,10 @@
     )
 
     block_out, exit_delta, residual, exit_grad, exit_total = run_exit(
-        size, scaled, scaled_turned, exit_mat, x, cot, exit_params, pair, pair.T, live_lanes
+        size, scaled, scaled_turned, exit_mat, x, cot, exit_params, pair, pull, live_lanes
     )
     exit_part = scatter(exit_grad, CHANNELS, size)
-    scaled_grad, gate_grad = run_gate(exit_delta, exit_mat, mixed, pool)
+    scaled_grad, gate_grad, block_out = run_gate(exit_delta, exit_mat, mixed, pool, block_out)
 
     pooled_gates, inner_grads, bias_rows = run_squeeze(
         gate_grad, pooled, inner, inner_rows, quarter, squeeze_mat, excite_mat

time: 604 us -> 578 us (0.957)
  local copies, waits for them, and re-layouts: 64 us -> 42.3 us
  waiting for transfers between devices: 2.75 us -> 15.1 us
  Pallas kernels: 508 us -> 497 us
    all_gather x3, waiting for transfers between devices: 0.06 us -> 12.9 us  [gather(): return lax.all_gather(piece, 'img', axis=0, tiled=True)]
    pallas_call x1, Pallas kernels: 87.4 us -> 80.7 us  [run_gather(): pl.pallas_call(gather_kernel, out_shape=(jax.ShapeDtypeStruct((SHARDS, CH...]
    reshape x4 -> x0, local copies, waits for them, and re-layouts: 6.46 us -> none  [the longest x1 6.21 us: local(): conv = conv.reshape(9, CHANNELS, GROUP_WIDTH)]
  transfers between devices with their start and end apart: 8 -> 8, of which waited for: 1 -> 2; matrix products, arithmetic and copies ran while one was open for 10% -> 6% of each run, Pallas kernels for 73% -> 75%
where the time goes in v4:
time: 578 us; the launch traced here: 576 us
  Pallas kernels  497 us (86%)
  local copies, waits for them, and re-layouts  42.3 us (7%)
  waiting for transfers between devices  15.1 us (3%)
  between operations  14.3 us (2%)
    pallas_call x1, Pallas kernels, run_back(): pl.pallas_call(functools.partial(back_kernel, size), grid=(max(BLOCKS + 2...  134 us
    pallas_call x1, Pallas kernels, run_input(): pl.pallas_call(input_kernel, grid=(BACK_REST + CONV_BLOCKS + 4 if reduced...  81.5 us
    pallas_call x1, Pallas kernels, run_gather(): pl.pallas_call(gather_kernel, out_shape=(jax.ShapeDtypeStruct((SHARDS, CH...  80.7 us
    pallas_call x1, Pallas kernels, run_entry(): pl.pallas_call(functools.partial(entry_kernel, size), grid=(BLOCKS + 2,),...  70.6 us
    pallas_call x1, Pallas kernels, run_exit(): pl.pallas_call(functools.partial(exit_kernel, size), grid=(blocks + 3,),...  66.8 us
    pallas_call x1, Pallas kernels, run_gate(): pl.pallas_call(gate_kernel, grid=(BLOCKS,), out_shape=(jax.ShapeDtypeStru...  31 us
    pallas_call x1, Pallas kernels, run_scale(): pl.pallas_call(scale_kernel, grid=(BLOCKS + OUT_BLOCKS,), out_shape=(jax....  23.3 us
    all_gather x3, waiting for transfers between devices, gather(): return lax.all_gather(piece, 'img', axis=0, tiled=True)  12.9 us
  transfers between devices with their start and end apart: 8, of which 2 were waited for; matrix products, arithmetic and copies ran while one was open for 6% of the time, Pallas kernels for 75%

profile of v4, /device:TPU:0, one launch (start us, length us, event | category | flops | bytes accessed | tf_op | source)
XLA Modules:
  0.0 575.6 jit_solution(15528809296485223031)
XLA Ops:
  11.0 1.8 reshape.95
  14.5 1.3 pad.44
  16.3 1.4 reshape.89
  18.5 2.1 reshape_reshape.6
  22.6 80.7 %gather.1 = (bf16[16,128,2304]{2,1,0:T(8,128)(2,1)}, bf16[18144,128]{1,0:T(8,128)(2,1)}, bf16[1568,2048]{1,0:T(8,128)(2,1)}, bf16[2048,1568]{1,0:T(8,128)(2,1)},...) custom-call(bf16[128,2304]{1,0:T(8,128)(2,1)} %pad.40.entry_ref, ...), custom_call_target="tpu_custom_call" | custom-call | flops 4932501504 | bytes 209715200 | tf_op jit(solution)/shard_map/gather/pallas_call | solution.py:1883
  104.3 70.6 %entry.1 = (f32[1568,2304]{1,0:T(8,128)}, bf16[9,256,1792]{2,1,0:T(8,128)(2,1)}, f32[1568,2304]{1,0:T(8,128)}, bf16[1568,2304]{1,0:T(8,128)(2,1)}, f32[16,2304]{1,0:T(8,128)}, /*index=5*/f32[9,2,8,128]{3,2,1,0:T(8,128)}) custom-call(bf16[1568,2048]{1,0:T(8,128)(2,1)} %get-tuple-element.61.x_ref, bf16[2048,2304]{1,0:T(8,128)(2,1)} %bitcast.90, ...), custom_call_target="tpu_custom_call" | custom-call | flops 31444697088 | bytes 73400320 | tf_op jit(solution)/shard_map/entry/pallas_call | solution.py:422
  175.0 23.3 %scale.1 = (bf16[1568,2048]{1,0:T(8,128)(2,1)}, bf16[2048,1568]{1,0:T(8,128)(2,1)}, bf16[32,2304]{1,0:T(8,128)(2,1)}, f32[16,2048]{1,0:T(8,128)}, f32[16,512]{1,...) custom-call(bf16[1568,2304]{1,0:T(8,128)(2,1)} %get-tuple-element.66.mixed_ref, ...), custom_call_target="tpu_custom_call" | custom-call | flops 6576668672 | bytes 31457280 | tf_op jit(solution)/shard_map/scale/pallas_call | solution.py:1179
  198.3 12.9 %all-gather.8.cloned.1.call-done.weight_ref = bf16[2048,2048]{1,0:T(8,128)(2,1)} async-done(((bf16[128,2048]{1,0:T(8,128)(2,1)}), bf16[2048,2048]{1,0:T(8,128)(2,1)}) %all-gather.8.cloned.1.call-update) | async-done | bytes 8388624 | tf_op jit(solution)/shard_map/all_gather | solution.py:2009
  211.2 66.8 %exit.1 = (bf16[1568,2016]{1,0:T(8,128)(2,1)}, bf16[1568,2048]{1,0:T(8,128)(2,1)}, bf16[1568,2048]{1,0:T(8,128)(2,1)}, bf16[2048,2048]{1,0:T(8,128)(2,1)}, f32[8,2,8,128]{3,2,1,0:T(8,128)}) custom-call(bf16[1568,2048]{1,0:T(8,128)(2,1)} %get-tuple-element.69.scaled_ref, bf16[2048,1568]{1,0:T(8,128)(2,1)} %get-tuple-element.70.turned_ref, ...), custom_call_target="tpu_custom_call" | custom-call | flops 26306674688 | bytes 73400320 | tf_op jit(solution)/shard_map/exit/pallas_call | solution.py:898
  278.0 31.0 %gate.1 = (f32[1568,2304]{1,0:T(8,128)}, f32[16,2304]{1,0:T(8,128)}, bf16[1568,2016]{1,0:T(8,128)(2,1)}) custom-call(bf16[1568,2048]{1,0:T(8,128)(2,1)} %get-tuple-element.75.delta_ref, bf16[2048,2048]{1,0:T(8,128)(2,1)} %all-gather.8.cloned.1.call-done.weight_ref, bf16[1568,2304]{1,0:T(8,128)(2,1)} %get-tuple-element.66.mixed_ref, ...), custom_call_target="tpu_custom_call" | custom-call | flops 14797504512 | bytes 41943040 | tf_op jit(solution)/shard_map/gate/pallas_call | solution.py:965
  309.0 9.8 %squeeze.45 = (bf16[32,2304]{1,0:T(8,128)(2,1)}, bf16[2048,1024]{1,0:T(8,128)(2,1)}, f32[8,512]{1,0:T(8,128)}) custom-call(f32[16,2304]{1,0:T(8,128)} %get-tuple-element.78.gate_grad_ref, f32[16,2048]{1,0:T(8,128)} %get-tuple-element.79.pooled_ref, f32[16,512]{1,0:T(8,128)} %get-tuple-element.80.inner_ref, f32[64,2048]{1,0:T(8,128)} %get-tuple-element.81.rows_ref, ...), custom_call_target="tpu_custom_call" | custom-call | flops 2147483648 | bytes 20971520 | tf_op jit(solution)/shard_map/squeeze/pallas_call | solution.py:1283
  318.8 1.3 reshape.96.bias_ref
  320.2 133.8 %back.1 = (bf16[1568,2304]{1,0:T(8,128)(2,1)}, f32[128,1536]{1,0:T(8,128)}, bf16[9,1008,112]{2,1,0:T(8,128)(2,1)}, f32[9,2,8,128]{3,2,1,0:T(8,128)}, f32[32,128]...) custom-call(f32[32,128]{1,0:T(8,128)} %reshape.96.bias_ref, f32[1568,2304]{1,0:T(8,128)} %get-tuple-element.84.grad_ref, ...), custom_call_target="tpu_custom_call" | custom-call | flops 48091889664 | bytes 94371840 | tf_op jit(solution)/shard_map/back/pallas_call | solution.py:1541
  457.0 2.0 reshape.97
  459.8 2.1 copy.57
  463.1 1.5 collective-permute-start.2
  464.6 81.5 %input.1 = (bf16[1568,2016]{1,0:T(8,128)(2,1)}, f32[6,2,128,128]{3,2,1,0:T(8,128)}) custom-call(bf16[1568,2304]{1,0:T(8,128)(2,1)} %get-tuple-element.95.delta_ref, bf16[2048,2304]{1,0:T(8,128)(2,1)} %bitcast.91, bf16[1568,2048]{1,0:T(8,128)(2,1)} %get-tuple-element.96.residual_ref, bf16[1568,128]{1,0:T(8,128)(2,1)} %get-tuple-element.74.live_ref, ...), custom_call_target="tpu_custom_call" | custom-call | flops 14797504512 | bytes 36700160 | tf_op jit(solution)/shard_map/input/pallas_call | solution.py:1973
  549.1 1.7 copy.46
  550.8 1.9 reshape_reshape.7
  552.7 1.6 collective-permute-start.1
  554.4 1.3 convert_add_fusion
  555.7 1.6 reshape.106
  557.3 2.0 collective-permute-done.1
  562.2 6.7 %copy.59 = bf16[1,1568,2016]{2,1,0:T(8,128)(2,1)} copy(bf16[1,1568,2016]{2,1,0:T(8,128)(2,1)} %bitcast.58) | data formatting | bytes 12644352
  (75 shorter events, 20.7 us)
Async XLA Ops:
  7.2 167.8 %all-gather.4.cloned.1.call-start = ((), (), s32[]{:S(2)}) async-start(), calls=%async_computation.2 | async-start | bytes 2228224 | tf_op jit(solution)/shard_map/all_gather | solution.py:2009
  9.1 165.9 %all-gather.6.cloned.1.call-start = ((), (), s32[]{:S(2)}) async-start(), calls=%async_computation.3 | async-start | bytes 2228224 | tf_op jit(solution)/shard_map/all_gather | solution.py:2009
  11.0 200.2 %all-gather.8.cloned.1.call-start = ((), (), s32[]{:S(2)}) async-start(), calls=%async_computation.4 | async-start | bytes 8912896 | tf_op jit(solution)/shard_map/all_gather | solution.py:2009
  13.6 440.4 %reduce-scatter.3.cloned.1.call-start = ((), (), s32[]{:S(2)}) async-start(), calls=%async_computation.5 | async-start | bytes 8912896 | tf_op jit(solution)/shard_map/reduce_scatter | solution.py:2017
  22.6 80.7 %copy-start.2 = (f32[2,424]{1,0:T(2,128)S(1)}, f32[2,424]{1,0:T(2,128)}, u32[]{:S(2)}) copy-start(f32[2,424]{1,0:T(2,128)} %constant.10.clone) | copy-start | bytes 10180
  278.0 274.8 %reduce-scatter.5.cloned.1.call-start = ((), (), s32[]{:S(2)}) async-start(), calls=%async_computation.6 | async-start | bytes 4456448 | tf_op jit(solution)/shard_map/reduce_scatter | solution.py:2017
  320.2 134.7 %copy-start.1 = (f32[8,2,8,128]{3,2,1,0:T(8,128)S(1)}, f32[8,2,8,128]{3,2,1,0:T(8,128)}, u32[]{:S(2)}) copy-start(f32[8,2,8,128]{3,2,1,0:T(8,128)} %get-tuple-element.103) | copy-start | bytes 196612
  456.4 5.4 collective-permute-start
  463.1 91.3 %collective-permute-start.2 = (bf16[128,2048]{1,0:T(8,128)(2,1)}, bf16[128,2048]{1,0:T(8,128)(2,1)}, u32[]{:S(2)}, u32[]{:S(2)}) collective-permute-start(bf16[128,2048]{1,0:T(8,128)(2,1)} %reduce-scatter.3.cloned.1.call-done), channel_id=1, source_target_pairs={{0,16},{16,0},{1,17},{17,1},{2,18},{18,2},{3,19},{19,3},{4,20},{20... | collective-permute-start | bytes 1572872 | tf_op jit(solution)/shard_map/ppermute | solution.py:2026
  464.6 84.0 %copy-start = (f32[128,1536]{1,0:T(8,128)S(1)}, f32[128,1536]{1,0:T(8,128)}, u32[]{:S(2)}) copy-start(f32[128,1536]{1,0:T(8,128)} %get-tuple-element.100) | copy-start | bytes 2359300
  552.7 6.6 %collective-permute-start.1 = (bf16[128,1024]{1,0:T(8,128)(2,1)}, bf16[128,1024]{1,0:T(8,128)(2,1)S(1)}, u32[]{:S(2)}, u32[]{:S(2)}) collective-permute-start(bf16[128,1024]{1,0:T(8,128)(2,1)} %reduce-scatter.5.cloned.1.call-done), channel_id=1, source_target_pairs={{0,16},{16,0},{1,17},{17,1},{2,18},{18,2},{3,19},{19,3},{4,20},{20... | collective-permute-start | bytes 786440 | tf_op jit(solution)/shard_map/ppermute | solution.py:2026
Sparse Core Ops, SparseCore 0:
  10.7 61.8 all-gather.3
  75.3 44.3 all-gather.5
  122.5 88.6 all-gather.7
  278.1 129.1 reduce-scatter.2
  454.2 89.1 reduce-scatter.4

commit v5 on v4

--- a/solution.py
+++ b/solution.py
@@ -503,8 +503,8 @@
             pltpu.VMEM((2, 3, 4, 2, 64, 128), bf16),
             pltpu.VMEM((2, 4, 2, 64, 128), bf16),
             pltpu.VMEM((2, 3, 2, 64, 128), bf16),
-            pltpu.VMEM((2, 2, 64, 128), f32),
-            pltpu.VMEM((2, 2, 64, 128), f32),
+            pltpu.VMEM((2, 2, 64, 128), bf16),
+            pltpu.VMEM((2, 2, 64, 128), bf16),
             pltpu.SemaphoreType.DMA((2, 2)),
             pltpu.SemaphoreType.DMA((2, 2, 3)),
             pltpu.SemaphoreType.DMA((2, 2, 3)),
@@ -578,8 +578,8 @@
         hold = lax.rem(block, 2)
         self.y_copy(block).wait()
         for tile in range(2):
-            put(tile, self.mine, self.final[hold, tile])
-            put(tile, self.theirs, self.final_got[hold, tile])
+            put(tile, self.mine, self.final[hold, tile].astype(f32))
+            put(tile, self.theirs, self.final_got[hold, tile].astype(f32))
 
     def after_z(self, block):
         hold = lax.rem(block, 2)
@@ -589,7 +589,7 @@
             total = self.plane_sum[hold, self.z, tile].astype(f32)
             for k in range(3):
                 total = total + self.z_got[hold, k, tile].astype(f32)
-            self.final[hold, tile] = total
+            self.final[hold, tile] = total.astype(bf16)
         self.y_copy(block).start()
 
     def after_plane(self, block):
@@ -1285,7 +1285,7 @@
         out_shape=(
             jax.ShapeDtypeStruct((2 * CROPS, WIDE), bf16),
             jax.ShapeDtypeStruct((PADDED, 2 * INNER), bf16),
-            jax.ShapeDtypeStruct((8, INNER), f32),
+            jax.ShapeDtypeStruct((6, INNER), f32),
         ),
         in_specs=[vmem] * 7,
         out_specs=(vmem,) * 3,
@@ -1302,7 +1302,7 @@
     )(gate_grad, pooled, inner, rows, quarter, squeeze, excite)
 
 
-BIAS_ROWS = 32
+BIAS_ROWS = 24
 
 
 def back_kernel(
@@ -2204,7 +2204,7 @@
     group_gain_grad, group_shift_grad = [narrow_lanes(v) for v in folded(totals[:, 0])]
     entry_gain_grad, entry_shift_grad = [narrow_lanes(v) for v in folded(totals[:, 1])]
     exit_gain_grad, exit_shift_grad = [v[:CHANNELS] for v in folded(exit_total[:, 1])]
-    bias_totals = bias_totals.reshape(8, INNER)[: 1 + QUARTERS, :SQUEEZE]
+    bias_totals = bias_totals.reshape(6, INNER)[: 1 + QUARTERS, :SQUEEZE]
     kept = jnp.concatenate(
         [
             jnp.stack(

time: 578 us -> 573 us (level)
  no operation moved by 1% of the time
where the time goes in v5:
time: 573 us; the launch traced here: 571 us
  Pallas kernels  493 us (86%)
  local copies, waits for them, and re-layouts  42.3 us (7%)
  waiting for transfers between devices  16.3 us (3%)
  between operations  14.3 us (2%)
    pallas_call x1, Pallas kernels, run_back(): pl.pallas_call(functools.partial(back_kernel, size), grid=(max(BLOCKS + 2...  132 us
    pallas_call x1, Pallas kernels, run_gather(): pl.pallas_call(gather_kernel, out_shape=(jax.ShapeDtypeStruct((SHARDS, CH...  80.7 us
    pallas_call x1, Pallas kernels, run_input(): pl.pallas_call(input_kernel, grid=(BACK_REST + CONV_BLOCKS + 4 if reduced...  78.9 us
    pallas_call x1, Pallas kernels, run_entry(): pl.pallas_call(functools.partial(entry_kernel, size), grid=(BLOCKS + 2,),...  70.6 us
    pallas_call x1, Pallas kernels, run_exit(): pl.pallas_call(functools.partial(exit_kernel, size), grid=(blocks + 3,),...  66.8 us
    pallas_call x1, Pallas kernels, run_gate(): pl.pallas_call(gate_kernel, grid=(BLOCKS,), out_shape=(jax.ShapeDtypeStru...  31 us
    pallas_call x1, Pallas kernels, run_scale(): pl.pallas_call(scale_kernel, grid=(BLOCKS + OUT_BLOCKS,), out_shape=(jax....  23.3 us
    all_gather x3, waiting for transfers between devices, gather(): return lax.all_gather(piece, 'img', axis=0, tiled=True)  12.9 us
  transfers between devices with their start and end apart: 8, of which 2 were waited for; matrix products, arithmetic and copies ran while one was open for 6% of the time, Pallas kernels for 75%

profile of v5, /device:TPU:0, one launch (start us, length us, event | category | flops | bytes accessed | tf_op | source)
XLA Modules:
  0.0 571.1 jit_solution(17528808271061529190)
XLA Ops:
  11.0 1.8 reshape.95
  14.5 1.3 pad.44
  16.3 1.4 reshape.89
  18.5 2.1 reshape_reshape.6
  22.6 80.7 %gather.1 = (bf16[16,128,2304]{2,1,0:T(8,128)(2,1)}, bf16[18144,128]{1,0:T(8,128)(2,1)}, bf16[1568,2048]{1,0:T(8,128)(2,1)}, bf16[2048,1568]{1,0:T(8,128)(2,1)},...) custom-call(bf16[128,2304]{1,0:T(8,128)(2,1)} %pad.40.entry_ref, ...), custom_call_target="tpu_custom_call" | custom-call | flops 4932501504 | bytes 209715200 | tf_op jit(solution)/shard_map/gather/pallas_call | solution.py:1883
  104.3 70.6 %entry.1 = (f32[1568,2304]{1,0:T(8,128)}, bf16[9,256,1792]{2,1,0:T(8,128)(2,1)}, f32[1568,2304]{1,0:T(8,128)}, bf16[1568,2304]{1,0:T(8,128)(2,1)}, f32[16,2304]{1,0:T(8,128)}, /*index=5*/f32[9,2,8,128]{3,2,1,0:T(8,128)}) custom-call(bf16[1568,2048]{1,0:T(8,128)(2,1)} %get-tuple-element.61.x_ref, bf16[2048,2304]{1,0:T(8,128)(2,1)} %bitcast.90, ...), custom_call_target="tpu_custom_call" | custom-call | flops 31444697088 | bytes 73400320 | tf_op jit(solution)/shard_map/entry/pallas_call | solution.py:422
  175.0 23.3 %scale.1 = (bf16[1568,2048]{1,0:T(8,128)(2,1)}, bf16[2048,1568]{1,0:T(8,128)(2,1)}, bf16[32,2304]{1,0:T(8,128)(2,1)}, f32[16,2048]{1,0:T(8,128)}, f32[16,512]{1,...) custom-call(bf16[1568,2304]{1,0:T(8,128)(2,1)} %get-tuple-element.66.mixed_ref, ...), custom_call_target="tpu_custom_call" | custom-call | flops 6576668672 | bytes 31457280 | tf_op jit(solution)/shard_map/scale/pallas_call | solution.py:1179
  198.3 12.9 %all-gather.8.cloned.1.call-done.weight_ref = bf16[2048,2048]{1,0:T(8,128)(2,1)} async-done(((bf16[128,2048]{1,0:T(8,128)(2,1)}), bf16[2048,2048]{1,0:T(8,128)(2,1)}) %all-gather.8.cloned.1.call-update) | async-done | bytes 8388624 | tf_op jit(solution)/shard_map/all_gather | solution.py:2009
  211.2 66.8 %exit.1 = (bf16[1568,2016]{1,0:T(8,128)(2,1)}, bf16[1568,2048]{1,0:T(8,128)(2,1)}, bf16[1568,2048]{1,0:T(8,128)(2,1)}, bf16[2048,2048]{1,0:T(8,128)(2,1)}, f32[8,2,8,128]{3,2,1,0:T(8,128)}) custom-call(bf16[1568,2048]{1,0:T(8,128)(2,1)} %get-tuple-element.69.scaled_ref, bf16[2048,1568]{1,0:T(8,128)(2,1)} %get-tuple-element.70.turned_ref, ...), custom_call_target="tpu_custom_call" | custom-call | flops 26306674688 | bytes 73400320 | tf_op jit(solution)/shard_map/exit/pallas_call | solution.py:898
  278.0 31.0 %gate.1 = (f32[1568,2304]{1,0:T(8,128)}, f32[16,2304]{1,0:T(8,128)}, bf16[1568,2016]{1,0:T(8,128)(2,1)}) custom-call(bf16[1568,2048]{1,0:T(8,128)(2,1)} %get-tuple-element.75.delta_ref, bf16[2048,2048]{1,0:T(8,128)(2,1)} %all-gather.8.cloned.1.call-done.weight_ref, bf16[1568,2304]{1,0:T(8,128)(2,1)} %get-tuple-element.66.mixed_ref, ...), custom_call_target="tpu_custom_call" | custom-call | flops 14797504512 | bytes 41943040 | tf_op jit(solution)/shard_map/gate/pallas_call | solution.py:965
  309.0 9.8 %squeeze.45 = (bf16[32,2304]{1,0:T(8,128)(2,1)}, bf16[2048,1024]{1,0:T(8,128)(2,1)}, f32[6,512]{1,0:T(8,128)}) custom-call(f32[16,2304]{1,0:T(8,128)} %get-tuple-element.78.gate_grad_ref, f32[16,2048]{1,0:T(8,128)} %get-tuple-element.79.pooled_ref, f32[16,512]{1,0:T(8,128)} %get-tuple-element.80.inner_ref, f32[64,2048]{1,0:T(8,128)} %get-tuple-element.81.rows_ref, ...), custom_call_target="tpu_custom_call" | custom-call | flops 2147483648 | bytes 20971520 | tf_op jit(solution)/shard_map/squeeze/pallas_call | solution.py:1283
  318.8 1.3 reshape.96.bias_ref
  320.2 131.8 %back.1 = (bf16[1568,2304]{1,0:T(8,128)(2,1)}, f32[128,1536]{1,0:T(8,128)}, bf16[9,1008,112]{2,1,0:T(8,128)(2,1)}, f32[9,2,8,128]{3,2,1,0:T(8,128)}, f32[24,128]...) custom-call(f32[24,128]{1,0:T(8,128)} %reshape.96.bias_ref, f32[1568,2304]{1,0:T(8,128)} %get-tuple-element.84.grad_ref, ...), custom_call_target="tpu_custom_call" | custom-call | flops 48091889664 | bytes 94371840 | tf_op jit(solution)/shard_map/back/pallas_call | solution.py:1541
  454.5 2.0 reshape.97
  457.3 2.1 copy.57
  460.6 2.0 collective-permute-start.2
  462.6 78.9 %input.1 = (bf16[1568,2016]{1,0:T(8,128)(2,1)}, f32[6,2,128,128]{3,2,1,0:T(8,128)}) custom-call(bf16[1568,2304]{1,0:T(8,128)(2,1)} %get-tuple-element.95.delta_ref, bf16[2048,2304]{1,0:T(8,128)(2,1)} %bitcast.91, bf16[1568,2048]{1,0:T(8,128)(2,1)} %get-tuple-element.96.residual_ref, bf16[1568,128]{1,0:T(8,128)(2,1)} %get-tuple-element.74.live_ref, ...), custom_call_target="tpu_custom_call" | custom-call | flops 14797504512 | bytes 36700160 | tf_op jit(solution)/shard_map/input/pallas_call | solution.py:1973
  541.5 1.2 fusion
  544.6 1.7 copy.46
  546.3 1.9 reshape_reshape.7
  548.6 1.3 convert_add_fusion
  549.9 1.6 reshape.106
  551.5 3.2 collective-permute-done.1
  557.6 6.7 %copy.59 = bf16[1,1568,2016]{2,1,0:T(8,128)(2,1)} copy(bf16[1,1568,2016]{2,1,0:T(8,128)(2,1)} %bitcast.58) | data formatting | bytes 12644352
  (75 shorter events, 19.4 us)
Async XLA Ops:
  7.2 167.8 %all-gather.4.cloned.1.call-start = ((), (), s32[]{:S(2)}) async-start(), calls=%async_computation.2 | async-start | bytes 2228224 | tf_op jit(solution)/shard_map/all_gather | solution.py:2009
  9.1 165.9 %all-gather.6.cloned.1.call-start = ((), (), s32[]{:S(2)}) async-start(), calls=%async_computation.3 | async-start | bytes 2228224 | tf_op jit(solution)/shard_map/all_gather | solution.py:2009
  11.0 200.2 %all-gather.8.cloned.1.call-start = ((), (), s32[]{:S(2)}) async-start(), calls=%async_computation.4 | async-start | bytes 8912896 | tf_op jit(solution)/shard_map/all_gather | solution.py:2009
  13.6 438.4 %reduce-scatter.3.cloned.1.call-start = ((), (), s32[]{:S(2)}) async-start(), calls=%async_computation.5 | async-start | bytes 8912896 | tf_op jit(solution)/shard_map/reduce_scatter | solution.py:2017
  22.6 80.7 %copy-start.2 = (f32[2,424]{1,0:T(2,128)S(1)}, f32[2,424]{1,0:T(2,128)}, u32[]{:S(2)}) copy-start(f32[2,424]{1,0:T(2,128)} %constant.10.clone) | copy-start | bytes 10180
  278.0 270.2 %reduce-scatter.5.cloned.1.call-start = ((), (), s32[]{:S(2)}) async-start(), calls=%async_computation.6 | async-start | bytes 4456448 | tf_op jit(solution)/shard_map/reduce_scatter | solution.py:2017
  320.2 132.7 %copy-start.1 = (f32[8,2,8,128]{3,2,1,0:T(8,128)S(1)}, f32[8,2,8,128]{3,2,1,0:T(8,128)}, u32[]{:S(2)}) copy-start(f32[8,2,8,128]{3,2,1,0:T(8,128)} %get-tuple-element.103) | copy-start | bytes 196612
  454.4 4.9 collective-permute-start
  460.6 88.0 %collective-permute-start.2 = (bf16[128,2048]{1,0:T(8,128)(2,1)}, bf16[128,2048]{1,0:T(8,128)(2,1)}, u32[]{:S(2)}, u32[]{:S(2)}) collective-permute-start(bf16[128,2048]{1,0:T(8,128)(2,1)} %reduce-scatter.3.cloned.1.call-done), channel_id=1, source_target_pairs={{0,16},{16,0},{1,17},{17,1},{2,18},{18,2},{3,19},{19,3},{4,20},{20... | collective-permute-start | bytes 1572872 | tf_op jit(solution)/shard_map/ppermute | solution.py:2026
  462.6 81.4 %copy-start = (f32[128,1536]{1,0:T(8,128)S(1)}, f32[128,1536]{1,0:T(8,128)}, u32[]{:S(2)}) copy-start(f32[128,1536]{1,0:T(8,128)} %get-tuple-element.100) | copy-start | bytes 2359300
  548.2 6.6 %collective-permute-start.1 = (bf16[128,1024]{1,0:T(8,128)(2,1)}, bf16[128,1024]{1,0:T(8,128)(2,1)S(1)}, u32[]{:S(2)}, u32[]{:S(2)}) collective-permute-start(bf16[128,1024]{1,0:T(8,128)(2,1)} %reduce-scatter.5.cloned.1.call-done), channel_id=1, source_target_pairs={{0,16},{16,0},{1,17},{17,1},{2,18},{18,2},{3,19},{19,3},{4,20},{20... | collective-permute-start | bytes 786440 | tf_op jit(solution)/shard_map/ppermute | solution.py:2026
Sparse Core Ops, SparseCore 0:
  10.7 61.8 all-gather.3
  75.3 44.3 all-gather.5
  122.5 88.6 all-gather.7
  278.1 129.6 reduce-scatter.2
  452.2 86.9 reduce-scatter.4
